TPU v7x, 32 devices: a whole 2x2x4 slice. The times are simulated.
32 devices in a mesh: groups: 2 (over x), resp: 4 (over z), expert: 4 (over y, core).
Axes of the slice: x: 2, y: 2, z: 4, core: 2. Of those that a mesh axis runs over, the one named last changes fastest.
Arguments:
- x_prompt: bfloat16 [8, 8, 4096], P(('groups', 'expert'), 'resp'), parts along dimension 0, may hold values from -6 to 6
- x_resp: bfloat16 [8, 4, 4, 4096], P(('groups', 'expert'), 'resp'), parts along dimension 0, may hold values from -6 to 6
- prompt_cot: bfloat16 [8, 4, 8, 4096], P(('groups', 'expert'), 'resp'), parts along dimension 0, may hold values from -6 to 6
- resp_cot: bfloat16 [8, 4, 4, 4096], P(('groups', 'expert'), 'resp'), parts along dimension 0, may hold values from -24 to 24
- route_prompt: int32 [8, 8, 2], P(('groups', 'expert'), 'resp'), parts along dimension 0, may hold values from 0 to 3, all different within a row; in each aligned block of 2 rows (0 to 1, 2 to 3, ..., all dimensions but the last counted through in order) at most 2 rows name the same one
- route_resp: int32 [8, 4, 4, 2], P(('groups', 'expert'), 'resp'), parts along dimension 0, may hold values from 0 to 3, all different within a row; in each aligned block of 4 rows (0 to 3, 4 to 7, ..., all dimensions but the last counted through in order) at most 2 rows name the same one
- weight_prompt: float32 [8, 8, 2], P(('groups', 'expert'), 'resp'), parts along dimension 0, may hold values from 0.03 to 0.4
- weight_resp: float32 [8, 4, 4, 2], P(('groups', 'expert'), 'resp'), parts along dimension 0, may hold values from 0.03 to 0.4
- w_gate: bfloat16 [4, 1536, 4096], P('expert', 'resp'), may hold values from -0.09375 to 0.09375
- w_up: bfloat16 [4, 1536, 4096], P('expert', 'resp'), may hold values from -0.09375 to 0.09375
- w_down: bfloat16 [4, 1536, 4096], P('expert', 'resp'), may hold values from -0.15625 to 0.15625
Outputs:
- grad_prompt: bfloat16 [8, 8, 4096], P(('groups', 'expert'), 'resp'), parts along dimension 0
- grad_resp: bfloat16 [8, 4, 4, 4096], P(('groups', 'expert'), 'resp'), parts along dimension 0
- grad_gate: bfloat16 [8, 1536, 4096], P(('groups', 'expert'), 'resp'), parts along dimension 0
- grad_up: bfloat16 [8, 1536, 4096], P(('groups', 'expert'), 'resp'), parts along dimension 0
- grad_down: bfloat16 [8, 1536, 4096], P(('groups', 'expert'), 'resp'), parts along dimension 0
There are 2 independent parts, one for each index of `groups`. A program takes and returns all parts, laid end to end along the dimension named above; an argument that names none is the same for every part. Nothing has to cross between parts.
Inputs may be any that keep to these rules, and one draw needn't show every extreme that they name: `route_prompt`: each row names 2 different experts; within each aligned block of 2 prompt rows (the rows of one device) no expert is named by more than 2 rows. `route_resp`: each token names 2 different experts; within the 4 tokens of one response no expert is named by more than 2 tokens, and some expert reaches 2.
All inputs are finite; a program needn't handle non-finite values.
Results may differ from a plain program's by a relative error of at most 0.019.
Values may be sent and summed in bfloat16 or wider, within the bound.
No kernel may reach another device: no remote copies, remote signals or barrier semaphores. Data moves between devices by JAX's collectives and lax.ppermute only.
A program may use at most 128 MiB of HBM per device.

v0:
```python
import jax
import jax.numpy as jnp
from jax import lax
from jax.sharding import PartitionSpec as P


def route_slots(expert_ids, experts):
    onehot = (expert_ids[..., None] == jnp.arange(experts, dtype=jnp.int32)).astype(jnp.int32)
    member = jnp.sum(onehot, axis=-2)
    before = jnp.cumsum(member, axis=-2) - member
    return jnp.sum(onehot * before[..., None, :], axis=-1)


def contract_last(left, right):
    return lax.dot_general(
        left, right, (((1,), (1,)), ((), ())), preferred_element_type=jnp.float32
    )


def contract_first(left, right):
    return lax.dot_general(
        left, right, (((0,), (0,)), ((), ())), preferred_element_type=jnp.float32
    )


def body(
    x_prompt,
    x_resp,
    prompt_cot,
    resp_cot,
    route_prompt,
    route_resp,
    weight_prompt,
    weight_resp,
    w_gate,
    w_up,
    w_down,
):
    n_resp = lax.axis_size("resp")
    n_expert = lax.axis_size("expert")
    prompt_in = x_prompt[0]
    resp_in = x_resp[0]
    width = prompt_in.shape[1]
    prompt_rows = prompt_in.shape[0]
    responses = resp_in.shape[0]
    length = resp_in.shape[1]
    top_count = route_prompt.shape[2]
    experts = n_expert * w_gate.shape[0]
    cap_prompt = max(2, prompt_rows * top_count * 3 // (2 * experts))
    cap_resp = max(2, length * top_count * 5 // (4 * experts))
    slots = cap_prompt + responses * cap_resp
    tokens = prompt_rows + responses * length
    local_sum = jnp.sum(prompt_cot[0].astype(jnp.float32), axis=0)
    dy_prompt = lax.psum_scatter(
        local_sum.astype(jnp.bfloat16), "resp", scatter_dimension=0, tiled=True
    )
    slot_prompt = route_slots(route_prompt[0], experts)
    slot_resp = (
        route_slots(route_resp[0], experts)
        + cap_prompt
        + cap_resp * jnp.arange(responses, dtype=jnp.int32)[:, None, None]
    )
    expert_ids = jnp.concatenate(
        [route_prompt[0], route_resp[0].reshape(responses * length, top_count)], axis=0
    )
    slot_all = jnp.concatenate(
        [slot_prompt, slot_resp.reshape(responses * length, top_count)], axis=0
    )
    position = expert_ids * slots + slot_all
    router = jnp.concatenate(
        [weight_prompt[0], weight_resp[0].reshape(responses * length, top_count)], axis=0
    )
    targets = jnp.arange(experts * slots, dtype=jnp.int32)
    matched = position[None, :, :] == targets[:, None, None]
    select = jnp.sum(matched.astype(jnp.float32), axis=2)
    weighted = jnp.sum(jnp.where(matched, router[None, :, :], 0.0), axis=2)
    inputs = jnp.concatenate([prompt_in, resp_in.reshape(responses * length, width)], axis=0)
    outgrad = jnp.concatenate([dy_prompt, resp_cot[0].reshape(responses * length, width)], axis=0)
    send_in = jnp.dot(select.astype(jnp.bfloat16), inputs, preferred_element_type=jnp.float32)
    send_in = send_in.astype(jnp.bfloat16).reshape(experts, slots, width)
    send_grad = jnp.dot(
        weighted,
        outgrad.astype(jnp.float32),
        precision=lax.Precision.HIGHEST,
        preferred_element_type=jnp.float32,
    )
    send_grad = send_grad.astype(jnp.bfloat16).reshape(experts, slots, width)
    spread_in = jnp.broadcast_to(send_in[None], (n_resp, experts, slots, width)).reshape(
        n_resp * experts, slots, width
    )
    spread_grad = jnp.broadcast_to(send_grad[None], (n_resp, experts, slots, width)).reshape(
        n_resp * experts, slots, width
    )
    rows_in, rows_grad = (
        lax.all_to_all(spread_in, ("resp", "expert"), split_axis=0, concat_axis=0, tiled=True),
        lax.all_to_all(spread_grad, ("resp", "expert"), split_axis=0, concat_axis=0, tiled=True),
    )
    rows_in = rows_in.reshape(n_resp * experts * slots, width)
    rows_grad = rows_grad.reshape(n_resp * experts * slots, width)
    gate_w = w_gate[0]
    up_w = w_up[0]
    down_w = w_down[0]
    gate = contract_last(rows_in, gate_w)
    upward = contract_last(rows_in, up_w)
    sigma = jax.nn.sigmoid(gate)
    active = gate * sigma
    hidden = (active * upward).astype(jnp.bfloat16)
    hidden_grad = contract_last(rows_grad, down_w)
    gate_grad = (hidden_grad * upward * sigma * (1.0 + gate * (1.0 - sigma))).astype(jnp.bfloat16)
    upward_grad = (hidden_grad * active).astype(jnp.bfloat16)
    grad_gate = contract_first(gate_grad, rows_in).astype(jnp.bfloat16)[None]
    grad_up = contract_first(upward_grad, rows_in).astype(jnp.bfloat16)[None]
    grad_down = contract_first(hidden, rows_grad).astype(jnp.bfloat16)[None]
    partial_value = jnp.dot(gate_grad, gate_w, preferred_element_type=jnp.float32)
    partial_value = (
        partial_value + jnp.dot(upward_grad, up_w, preferred_element_type=jnp.float32)
    ).astype(jnp.bfloat16)
    returned = lax.all_to_all(
        partial_value.reshape(n_resp * experts, slots, width),
        ("resp", "expert"),
        split_axis=0,
        concat_axis=0,
        tiled=True,
    )
    returned = returned.reshape(n_resp, experts * slots, width).astype(jnp.float32)
    route_dx = jnp.sum(returned, axis=0).astype(jnp.bfloat16)
    token_grad = jnp.dot(
        select.T.astype(jnp.bfloat16), route_dx, preferred_element_type=jnp.float32
    ).astype(jnp.bfloat16)
    grad_prompt = token_grad[:prompt_rows][None]
    grad_resp = token_grad[prompt_rows:tokens].reshape(responses, length, width)[None]
    return (grad_prompt, grad_resp, grad_gate, grad_up, grad_down)


def solution(mesh):
    return jax.shard_map(
        body,
        mesh=mesh,
        in_specs=(
            P(("groups", "expert"), "resp", None),
            P(("groups", "expert"), "resp", None, None),
            P(("groups", "expert"), "resp", None, None),
            P(("groups", "expert"), "resp", None, None),
            P(("groups", "expert"), "resp", None),
            P(("groups", "expert"), "resp", None, None),
            P(("groups", "expert"), "resp", None),
            P(("groups", "expert"), "resp", None, None),
            P("expert", "resp", None),
            P("expert", "resp", None),
            P("expert", "resp", None),
        ),
        out_specs=(
            P(("groups", "expert"), "resp", None),
            P(("groups", "expert"), "resp", None, None),
            P(("groups", "expert"), "resp", None),
            P(("groups", "expert"), "resp", None),
            P(("groups", "expert"), "resp", None),
        ),
        check_vma=False,
    )
```

profile of v0, /device:TPU:0, one launch (start us, length us, event | category | flops | bytes accessed | tf_op | source)
XLA Modules:
  0.0 123.8 jit_solution(7390920151606675721)
XLA Ops:
  7.2 0.0 copy-start
  7.2 0.9 convert_reduce_fusion.2
  8.1 0.8 copy.26
  8.9 0.9 select_reduce_fusion.2
  9.8 0.1 copy.27
  9.9 0.8 copy.29
  10.7 0.8 convert_reduce_fusion.1
  11.5 0.9 select_reduce_fusion.1
  12.4 0.8 fusion.21
  13.2 0.1 copy.28
  13.3 0.8 pad_maximum_fusion
  14.0 0.1 copy.30
  14.1 0.1 select_reduce_fusion
  14.2 1.0 convolution_convert_fusion.3
  15.2 0.1 broadcast_in_dim.49
  15.3 1.0 broadcast_in_dim.50
  16.3 7.4 %all-to-all-start.1 = ((bf16[16,4,4096]{2,1,0:T(4,128)(2,1)}), bf16[16,4,4096]{2,1,0:T(4,128)(2,1)}, u32[]{:S(2)}, u32[]{:S(2)}) async-start(bf16[16,4,4096]{2,1,0:T(4,128)(2,1)} %bitcast.50), calls=%async_computation.1 | async-start | bytes 1048576 | tf_op jit(solution)/shard_map/all_to_all | solution.py:95
  23.7 0.0 all-reduce.3.cloned.1.call-start
  23.8 0.7 all-reduce.3.cloned.1.call-update
  24.4 1.2 %dynamic-slice = u32[1]{0:T(128)} dynamic-slice(u32[32]{0:T(128)} %constant.33, u32[]{:T(128)S(6)} %add.32), dynamic_slice_sizes={1} | dynamic-slice | bytes 12
  26.3 35.8 %all-reduce.3.cloned.1.call-done = bf16[8,4096]{1,0:T(8,128)(2,1)} async-done(((bf16[8,4096]{1,0:T(8,128)(2,1)}), bf16[8,4096]{1,0:T(8,128)(2,1)}) %all-reduce.3.cloned.1.call-update) | async-done | bytes 65552
  62.2 0.9 constant_dynamic-slice_fusion
  63.0 1.1 convolution_convert_fusion.4
  64.2 0.1 broadcast_in_dim.47
  64.2 0.0 all-to-all-done.1
  64.2 1.0 broadcast_in_dim.48
  65.2 4.5 %all-to-all-start = ((bf16[16,4,4096]{2,1,0:T(4,128)(2,1)}), bf16[16,4,4096]{2,1,0:T(4,128)(2,1)}, u32[]{:S(2)}, u32[]{:S(2)}) async-start(bf16[16,4,4096]{2,1,0:T(4,128)(2,1)} %bitcast.51), calls=%async_computation | async-start | bytes 1048576 | tf_op jit(solution)/shard_map/all_to_all | solution.py:96
  69.7 2.0 %reshape.121 = bf16[64,4096]{1,0:T(8,128)(2,1)} reshape(bf16[16,4,4096]{2,1,0:T(4,128)(2,1)} %all-to-all-done.1) | data formatting | bytes 1048576 | tf_op jit(solution)/shard_map/reshape | solution.py:98
  71.7 2.3 %fusion.6 = f32[64,384]{1,0:T(8,128)S(1)} fusion(bf16[64,4096]{1,0:T(8,128)(2,1)} %reshape.121, bf16[1,384,4096]{2,1,0:T(8,128)(2,1)S(1)} %copy-done), kind=kOutput, calls=%fused_computation.13 | convolution fusion | flops 201326592 | bytes 3768320 | tf_op jit(solution)/shard_map/dot_general | solution.py:15
  73.9 1.1 fusion.9
  75.0 9.2 %all-to-all-done = bf16[16,4,4096]{2,1,0:T(4,128)(2,1)} async-done(((bf16[16,4,4096]{2,1,0:T(4,128)(2,1)}), bf16[16,4,4096]{2,1,0:T(4,128)(2,1)}, u32[]{:S(2)}, u32[]{:S(2)}) %all-to-all-start) | async-done | bytes 524320 | tf_op jit(solution)/shard_map/all_to_all | solution.py:96
  84.2 2.0 %reshape.119 = bf16[64,4096]{1,0:T(8,128)(2,1)} reshape(bf16[16,4,4096]{2,1,0:T(4,128)(2,1)} %all-to-all-done) | data formatting | bytes 1048576 | tf_op jit(solution)/shard_map/reshape | solution.py:99
  86.2 3.3 %multiply_convert_fusion.1 = (bf16[64,384]{1,0:T(8,128)(2,1)S(1)}, bf16[64,384]{1,0:T(8,128)(2,1)S(1)}) fusion(f32[64,384]{1,0:T(8,128)S(1)} %fusion.6, f32[64,384]{1,0:T(8,128)S(1)} %fusion.9, bf16[64,4096]{1,0:T(8,128)(2,1)} %reshape.119, bf16[1,384,4096]{2,1,0:T(8,128)(2,1)} %param.21), kind=kOutput, calls=%fused_computation.21 | convolution fusion | flops 201646080 | bytes 3964928 | tf_op jit(solution)/shard_map/dot_general | solution.py:15
  89.5 0.7 fusion.4
  90.2 1.5 %fusion.3 = bf16[64,4096]{1,0:T(8,128)(2,1)} fusion(f32[64,4096]{1,0:T(8,128)S(1)} %fusion.4, bf16[64,384]{1,0:T(8,128)(2,1)S(1)} %get-tuple-element.7, bf16[1,384,4096]{2,1,0:T(8,128)(2,1)S(1)} %copy-done.4), kind=kOutput, calls=%fused_computation.7 | convolution fusion | flops 201850880 | bytes 4767744 | tf_op jit(solution)/shard_map/dot_general | solution.py:116
  91.7 2.1 %reshape.122 = bf16[16,4,4096]{2,1,0:T(4,128)(2,1)} reshape(bf16[64,4096]{1,0:T(8,128)(2,1)} %fusion.3) | data formatting | bytes 1048576 | tf_op jit(solution)/shard_map/reshape | solution.py:119
  93.7 4.2 %all-to-all-start.2 = ((bf16[16,4,4096]{2,1,0:T(4,128)(2,1)}), bf16[16,4,4096]{2,1,0:T(4,128)(2,1)}, u32[]{:S(2)}, u32[]{:S(2)}) async-start(bf16[16,4,4096]{2,1,0:T(4,128)(2,1)} %reshape.122), calls=%async_computation.2 | async-start | bytes 1048576 | tf_op jit(solution)/shard_map/all_to_all | solution.py:118
  98.0 0.0 copy-start.2
  98.0 0.0 copy-start.5
  98.0 3.8 %fusion.1 = bf16[1,384,4096]{2,1,0:T(8,128)(2,1)} fusion(bf16[64,384]{1,0:T(8,128)(2,1)S(1)} %get-tuple-element.7, bf16[64,4096]{1,0:T(8,128)(2,1)} %reshape.121), kind=kOutput, calls=%fused_computation.4 | convolution fusion | flops 202899456 | bytes 3719168 | tf_op jit(solution)/shard_map/dot_general | solution.py:21
  101.8 2.7 %fusion = bf16[1,384,4096]{2,1,0:T(8,128)(2,1)} fusion(bf16[64,384]{1,0:T(8,128)(2,1)S(1)} %get-tuple-element.8, bf16[64,4096]{1,0:T(8,128)(2,1)S(1)} %copy-done.2), kind=kOutput, calls=%fused_computation.3 | convolution fusion | flops 202899456 | bytes 3719168 | tf_op jit(solution)/shard_map/dot_general | solution.py:21
  104.5 2.7 %fusion.2 = bf16[1,384,4096]{2,1,0:T(8,128)(2,1)} fusion(bf16[64,4096]{1,0:T(8,128)(2,1)S(1)} %copy-done.5, f32[64,384]{1,0:T(8,128)S(1)} %fusion.9, f32[64,384]{1,0:T(8,128)S(1)} %fusion.6), kind=kOutput, calls=%fused_computation.5 | convolution fusion | flops 203046912 | bytes 3866624 | tf_op jit(solution)/shard_map/dot_general | solution.py:21
  107.2 5.3 %all-to-all-done.2 = bf16[16,4,4096]{2,1,0:T(4,128)(2,1)} async-done(((bf16[16,4,4096]{2,1,0:T(4,128)(2,1)}), bf16[16,4,4096]{2,1,0:T(4,128)(2,1)}, u32[]{:S(2)}, u32[]{:S(2)}) %all-to-all-start.2) | async-done | bytes 524320 | tf_op jit(solution)/shard_map/all_to_all | solution.py:118
  112.5 2.0 %reshape.123 = bf16[4,16,4096]{2,1,0:T(8,128)(2,1)} reshape(bf16[16,4,4096]{2,1,0:T(4,128)(2,1)} %all-to-all-done.2) | data formatting | bytes 1048576 | tf_op jit(solution)/shard_map/reshape | solution.py:125
  114.4 1.1 reduce_sum.76
  115.6 0.1 convolution_convert_fusion.5
  115.7 0.6 slice_bitcast_fusion.1
  116.3 0.6 slice_bitcast_fusion
  (14 shorter events, 0.1 us)
Async XLA Ops:
  7.2 64.5 %copy-start = (bf16[1,384,4096]{2,1,0:T(8,128)(2,1)S(1)}, bf16[1,384,4096]{2,1,0:T(8,128)(2,1)}, u32[]{:S(2)}) copy-start(bf16[1,384,4096]{2,1,0:T(8,128)(2,1)} %param.19) | copy-start | bytes 9437188
  16.3 48.0 %all-to-all-start.1 = ((bf16[16,4,4096]{2,1,0:T(4,128)(2,1)}), bf16[16,4,4096]{2,1,0:T(4,128)(2,1)}, u32[]{:S(2)}, u32[]{:S(2)}) async-start(bf16[16,4,4096]{2,1,0:T(4,128)(2,1)} %bitcast.50), calls=%async_computation.1 | async-start | bytes 1048576 | tf_op jit(solution)/shard_map/all_to_all | solution.py:95
  23.7 38.5 %all-reduce.3.cloned.1.call-start = ((), (), s32[]{:S(2)}) async-start(), calls=%async_computation.3 | async-start | bytes 131072
  65.2 19.0 %all-to-all-start = ((bf16[16,4,4096]{2,1,0:T(4,128)(2,1)}), bf16[16,4,4096]{2,1,0:T(4,128)(2,1)}, u32[]{:S(2)}, u32[]{:S(2)}) async-start(bf16[16,4,4096]{2,1,0:T(4,128)(2,1)} %bitcast.51), calls=%async_computation | async-start | bytes 1048576 | tf_op jit(solution)/shard_map/all_to_all | solution.py:96
  71.6 2.3 %copy-start.1 = (bf16[64,4096]{1,0:T(8,128)(2,1)S(1)}, bf16[64,4096]{1,0:T(8,128)(2,1)}, u32[]{:S(2)}) copy-start(bf16[64,4096]{1,0:T(8,128)(2,1)} %reshape.121) | copy-start | bytes 1572868
  71.6 2.3 %copy-start.3 = (bf16[1,384,4096]{2,1,0:T(8,128)(2,1)S(1)}, bf16[1,384,4096]{2,1,0:T(8,128)(2,1)}, u32[]{:S(2)}) copy-start(bf16[1,384,4096]{2,1,0:T(8,128)(2,1)} %param.20) | copy-start | bytes 9437188
  86.2 4.0 %copy-start.4 = (bf16[1,384,4096]{2,1,0:T(8,128)(2,1)S(1)}, bf16[1,384,4096]{2,1,0:T(8,128)(2,1)}, u32[]{:S(2)}) copy-start(bf16[1,384,4096]{2,1,0:T(8,128)(2,1)} %param.20) | copy-start | bytes 9437188
  93.7 18.7 %all-to-all-start.2 = ((bf16[16,4,4096]{2,1,0:T(4,128)(2,1)}), bf16[16,4,4096]{2,1,0:T(4,128)(2,1)}, u32[]{:S(2)}, u32[]{:S(2)}) async-start(bf16[16,4,4096]{2,1,0:T(4,128)(2,1)} %reshape.122), calls=%async_computation.2 | async-start | bytes 1048576 | tf_op jit(solution)/shard_map/all_to_all | solution.py:118
  98.0 3.8 %copy-start.2 = (bf16[64,4096]{1,0:T(8,128)(2,1)S(1)}, bf16[64,4096]{1,0:T(8,128)(2,1)}, u32[]{:S(2)}) copy-start(bf16[64,4096]{1,0:T(8,128)(2,1)} %reshape.121) | copy-start | bytes 1572868
  98.0 6.5 %copy-start.5 = (bf16[64,4096]{1,0:T(8,128)(2,1)S(1)}, bf16[64,4096]{1,0:T(8,128)(2,1)}, u32[]{:S(2)}) copy-start(bf16[64,4096]{1,0:T(8,128)(2,1)} %reshape.119) | copy-start | bytes 1572868
Sparse Core Ops, SparseCore 0:
  26.8 35.2 all-reduce.2
where the time goes:
time: 125 us; the launch traced here: 124 us
  waiting for transfers between devices  51 us (41%)
  matrix products  20.2 us (16%)
  starting transfers between devices  16.2 us (13%)
  local copies, waits for them, and re-layouts  15.3 us (12%)
  between operations  14.8 us (12%)
  other arithmetic  6.27 us (5%)
    unnamed x2, waiting for transfers between devices  36.5 us
    all_to_all x1, waiting for transfers between devices, body(): lax.all_to_all(spread_grad, ('resp', 'expert'), split_axis=0, concat_axis...  9.17 us
    dot_general x3, matrix products, contract_first(): lax.dot_general(left, right, (((0,), (0,)), ((), ())), preferred_element_...  9.14 us
    all_to_all x1, starting transfers between devices, body(): lax.all_to_all(spread_in, ('resp', 'expert'), split_axis=0, concat_axis=0...  7.44 us
    dot_general x3, matrix products, contract_last(): lax.dot_general(left, right, (((1,), (1,)), ((), ())), preferred_element_...  6.64 us
    all_to_all x1, waiting for transfers between devices, body(): lax.all_to_all(partial_value.reshape(n_resp * experts, slots, width), ('r...  5.3 us
    all_to_all x1, starting transfers between devices, body(): lax.all_to_all(spread_grad, ('resp', 'expert'), split_axis=0, concat_axis...  4.46 us
    all_to_all x1, starting transfers between devices, body(): lax.all_to_all(partial_value.reshape(n_resp * experts, slots, width), ('r...  4.23 us
  transfers between devices with their start and end apart: 4, of which 3 were waited for; matrix products, arithmetic and copies ran while one was open for 14% of the time, Pallas kernels for 0%

commit v1 on v0

v1 whole, which is shorter than its diff:
```python
import functools

import jax
import jax.numpy as jnp
from jax import lax
from jax.experimental import pallas as pl
from jax.experimental.pallas import tpu as pltpu
from jax.sharding import PartitionSpec as P

LANES = 128
VMEM = pl.BlockSpec(memory_space=pltpu.VMEM)
SMEM = pl.BlockSpec(memory_space=pltpu.SMEM)


def params(mib):
    return pltpu.CompilerParams(vmem_limit_bytes=mib * 2**20)


def contract_last(left, right):
    return lax.dot_general(
        left, right, (((1,), (1,)), ((), ())), preferred_element_type=jnp.float32
    )


def contract_first(left, right):
    return lax.dot_general(
        left, right, (((0,), (0,)), ((), ())), preferred_element_type=jnp.float32
    )


def along(axis, size, by):
    return lambda value: lax.ppermute(value, axis, [(i, (i + by) % size) for i in range(size)])


def other_core(value, size):
    return lax.ppermute(value, "expert", [(i, i ^ 1) for i in range(size)])


def router_row(routes, weights, row, top, experts):
    lane = lax.broadcasted_iota(jnp.int32, (1, LANES), 1)
    dense = jnp.zeros((1, LANES), jnp.float32)
    for k in range(top):
        dense = dense + jnp.where(lane % experts == routes(row, k), weights(row, k), 0.0)
    high = dense.astype(jnp.bfloat16).astype(jnp.float32)
    middle = (dense - high).astype(jnp.bfloat16).astype(jnp.float32)
    low = dense - high - middle
    part = lane // experts
    return jnp.where(part == 0, high, jnp.where(part == 1, middle, jnp.where(part == 2, low, 0.0)))


def prepare_kernel(experts, x_prompt, x_resp, prompt_cot, resp_cot, route_p, route_r, weight_p, weight_r, sent_r, sent_p, *shares):
    width = x_prompt.shape[-1]
    rows_p = x_prompt.shape[1]
    responses, length = x_resp.shape[1:3]
    top = route_p.shape[-2]
    x = [x_resp[0, i].astype(jnp.float32) for i in range(responses)]
    dy = [resp_cot[0, i].astype(jnp.float32) for i in range(responses)]
    sent_r[:, :width] = jnp.concatenate(x + dy, axis=0).astype(jnp.bfloat16)
    rows = [
        router_row(lambda t, k: route_r[0, i, k, t], lambda t, k: weight_r[0, i, k, t], t, top, experts)
        for i in range(responses)
        for t in range(length)
    ]
    rows.append(jnp.zeros((len(rows), LANES), jnp.float32))
    sent_r[:, width:] = jnp.concatenate(rows, axis=0).astype(jnp.bfloat16)
    sent_p[:, :width] = x_prompt[0]
    rows = [
        router_row(lambda t, k: route_p[0, k, t], lambda t, k: weight_p[0, k, t], t, top, experts)
        for t in range(rows_p)
    ]
    sent_p[:, width:] = jnp.concatenate(rows, axis=0).astype(jnp.bfloat16)
    cot = prompt_cot[0, 0].astype(jnp.float32)
    for i in range(1, responses):
        cot = cot + prompt_cot[0, i].astype(jnp.float32)
    rows = cot.shape[0]
    here = lax.axis_index("resp") * rows_p
    cot = pltpu.roll(cot, (rows - here) % rows, 0)
    for k, share in enumerate(shares):
        share[...] = cot[k * rows_p : (k + 1) * rows_p].astype(jnp.bfloat16)


def expert_kernel(count, spans, experts, *refs):
    width = refs[2 * count].shape[-1]
    blocks_r, blocks_p = refs[:count], refs[count : 2 * count]
    gate_w, up_w, down_w, part, rows_out, gate_out, up_out, hidden_out = refs[2 * count :]
    span_r, span_p = spans
    tails = []
    base = 0
    for block in (*blocks_r, *blocks_p):
        rows = block.shape[0]
        rows_out[base : base + rows, :] = block[:, :width]
        tails.append(block[:, width:].astype(jnp.float32))
        base += rows
    total = base
    split = sum(b.shape[0] for b in blocks_r)
    tail = jnp.concatenate(tails, axis=0)
    lane = lax.broadcasted_iota(jnp.int32, tail.shape, 1)
    mine = (lane % experts == lax.axis_index("expert")) & (lane < 3 * experts)
    router = jnp.sum(jnp.where(mine, tail, 0.0), axis=1, keepdims=True)
    values = rows_out[...]
    gate = contract_last(values, gate_w[0])
    upward = contract_last(values, up_w[0])
    wide = contract_last(values, down_w[0])

    def moved(value, up):
        top, low = value[:split], value[split:]
        by_r, by_p = (split - span_r, total - split - span_p) if up else (span_r, span_p)
        return jnp.concatenate([pltpu.roll(top, by_r, 0), pltpu.roll(low, by_p, 0)], axis=0)

    sigma = jax.nn.sigmoid(gate)
    active = gate * sigma
    hidden = router * active * upward
    hidden_grad = router * moved(wide, True)
    gate_grad = (hidden_grad * upward * sigma * (1.0 + gate * (1.0 - sigma))).astype(jnp.bfloat16)
    upward_grad = (hidden_grad * active).astype(jnp.bfloat16)
    gate_out[...] = gate_grad
    up_out[...] = upward_grad
    hidden_out[...] = moved(hidden, False).astype(jnp.bfloat16)
    tokens = part.shape[0]
    each = span_r + span_p
    slot = lax.broadcasted_iota(jnp.int32, (tokens, total), 0)
    row = lax.broadcasted_iota(jnp.int32, (tokens, total), 1)
    source, token = slot // each, slot % each
    from_r = source * (2 * span_r) + token
    from_p = split + source * (2 * span_p) + token - span_r
    chosen = (row == jnp.where(token < span_r, from_r, from_p)).astype(jnp.float32).astype(jnp.bfloat16)
    gate_grad = jnp.dot(chosen, gate_grad, preferred_element_type=jnp.float32).astype(jnp.bfloat16)
    upward_grad = jnp.dot(chosen, upward_grad, preferred_element_type=jnp.float32).astype(jnp.bfloat16)
    step = 1024 if width % 1024 == 0 else width
    for c in range(0, width, step):
        value = jnp.dot(gate_grad, gate_w[0, :, c : c + step], preferred_element_type=jnp.float32)
        value = value + jnp.dot(upward_grad, up_w[0, :, c : c + step], preferred_element_type=jnp.float32)
        part[:, c : c + step] = value.astype(jnp.bfloat16)


def body(
    x_prompt,
    x_resp,
    prompt_cot,
    resp_cot,
    route_prompt,
    route_resp,
    weight_prompt,
    weight_resp,
    w_gate,
    w_up,
    w_down,
):
    n_resp = lax.axis_size("resp")
    n_expert = lax.axis_size("expert")
    chips = n_expert // 2
    experts = n_expert * w_gate.shape[0]
    hidden_units = w_gate.shape[1]
    width = x_prompt.shape[-1]
    rows_p = x_prompt.shape[1]
    rows_r = x_resp.shape[1] * x_resp.shape[2]
    bf16 = jnp.bfloat16

    sent_r, half_p, *shares = pl.pallas_call(
        functools.partial(prepare_kernel, experts),
        out_shape=[
            jax.ShapeDtypeStruct((2 * rows_r, width + LANES), bf16),
            jax.ShapeDtypeStruct((rows_p, width + LANES), bf16),
        ]
        + [jax.ShapeDtypeStruct((rows_p, width), bf16)] * n_resp,
        in_specs=[VMEM] * 4 + [SMEM] * 4,
        out_specs=[VMEM] * (2 + n_resp),
        compiler_params=params(16),
        name="prepare",
    )(
        x_prompt,
        x_resp,
        prompt_cot,
        resp_cot,
        jnp.swapaxes(route_prompt, -1, -2),
        jnp.swapaxes(route_resp, -1, -2),
        jnp.swapaxes(weight_prompt, -1, -2),
        jnp.swapaxes(weight_resp, -1, -2),
    )

    def gather(message):
        line = jnp.concatenate([message] + [along("resp", n_resp, k)(message) for k in range(1, n_resp)], axis=0)
        near = [line] + [along("expert", n_expert, 2 * j)(line) for j in range(1, chips)]
        return near + [other_core(block, n_expert) for block in near]

    all_r = gather(sent_r)
    dy_prompt = shares[0].astype(jnp.float32)
    for k in range(1, n_resp):
        dy_prompt = dy_prompt + along("resp", n_resp, k)(shares[k]).astype(jnp.float32)
    dy_prompt = jnp.pad(dy_prompt.astype(bf16), ((0, 0), (0, LANES)))
    all_p = gather(jnp.concatenate([half_p, dy_prompt], axis=0))

    count = len(all_r)
    rows = sum(b.shape[0] for b in (*all_r, *all_p))
    tokens = rows // 2
    part, values, gate_grad, upward_grad, hidden = pl.pallas_call(
        functools.partial(expert_kernel, count, (rows_r, rows_p), experts),
        out_shape=[
            jax.ShapeDtypeStruct((tokens, width), bf16),
            jax.ShapeDtypeStruct((rows, width), bf16),
        ]
        + [jax.ShapeDtypeStruct((rows, hidden_units), bf16)] * 3,
        in_specs=[VMEM] * (2 * count + 3),
        out_specs=[VMEM] * 5,
        compiler_params=params(60),
        cost_estimate=pl.CostEstimate(flops=10 * rows * width * hidden_units, bytes_accessed=20 * 2**20, transcendentals=0),
        name="expert",
    )(*all_r, *all_p, w_gate, w_up, w_down)

    half = tokens // 2
    total = part[:half].astype(jnp.float32) + other_core(part[half:], n_expert).astype(jnp.float32)
    total = total.astype(bf16)
    block = half // chips
    line = total[:block].astype(jnp.float32)
    for j in range(1, chips):
        line = line + along("expert", n_expert, -2 * j)(total[j * block : (j + 1) * block]).astype(jnp.float32)
    line = line.astype(bf16)
    each = rows_r + rows_p
    own = line[:each].astype(jnp.float32)
    for k in range(1, n_resp):
        own = own + along("resp", n_resp, -k)(line[k * each : (k + 1) * each]).astype(jnp.float32)
    own = own.astype(bf16)

    grad_gate = contract_first(gate_grad, values).astype(bf16)[None]
    grad_up = contract_first(upward_grad, values).astype(bf16)[None]
    grad_down = contract_first(hidden, values).astype(bf16)[None]
    return (own[rows_r:][None], own[:rows_r].reshape(x_resp.shape), grad_gate, grad_up, grad_down)


def solution(mesh):
    return jax.shard_map(
        body,
        mesh=mesh,
        in_specs=(
            P(("groups", "expert"), "resp", None),
            P(("groups", "expert"), "resp", None, None),
            P(("groups", "expert"), "resp", None, None),
            P(("groups", "expert"), "resp", None, None),
            P(("groups", "expert"), "resp", None),
            P(("groups", "expert"), "resp", None, None),
            P(("groups", "expert"), "resp", None),
            P(("groups", "expert"), "resp", None, None),
            P("expert", "resp", None),
            P("expert", "resp", None),
            P("expert", "resp", None),
        ),
        out_specs=(
            P(("groups", "expert"), "resp", None),
            P(("groups", "expert"), "resp", None, None),
            P(("groups", "expert"), "resp", None),
            P(("groups", "expert"), "resp", None),
            P(("groups", "expert"), "resp", None),
        ),
        check_vma=False,
    )
```

time: 125 us -> 74.4 us (0.60)
  waiting for transfers between devices: 51 us -> 23.9 us
  between operations: 14.8 us -> 0.84 us
  matrix products: 20.2 us -> 9.63 us
  Pallas kernels: 0 us -> 10.4 us
  other arithmetic: 6.27 us -> 0.26 us
  local copies, waits for them, and re-layouts: 15.3 us -> 10 us
  starting transfers between devices: 16.2 us -> 18.9 us
    unnamed x2 -> x0, waiting for transfers between devices: 36.5 us -> none
    ppermute x0 -> x20, waiting for transfers between devices: none -> 23.9 us  [the longest x15 22.6 us: along(): lax.ppermute(value, axis, [(i, (i + by) % size) for i in range(size)])]
    ppermute x0 -> x20, starting transfers between devices: none -> 18.9 us  [the longest x15 18.1 us: along(): lax.ppermute(value, axis, [(i, (i + by) % size) for i in range(size)])]
    all_to_all x3 -> x0, starting transfers between devices: 16.1 us -> none  [the longest x1 7.44 us: body(): lax.all_to_all(spread_in, ('resp', 'expert'), split_axis=0, concat_axis=0...]
    all_to_all x3 -> x0, waiting for transfers between devices: 14.5 us -> none  [the longest x1 9.17 us: body(): lax.all_to_all(spread_grad, ('resp', 'expert'), split_axis=0, concat_axis...]
    dot_general x8 -> x0, matrix products: 11.1 us -> none  [the longest x3 6.64 us: contract_last(): lax.dot_general(left, right, (((1,), (1,)), ((), ())), preferred_element_...]
    pallas_call x0 -> x2, Pallas kernels: none -> 10.4 us  [the longest x1 9.78 us: body(): pl.pallas_call(functools.partial(expert_kernel, count, (rows_r, rows_p),...]
    reshape x4 -> x1, local copies, waits for them, and re-layouts: 7.95 us -> 0.63 us  [body(): own[:rows_r].reshape(x_resp.shape)]
  transfers between devices with their start and end apart: 4 -> 20, of which waited for: 3 -> 11; matrix products, arithmetic and copies ran while one was open for 14% -> 13% of each run, Pallas kernels for 0% -> 0%
where the time goes in v1:
time: 74.4 us; the launch traced here: 74 us
  waiting for transfers between devices  23.9 us (32%)
  starting transfers between devices  18.9 us (25%)
  Pallas kernels  10.4 us (14%)
  local copies, waits for them, and re-layouts  10 us (13%)
  matrix products  9.63 us (13%)
  between operations  0.84 us (1%)
    ppermute x15, waiting for transfers between devices, along(): lax.ppermute(value, axis, [(i, (i + by) % size) for i in range(size)])  22.6 us
    ppermute x15, starting transfers between devices, along(): lax.ppermute(value, axis, [(i, (i + by) % size) for i in range(size)])  18.1 us
    pallas_call x1, Pallas kernels, body(): pl.pallas_call(functools.partial(expert_kernel, count, (rows_r, rows_p),...  9.78 us
    dot_general x3, matrix products, contract_first(): lax.dot_general(left, right, (((0,), (0,)), ((), ())), preferred_element_...  9.63 us
    unnamed x41, local copies, waits for them, and re-layouts  7.43 us
  transfers between devices with their start and end apart: 20, of which 11 were waited for; matrix products, arithmetic and copies ran while one was open for 13% of the time, Pallas kernels for 0%

profile of v1, /device:TPU:0, one launch (start us, length us, event | category | flops | bytes accessed | tf_op | source)
XLA Modules:
  0.0 74.0 jit_solution(767305694984393456)
XLA Ops:
  0.6 0.8 %copy.16 = s32[1,2,2]{1,2,0:T(2,128)S(1)} copy(s32[1,2,2]{2,1,0:T(2,128)} %param.15) | data formatting | bytes 32 | tf_op args[4]
  1.4 0.8 %copy.17 = f32[1,2,2]{1,2,0:T(2,128)S(1)} copy(f32[1,2,2]{2,1,0:T(2,128)} %param.17) | data formatting | bytes 32 | tf_op args[6]
  2.2 0.8 %copy-done = bf16[1,1,8,4096]{3,2,1,0:T(8,128)(2,1)S(1)} copy-done((bf16[1,1,8,4096]{3,2,1,0:T(8,128)(2,1)S(1)}, bf16[1,1,8,4096]{3,2,1,0:T(8,128)(2,1)}, u32[]{:S(2)}) %copy-start) | copy-done | bytes 65560
  3.0 0.8 %copy-done.1 = bf16[1,1,4,4096]{3,2,1,0:T(4,128)(2,1)S(1)} copy-done((bf16[1,1,4,4096]{3,2,1,0:T(4,128)(2,1)S(1)}, bf16[1,1,4,4096]{3,2,1,0:T(4,128)(2,1)}, u32[]{:S(2)}) %copy-start.1) | copy-done | bytes 32792
  3.8 0.8 %copy-done.2 = bf16[1,1,4,4096]{3,2,1,0:T(4,128)(2,1)S(1)} copy-done((bf16[1,1,4,4096]{3,2,1,0:T(4,128)(2,1)S(1)}, bf16[1,1,4,4096]{3,2,1,0:T(4,128)(2,1)}, u32[]{:S(2)}) %copy-start.2) | copy-done | bytes 32792
  4.5 0.7 copy-done.3
  5.2 0.7 copy-done.4
  5.9 0.7 copy-done.5
  6.6 0.6 prepare.1
  7.3 5.1 %collective-permute-start.2 = (bf16[8,4224]{1,0:T(8,128)(2,1)S(1)}, bf16[8,4224]{1,0:T(8,128)(2,1)S(1)}, u32[]{:S(2)}, u32[]{:S(2)}) collective-permute-start(bf16[8,4224]{1,0:T(8,128)(2,1)S(1)} %get-tuple-element.16), channel_id=1, source_target_pairs={{0,12},{4,0},{8,4},{12,8},{1,13},{5,1},{9,5},{13,9},{2,14},{6,2},{... | collective-permute-start | bytes 202760 | tf_op jit(solution)/shard_map/ppermute | solution.py:32
  12.4 1.0 %collective-permute-start.6 = (bf16[2,4096]{1,0:T(2,128)(2,1)S(1)}, bf16[2,4096]{1,0:T(2,128)(2,1)S(1)}, u32[]{:S(2)}, u32[]{:S(2)}) collective-permute-start(bf16[2,4096]{1,0:T(2,128)(2,1)S(1)} %get-tuple-element.19), channel_id=1, source_target_pairs={{0,4},{4,8},{8,12},{12,0},{1,5},{5,9},{9,13},{13,1},{2,6},{6,10},{... | collective-permute-start | bytes 49160 | tf_op jit(solution)/shard_map/ppermute | solution.py:32
  13.4 1.9 %collective-permute-start.7 = (bf16[2,4096]{1,0:T(2,128)(2,1)S(1)}, bf16[2,4096]{1,0:T(2,128)(2,1)S(1)}, u32[]{:S(2)}, u32[]{:S(2)}) collective-permute-start(bf16[2,4096]{1,0:T(2,128)(2,1)S(1)} %get-tuple-element.20), channel_id=1, source_target_pairs={{0,8},{4,12},{8,0},{12,4},{1,9},{5,13},{9,1},{13,5},{2,10},{6,14},... | collective-permute-start | bytes 49160 | tf_op jit(solution)/shard_map/ppermute | solution.py:32
  15.3 2.9 %collective-permute-start.8 = (bf16[2,4096]{1,0:T(2,128)(2,1)S(1)}, bf16[2,4096]{1,0:T(2,128)(2,1)S(1)}, u32[]{:S(2)}, u32[]{:S(2)}) collective-permute-start(bf16[2,4096]{1,0:T(2,128)(2,1)S(1)} %get-tuple-element.21), channel_id=1, source_target_pairs={{0,12},{4,0},{8,4},{12,8},{1,13},{5,1},{9,5},{13,9},{2,14},{6,2},{... | collective-permute-start | bytes 49160 | tf_op jit(solution)/shard_map/ppermute | solution.py:32
  18.2 0.1 collective-permute-start
  18.3 0.3 collective-permute-done.7
  18.6 1.0 %collective-permute-done.8 = bf16[2,4096]{1,0:T(2,128)(2,1)S(1)} collective-permute-done((bf16[2,4096]{1,0:T(2,128)(2,1)S(1)}, bf16[2,4096]{1,0:T(2,128)(2,1)S(1)}, u32[]{:S(2)}, u32[]{:S(2)}) %collective-permute-start.8) | collective-permute-done | bytes 16416 | tf_op jit(solution)/shard_map/ppermute | solution.py:32
  19.7 4.6 %collective-permute-done = bf16[8,4224]{1,0:T(8,128)(2,1)S(1)} collective-permute-done((bf16[8,4224]{1,0:T(8,128)(2,1)S(1)}, bf16[8,4224]{1,0:T(8,128)(2,1)S(1)}, u32[]{:S(2)}, u32[]{:S(2)}) %collective-permute-start) | collective-permute-done | bytes 67616 | tf_op jit(solution)/shard_map/ppermute | solution.py:32
  24.4 1.7 %collective-permute-start.3 = (bf16[32,4224]{1,0:T(8,128)(2,1)S(1)}, bf16[32,4224]{1,0:T(8,128)(2,1)S(1)}, u32[]{:S(2)}, u32[]{:S(2)}) collective-permute-start(bf16[32,4224]{1,0:T(8,128)(2,1)S(1)} %constant_dynamic-update-slice_fusion.refs_0_), channel_id=1, source_target_pairs={{0,2},{1,3},{2,0},{3,1},{4,6},{5,7},{6,4},{7,5},{8,10},{9,11},{10,... | collective-permute-start | bytes 811016 | tf_op jit(solution)/shard_map/ppermute | solution.py:32
  26.2 0.1 collective-permute-start.10
  26.3 1.9 %collective-permute-start.9 = (bf16[4,4224]{1,0:T(4,128)(2,1)S(1)}, bf16[4,4224]{1,0:T(4,128)(2,1)S(1)}, u32[]{:S(2)}, u32[]{:S(2)}) collective-permute-start(bf16[4,4224]{1,0:T(4,128)(2,1)S(1)} %pad_maximum_fusion), channel_id=1, source_target_pairs={{0,4},{4,8},{8,12},{12,0},{1,5},{5,9},{9,13},{13,1},{2,6},{6,10},{... | collective-permute-start | bytes 101384 | tf_op jit(solution)/shard_map/ppermute | solution.py:32
  28.2 1.9 %collective-permute-done.11 = bf16[4,4224]{1,0:T(4,128)(2,1)S(1)} collective-permute-done((bf16[4,4224]{1,0:T(4,128)(2,1)S(1)}, bf16[4,4224]{1,0:T(4,128)(2,1)S(1)}, u32[]{:S(2)}, u32[]{:S(2)}) %collective-permute-start.11) | collective-permute-done | bytes 33824 | tf_op jit(solution)/shard_map/ppermute | solution.py:32
  30.1 1.0 %collective-permute-done.10 = bf16[4,4224]{1,0:T(4,128)(2,1)S(1)} collective-permute-done((bf16[4,4224]{1,0:T(4,128)(2,1)S(1)}, bf16[4,4224]{1,0:T(4,128)(2,1)S(1)}, u32[]{:S(2)}, u32[]{:S(2)}) %collective-permute-start.10) | collective-permute-done | bytes 33824 | tf_op jit(solution)/shard_map/ppermute | solution.py:32
  31.1 1.7 %collective-permute-done.9 = bf16[4,4224]{1,0:T(4,128)(2,1)S(1)} collective-permute-done((bf16[4,4224]{1,0:T(4,128)(2,1)S(1)}, bf16[4,4224]{1,0:T(4,128)(2,1)S(1)}, u32[]{:S(2)}, u32[]{:S(2)}) %collective-permute-start.9) | collective-permute-done | bytes 33824 | tf_op jit(solution)/shard_map/ppermute | solution.py:32
  32.9 0.1 concatenate.12.refs_4_
  33.0 0.5 collective-permute-start.12
  33.5 0.5 collective-permute-start.5
  34.0 0.1 collective-permute-start.13
  34.1 4.0 %collective-permute-done.12.refs_5_ = bf16[16,4224]{1,0:T(8,128)(2,1)S(1)} collective-permute-done((bf16[16,4224]{1,0:T(8,128)(2,1)S(1)}, bf16[16,4224]{1,0:T(8,128)(2,1)S(1)}, u32[]{:S(2)}, u32[]{:S(2)}) %collective-permute-start.12) | collective-permute-done | bytes 135200 | tf_op jit(solution)/shard_map/ppermute | solution.py:32
  38.1 1.3 %collective-permute-done.14.refs_7_ = bf16[16,4224]{1,0:T(8,128)(2,1)S(1)} collective-permute-done((bf16[16,4224]{1,0:T(8,128)(2,1)S(1)}, bf16[16,4224]{1,0:T(8,128)(2,1)S(1)}, u32[]{:S(2)}, u32[]{:S(2)}) %collective-permute-start.14) | collective-permute-done | bytes 135200 | tf_op jit(solution)/shard_map/ppermute | solution.py:36
  39.5 0.6 copy-done.17
  40.1 0.1 copy-done.13
  40.2 0.7 copy-done.14
  40.9 9.8 %expert.1 = (bf16[96,4096]{1,0:T(8,128)(2,1)}, bf16[192,4096]{1,0:T(8,128)(2,1)}, bf16[192,384]{1,0:T(8,128)(2,1)}, bf16[192,384]{1,0:T(8,128)(2,1)}, bf16[192,384]{1,0:T(8,128)(2,1)}) custom-call(bf16[32,4224]{1,0:T(8,128)(2,1)} %copy-done.11, bf16[32,4224]{1,0:T(8,128)(2,1)} %copy-done.12, bf16[32,4224]{1,0:T(8,128)(2,1)} %copy-done.13, ...), custom_call_target="tpu_custom_call" | custom-call | flops 3019898880 | bytes 20971520 | tf_op jit(solution)/shard_map/expert/pallas_call | solution.py:196
  50.7 1.1 %slice.31 = bf16[48,4096]{1,0:T(8,128)(2,1)S(1)} slice(bf16[96,4096]{1,0:T(8,128)(2,1)} %get-tuple-element.22), slice={[48:96], [0:4096]} | slice | bytes 786432 | tf_op jit(solution)/shard_map/slice | solution.py:211
  51.8 0.2 collective-permute-start.15
  52.0 4.3 %fusion = bf16[1,384,4096]{2,1,0:T(8,128)(2,1)} fusion(bf16[192,384]{1,0:T(8,128)(2,1)} %get-tuple-element.23, bf16[192,4096]{1,0:T(8,128)(2,1)} %get-tuple-element.24), kind=kOutput, calls=%fused_computation.3 | convolution fusion | flops 605552640 | bytes 4866048 | tf_op jit(solution)/shard_map/dot_general | solution.py:26
  56.3 0.1 add_convert_fusion
  56.4 0.5 collective-permute-start.16
  56.9 2.7 %fusion.1 = bf16[1,384,4096]{2,1,0:T(8,128)(2,1)} fusion(bf16[192,384]{1,0:T(8,128)(2,1)S(1)} %copy-done.9, bf16[192,4096]{1,0:T(8,128)(2,1)S(1)} %copy-done.6), kind=kOutput, calls=%fused_computation.4 | convolution fusion | flops 605552640 | bytes 4866048 | tf_op jit(solution)/shard_map/dot_general | solution.py:26
  59.6 4.1 %collective-permute-done.16 = bf16[24,4096]{1,0:T(8,128)(2,1)S(1)} collective-permute-done((bf16[24,4096]{1,0:T(8,128)(2,1)S(1)}, bf16[24,4096]{1,0:T(8,128)(2,1)S(1)}, u32[]{:S(2)}, u32[]{:S(2)}) %collective-permute-start.16) | collective-permute-done | bytes 196640 | tf_op jit(solution)/shard_map/ppermute | solution.py:32
  63.8 1.7 %collective-permute-start.17 = (bf16[6,4096]{1,0:T(8,128)(2,1)S(1)}, bf16[6,4096]{1,0:T(8,128)(2,1)S(1)}, u32[]{:S(2)}, u32[]{:S(2)}) collective-permute-start(bf16[6,4096]{1,0:T(8,128)(2,1)S(1)} %get-tuple-element.27), channel_id=1, source_target_pairs={{0,12},{4,0},{8,4},{12,8},{1,13},{5,1},{9,5},{13,9},{2,14},{6,2},{... | collective-permute-start | bytes 147464 | tf_op jit(solution)/shard_map/ppermute | solution.py:32
  65.5 0.4 collective-permute-start.19
  65.9 0.3 collective-permute-start.18
  66.1 2.7 %fusion.2 = bf16[1,384,4096]{2,1,0:T(8,128)(2,1)} fusion(bf16[192,384]{1,0:T(8,128)(2,1)S(1)} %copy-done.8, bf16[192,4096]{1,0:T(8,128)(2,1)S(1)} %copy-done.6), kind=kOutput, calls=%fused_computation.5 | convolution fusion | flops 605552640 | bytes 4866048 | tf_op jit(solution)/shard_map/dot_general | solution.py:26
  68.8 2.7 %collective-permute-done.19 = bf16[6,4096]{1,0:T(8,128)(2,1)S(1)} collective-permute-done((bf16[6,4096]{1,0:T(8,128)(2,1)S(1)}, bf16[6,4096]{1,0:T(8,128)(2,1)S(1)}, u32[]{:S(2)}, u32[]{:S(2)}) %collective-permute-start.19) | collective-permute-done | bytes 49184 | tf_op jit(solution)/shard_map/ppermute | solution.py:32
  71.6 1.1 %collective-permute-done.18 = bf16[6,4096]{1,0:T(8,128)(2,1)S(1)} collective-permute-done((bf16[6,4096]{1,0:T(8,128)(2,1)S(1)}, bf16[6,4096]{1,0:T(8,128)(2,1)S(1)}, u32[]{:S(2)}, u32[]{:S(2)}) %collective-permute-start.18) | collective-permute-done | bytes 49184 | tf_op jit(solution)/shard_map/ppermute | solution.py:32
  72.7 0.6 slice_bitcast_fusion.1
  73.3 0.6 slice_bitcast_fusion
  (51 shorter events, 0.4 us)
Async XLA Ops:
  2.2 0.8 %copy-start = (bf16[1,1,8,4096]{3,2,1,0:T(8,128)(2,1)S(1)}, bf16[1,1,8,4096]{3,2,1,0:T(8,128)(2,1)}, u32[]{:S(2)}) copy-start(bf16[1,1,8,4096]{3,2,1,0:T(8,128)(2,1)} %prompt_cot.1) | copy-start | bytes 196612
  3.0 0.8 %copy-start.1 = (bf16[1,1,4,4096]{3,2,1,0:T(4,128)(2,1)S(1)}, bf16[1,1,4,4096]{3,2,1,0:T(4,128)(2,1)}, u32[]{:S(2)}) copy-start(bf16[1,1,4,4096]{3,2,1,0:T(4,128)(2,1)} %x_resp.1) | copy-start | bytes 98308
  3.8 0.8 %copy-start.2 = (bf16[1,1,4,4096]{3,2,1,0:T(4,128)(2,1)S(1)}, bf16[1,1,4,4096]{3,2,1,0:T(4,128)(2,1)}, u32[]{:S(2)}) copy-start(bf16[1,1,4,4096]{3,2,1,0:T(4,128)(2,1)} %resp_cot.1) | copy-start | bytes 98308
  4.5 0.7 copy-start.3
  5.2 0.7 copy-start.4
  5.9 0.7 copy-start.5
  7.3 17.1 %collective-permute-start.2 = (bf16[8,4224]{1,0:T(8,128)(2,1)S(1)}, bf16[8,4224]{1,0:T(8,128)(2,1)S(1)}, u32[]{:S(2)}, u32[]{:S(2)}) collective-permute-start(bf16[8,4224]{1,0:T(8,128)(2,1)S(1)} %get-tuple-element.16), channel_id=1, source_target_pairs={{0,12},{4,0},{8,4},{12,8},{1,13},{5,1},{9,5},{13,9},{2,14},{6,2},{... | collective-permute-start | bytes 202760 | tf_op jit(solution)/shard_map/ppermute | solution.py:32
  12.4 12.0 %collective-permute-start.1 = (bf16[8,4224]{1,0:T(8,128)(2,1)S(1)}, bf16[8,4224]{1,0:T(8,128)(2,1)S(1)}, u32[]{:S(2)}, u32[]{:S(2)}) collective-permute-start(bf16[8,4224]{1,0:T(8,128)(2,1)S(1)} %get-tuple-element.16), channel_id=1, source_target_pairs={{0,8},{4,12},{8,0},{12,4},{1,9},{5,13},{9,1},{13,5},{2,10},{6,14},... | collective-permute-start | bytes 202760 | tf_op jit(solution)/shard_map/ppermute | solution.py:32
  12.4 5.9 %collective-permute-start.6 = (bf16[2,4096]{1,0:T(2,128)(2,1)S(1)}, bf16[2,4096]{1,0:T(2,128)(2,1)S(1)}, u32[]{:S(2)}, u32[]{:S(2)}) collective-permute-start(bf16[2,4096]{1,0:T(2,128)(2,1)S(1)} %get-tuple-element.19), channel_id=1, source_target_pairs={{0,4},{4,8},{8,12},{12,0},{1,5},{5,9},{9,13},{13,1},{2,6},{6,10},{... | collective-permute-start | bytes 49160 | tf_op jit(solution)/shard_map/ppermute | solution.py:32
  13.4 5.2 %collective-permute-start.7 = (bf16[2,4096]{1,0:T(2,128)(2,1)S(1)}, bf16[2,4096]{1,0:T(2,128)(2,1)S(1)}, u32[]{:S(2)}, u32[]{:S(2)}) collective-permute-start(bf16[2,4096]{1,0:T(2,128)(2,1)S(1)} %get-tuple-element.20), channel_id=1, source_target_pairs={{0,8},{4,12},{8,0},{12,4},{1,9},{5,13},{9,1},{13,5},{2,10},{6,14},... | collective-permute-start | bytes 49160 | tf_op jit(solution)/shard_map/ppermute | solution.py:32
  15.3 4.4 %collective-permute-start.8 = (bf16[2,4096]{1,0:T(2,128)(2,1)S(1)}, bf16[2,4096]{1,0:T(2,128)(2,1)S(1)}, u32[]{:S(2)}, u32[]{:S(2)}) collective-permute-start(bf16[2,4096]{1,0:T(2,128)(2,1)S(1)} %get-tuple-element.21), channel_id=1, source_target_pairs={{0,12},{4,0},{8,4},{12,8},{1,13},{5,1},{9,5},{13,9},{2,14},{6,2},{... | collective-permute-start | bytes 49160 | tf_op jit(solution)/shard_map/ppermute | solution.py:32
  18.2 6.1 %collective-permute-start = (bf16[8,4224]{1,0:T(8,128)(2,1)S(1)}, bf16[8,4224]{1,0:T(8,128)(2,1)S(1)}, u32[]{:S(2)}, u32[]{:S(2)}) collective-permute-start(bf16[8,4224]{1,0:T(8,128)(2,1)S(1)} %get-tuple-element.16), channel_id=1, source_target_pairs={{0,4},{4,8},{8,12},{12,0},{1,5},{5,9},{9,13},{13,1},{2,6},{6,10},{... | collective-permute-start | bytes 202760 | tf_op jit(solution)/shard_map/ppermute | solution.py:32
  24.4 15.0 %copy-start.11 = (bf16[32,4224]{1,0:T(8,128)(2,1)}, bf16[32,4224]{1,0:T(8,128)(2,1)S(1)}, u32[]{:S(2)}) copy-start(bf16[32,4224]{1,0:T(8,128)(2,1)S(1)} %constant_dynamic-update-slice_fusion.refs_0_) | copy-start | bytes 811012
  24.4 9.1 %collective-permute-start.3 = (bf16[32,4224]{1,0:T(8,128)(2,1)S(1)}, bf16[32,4224]{1,0:T(8,128)(2,1)S(1)}, u32[]{:S(2)}, u32[]{:S(2)}) collective-permute-start(bf16[32,4224]{1,0:T(8,128)(2,1)S(1)} %constant_dynamic-update-slice_fusion.refs_0_), channel_id=1, source_target_pairs={{0,2},{1,3},{2,0},{3,1},{4,6},{5,7},{6,4},{7,5},{8,10},{9,11},{10,... | collective-permute-start | bytes 811016 | tf_op jit(solution)/shard_map/ppermute | solution.py:32
  26.2 4.0 %collective-permute-start.11 = (bf16[4,4224]{1,0:T(4,128)(2,1)S(1)}, bf16[4,4224]{1,0:T(4,128)(2,1)S(1)}, u32[]{:S(2)}, u32[]{:S(2)}) collective-permute-start(bf16[4,4224]{1,0:T(4,128)(2,1)S(1)} %pad_maximum_fusion), channel_id=1, source_target_pairs={{0,12},{4,0},{8,4},{12,8},{1,13},{5,1},{9,5},{13,9},{2,14},{6,2},{... | collective-permute-start | bytes 101384 | tf_op jit(solution)/shard_map/ppermute | solution.py:32
  26.2 4.9 %collective-permute-start.10 = (bf16[4,4224]{1,0:T(4,128)(2,1)S(1)}, bf16[4,4224]{1,0:T(4,128)(2,1)S(1)}, u32[]{:S(2)}, u32[]{:S(2)}) collective-permute-start(bf16[4,4224]{1,0:T(4,128)(2,1)S(1)} %pad_maximum_fusion), channel_id=1, source_target_pairs={{0,8},{4,12},{8,0},{12,4},{1,9},{5,13},{9,1},{13,5},{2,10},{6,14},... | collective-permute-start | bytes 101384 | tf_op jit(solution)/shard_map/ppermute | solution.py:32
  26.3 6.6 %collective-permute-start.9 = (bf16[4,4224]{1,0:T(4,128)(2,1)S(1)}, bf16[4,4224]{1,0:T(4,128)(2,1)S(1)}, u32[]{:S(2)}, u32[]{:S(2)}) collective-permute-start(bf16[4,4224]{1,0:T(4,128)(2,1)S(1)} %pad_maximum_fusion), channel_id=1, source_target_pairs={{0,4},{4,8},{8,12},{12,0},{1,5},{5,9},{9,13},{13,1},{2,6},{6,10},{... | collective-permute-start | bytes 101384 | tf_op jit(solution)/shard_map/ppermute | solution.py:32
  33.0 6.5 %copy-start.10 = (bf16[16,4224]{1,0:T(8,128)(2,1)}, bf16[16,4224]{1,0:T(8,128)(2,1)S(1)}, u32[]{:S(2)}) copy-start(bf16[16,4224]{1,0:T(8,128)(2,1)S(1)} %concatenate.12.refs_4_) | copy-start | bytes 405508
  33.0 5.1 %collective-permute-start.12 = (bf16[16,4224]{1,0:T(8,128)(2,1)S(1)}, bf16[16,4224]{1,0:T(8,128)(2,1)S(1)}, u32[]{:S(2)}, u32[]{:S(2)}) collective-permute-start(bf16[16,4224]{1,0:T(8,128)(2,1)S(1)} %concatenate.12.refs_4_), channel_id=1, source_target_pairs={{0,2},{1,3},{2,0},{3,1},{4,6},{5,7},{6,4},{7,5},{8,10},{9,11},{10,... | collective-permute-start | bytes 405512 | tf_op jit(solution)/shard_map/ppermute | solution.py:32
  33.5 6.0 %collective-permute-start.4 = (bf16[32,4224]{1,0:T(8,128)(2,1)S(1)}, bf16[32,4224]{1,0:T(8,128)(2,1)S(1)}, u32[]{:S(2)}, u32[]{:S(2)}) collective-permute-start(bf16[32,4224]{1,0:T(8,128)(2,1)S(1)} %constant_dynamic-update-slice_fusion.refs_0_), channel_id=1, source_target_pairs={{0,1},{1,0},{2,3},{3,2},{4,5},{5,4},{6,7},{7,6},{8,9},{9,8},{10,11... | collective-permute-start | bytes 811016 | tf_op jit(solution)/shard_map/ppermute | solution.py:36
  33.5 6.0 %copy-start.12 = (bf16[32,4224]{1,0:T(8,128)(2,1)}, bf16[32,4224]{1,0:T(8,128)(2,1)S(1)}, u32[]{:S(2)}) copy-start(bf16[32,4224]{1,0:T(8,128)(2,1)S(1)} %collective-permute-done.3.refs_1_) | copy-start | bytes 811012
  33.5 6.0 %collective-permute-start.5 = (bf16[32,4224]{1,0:T(8,128)(2,1)S(1)}, bf16[32,4224]{1,0:T(8,128)(2,1)S(1)}, u32[]{:S(2)}, u32[]{:S(2)}) collective-permute-start(bf16[32,4224]{1,0:T(8,128)(2,1)S(1)} %collective-permute-done.3.refs_1_), channel_id=1, source_target_pairs={{0,1},{1,0},{2,3},{3,2},{4,5},{5,4},{6,7},{7,6},{8,9},{9,8},{10,11... | collective-permute-start | bytes 811016 | tf_op jit(solution)/shard_map/ppermute | solution.py:36
  34.0 4.1 %collective-permute-start.13 = (bf16[16,4224]{1,0:T(8,128)(2,1)S(1)}, bf16[16,4224]{1,0:T(8,128)(2,1)S(1)}, u32[]{:S(2)}, u32[]{:S(2)}) collective-permute-start(bf16[16,4224]{1,0:T(8,128)(2,1)S(1)} %concatenate.12.refs_4_), channel_id=1, source_target_pairs={{0,1},{1,0},{2,3},{3,2},{4,5},{5,4},{6,7},{7,6},{8,9},{9,8},{10,11... | collective-permute-start | bytes 405512 | tf_op jit(solution)/shard_map/ppermute | solution.py:36
  38.1 1.4 %copy-start.15 = (bf16[16,4224]{1,0:T(8,128)(2,1)}, bf16[16,4224]{1,0:T(8,128)(2,1)S(1)}, u32[]{:S(2)}) copy-start(bf16[16,4224]{1,0:T(8,128)(2,1)S(1)} %collective-permute-done.12.refs_5_) | copy-start | bytes 405508
  38.1 1.4 %collective-permute-start.14 = (bf16[16,4224]{1,0:T(8,128)(2,1)S(1)}, bf16[16,4224]{1,0:T(8,128)(2,1)S(1)}, u32[]{:S(2)}, u32[]{:S(2)}) collective-permute-start(bf16[16,4224]{1,0:T(8,128)(2,1)S(1)} %collective-permute-done.12.refs_5_), channel_id=1, source_target_pairs={{0,1},{1,0},{2,3},{3,2},{4,5},{5,4},{6,7},{7,6},{8,9},{9,8},{10,11... | collective-permute-start | bytes 405512 | tf_op jit(solution)/shard_map/ppermute | solution.py:36
  38.1 1.4 %copy-start.16 = (bf16[16,4224]{1,0:T(8,128)(2,1)}, bf16[16,4224]{1,0:T(8,128)(2,1)S(1)}, u32[]{:S(2)}) copy-start(bf16[16,4224]{1,0:T(8,128)(2,1)S(1)} %collective-permute-done.13.refs_6_) | copy-start | bytes 405508
  39.4 0.7 copy-start.17
  39.4 0.8 %copy-start.13 = (bf16[32,4224]{1,0:T(8,128)(2,1)}, bf16[32,4224]{1,0:T(8,128)(2,1)S(1)}, u32[]{:S(2)}) copy-start(bf16[32,4224]{1,0:T(8,128)(2,1)S(1)} %collective-permute-done.4.refs_2_) | copy-start | bytes 811012
  40.2 0.7 copy-start.14
  50.7 5.6 %copy-start.7 = (bf16[96,4096]{1,0:T(8,128)(2,1)S(1)}, bf16[96,4096]{1,0:T(8,128)(2,1)}, u32[]{:S(2)}) copy-start(bf16[96,4096]{1,0:T(8,128)(2,1)} %get-tuple-element.22) | copy-start | bytes 2359300
  51.8 4.5 %collective-permute-start.15 = (bf16[48,4096]{1,0:T(8,128)(2,1)S(1)}, bf16[48,4096]{1,0:T(8,128)(2,1)S(1)}, u32[]{:S(2)}, u32[]{:S(2)}) collective-permute-start(bf16[48,4096]{1,0:T(8,128)(2,1)S(1)} %slice.31), channel_id=1, source_target_pairs={{0,1},{1,0},{2,3},{3,2},{4,5},{5,4},{6,7},{7,6},{8,9},{9,8},{10,11... | collective-permute-start | bytes 1179656 | tf_op jit(solution)/shard_map/ppermute | solution.py:36
  52.0 4.9 %copy-start.6 = (bf16[192,4096]{1,0:T(8,128)(2,1)S(1)}, bf16[192,4096]{1,0:T(8,128)(2,1)}, u32[]{:S(2)}) copy-start(bf16[192,4096]{1,0:T(8,128)(2,1)} %get-tuple-element.24) | copy-start | bytes 4718596
  52.0 4.9 %copy-start.9 = (bf16[192,384]{1,0:T(8,128)(2,1)S(1)}, bf16[192,384]{1,0:T(8,128)(2,1)}, u32[]{:S(2)}) copy-start(bf16[192,384]{1,0:T(8,128)(2,1)} %get-tuple-element.25) | copy-start | bytes 442372
  56.4 9.7 %copy-start.8 = (bf16[192,384]{1,0:T(8,128)(2,1)S(1)}, bf16[192,384]{1,0:T(8,128)(2,1)}, u32[]{:S(2)}) copy-start(bf16[192,384]{1,0:T(8,128)(2,1)} %get-tuple-element.26) | copy-start | bytes 442372
  56.4 7.2 %collective-permute-start.16 = (bf16[24,4096]{1,0:T(8,128)(2,1)S(1)}, bf16[24,4096]{1,0:T(8,128)(2,1)S(1)}, u32[]{:S(2)}, u32[]{:S(2)}) collective-permute-start(bf16[24,4096]{1,0:T(8,128)(2,1)S(1)} %slice.41), channel_id=1, source_target_pairs={{0,2},{1,3},{2,0},{3,1},{4,6},{5,7},{6,4},{7,5},{8,10},{9,11},{10,... | collective-permute-start | bytes 589832 | tf_op jit(solution)/shard_map/ppermute | solution.py:32
  63.8 5.0 %collective-permute-start.17 = (bf16[6,4096]{1,0:T(8,128)(2,1)S(1)}, bf16[6,4096]{1,0:T(8,128)(2,1)S(1)}, u32[]{:S(2)}, u32[]{:S(2)}) collective-permute-start(bf16[6,4096]{1,0:T(8,128)(2,1)S(1)} %get-tuple-element.27), channel_id=1, source_target_pairs={{0,12},{4,0},{8,4},{12,8},{1,13},{5,1},{9,5},{13,9},{2,14},{6,2},{... | collective-permute-start | bytes 147464 | tf_op jit(solution)/shard_map/ppermute | solution.py:32
  65.5 6.1 %collective-permute-start.19 = (bf16[6,4096]{1,0:T(8,128)(2,1)S(1)}, bf16[6,4096]{1,0:T(8,128)(2,1)S(1)}, u32[]{:S(2)}, u32[]{:S(2)}) collective-permute-start(bf16[6,4096]{1,0:T(8,128)(2,1)S(1)} %get-tuple-element.28), channel_id=1, source_target_pairs={{0,4},{4,8},{8,12},{12,0},{1,5},{5,9},{9,13},{13,1},{2,6},{6,10},{... | collective-permute-start | bytes 147464 | tf_op jit(solution)/shard_map/ppermute | solution.py:32
  65.9 6.8 %collective-permute-start.18 = (bf16[6,4096]{1,0:T(8,128)(2,1)S(1)}, bf16[6,4096]{1,0:T(8,128)(2,1)S(1)}, u32[]{:S(2)}, u32[]{:S(2)}) collective-permute-start(bf16[6,4096]{1,0:T(8,128)(2,1)S(1)} %get-tuple-element.29), channel_id=1, source_target_pairs={{0,8},{4,12},{8,0},{12,4},{1,9},{5,13},{9,1},{13,5},{2,10},{6,14},... | collective-permute-start | bytes 147464 | tf_op jit(solution)/shard_map/ppermute | solution.py:32

commit v2 on v1

--- a/solution.py
+++ b/solution.py
@@ -8,8 +8,9 @@
 from jax.sharding import PartitionSpec as P
 
 LANES = 128
+held = pltpu.with_memory_space_constraint
 VMEM = pl.BlockSpec(memory_space=pltpu.VMEM)
-SMEM = pl.BlockSpec(memory_space=pltpu.SMEM)
+HBM = pl.BlockSpec(memory_space=pltpu.HBM)
 
 
 def params(mib):
@@ -48,11 +49,21 @@
     return jnp.where(part == 0, high, jnp.where(part == 1, middle, jnp.where(part == 2, low, 0.0)))
 
 
-def prepare_kernel(experts, x_prompt, x_resp, prompt_cot, resp_cot, route_p, route_r, weight_p, weight_r, sent_r, sent_p, *shares):
+def prepare_kernel(experts, *refs):
+    n_in = 8
+    sources, outs, scratch = refs[:n_in], refs[n_in : len(refs) - n_in - 1], refs[len(refs) - n_in - 1 : -1]
+    arrived = refs[-1]
+    copies = [pltpu.make_async_copy(a, b, arrived.at[i]) for i, (a, b) in enumerate(zip(sources, scratch, strict=True))]
+    for copy in copies:
+        copy.start()
+    for copy in copies:
+        copy.wait()
+    x_prompt, x_resp, prompt_cot, resp_cot, route_p, route_r, weight_p, weight_r = scratch
+    sent_r, sent_p = outs
     width = x_prompt.shape[-1]
     rows_p = x_prompt.shape[1]
     responses, length = x_resp.shape[1:3]
-    top = route_p.shape[-2]
+    top = route_p.shape[-1]
     x = [x_resp[0, i].astype(jnp.float32) for i in range(responses)]
     dy = [resp_cot[0, i].astype(jnp.float32) for i in range(responses)]
     sent_r[:, :width] = jnp.concatenate(x + dy, axis=0).astype(jnp.bfloat16)
@@ -63,27 +74,27 @@
     ]
     rows.append(jnp.zeros((len(rows), LANES), jnp.float32))
     sent_r[:, width:] = jnp.concatenate(rows, axis=0).astype(jnp.bfloat16)
-    sent_p[:, :width] = x_prompt[0]
-    rows = [
-        router_row(lambda t, k: route_p[0, k, t], lambda t, k: weight_p[0, k, t], t, top, experts)
-        for t in range(rows_p)
-    ]
-    sent_p[:, width:] = jnp.concatenate(rows, axis=0).astype(jnp.bfloat16)
     cot = prompt_cot[0, 0].astype(jnp.float32)
     for i in range(1, responses):
         cot = cot + prompt_cot[0, i].astype(jnp.float32)
-    rows = cot.shape[0]
+    prompts = cot.shape[0]
     here = lax.axis_index("resp") * rows_p
-    cot = pltpu.roll(cot, (rows - here) % rows, 0)
-    for k, share in enumerate(shares):
-        share[...] = cot[k * rows_p : (k + 1) * rows_p].astype(jnp.bfloat16)
+    own = jnp.concatenate([x_prompt[0].astype(jnp.float32), jnp.zeros((prompts - rows_p, width), jnp.float32)], axis=0)
+    sent_p[:, :width] = jnp.concatenate([pltpu.roll(own, here, 0), cot], axis=0).astype(jnp.bfloat16)
+    rows = [
+        router_row(lambda t, k: route_p[0, t, k], lambda t, k: weight_p[0, t, k], t, top, experts)
+        for t in range(rows_p)
+    ]
+    rows.append(jnp.zeros((prompts - rows_p, LANES), jnp.float32))
+    own = pltpu.roll(jnp.concatenate(rows, axis=0), here, 0)
+    sent_p[:, width:] = jnp.concatenate([own, jnp.zeros((prompts, LANES), jnp.float32)], axis=0).astype(jnp.bfloat16)
 
 
 def expert_kernel(count, spans, experts, *refs):
     width = refs[2 * count].shape[-1]
     blocks_r, blocks_p = refs[:count], refs[count : 2 * count]
-    gate_w, up_w, down_w, part, rows_out, gate_out, up_out, hidden_out = refs[2 * count :]
-    span_r, span_p = spans
+    gate_w, up_w, down_w, near, far, rows_out, gate_out, up_out, hidden_out = refs[2 * count :]
+    span_r, span_p, prompts = spans
     tails = []
     base = 0
     for block in (*blocks_r, *blocks_p):
@@ -104,7 +115,7 @@
 
     def moved(value, up):
         top, low = value[:split], value[split:]
-        by_r, by_p = (split - span_r, total - split - span_p) if up else (span_r, span_p)
+        by_r, by_p = (split - span_r, total - split - prompts) if up else (span_r, prompts)
         return jnp.concatenate([pltpu.roll(top, by_r, 0), pltpu.roll(low, by_p, 0)], axis=0)
 
     sigma = jax.nn.sigmoid(gate)
@@ -116,13 +127,16 @@
     gate_out[...] = gate_grad
     up_out[...] = upward_grad
     hidden_out[...] = moved(hidden, False).astype(jnp.bfloat16)
-    tokens = part.shape[0]
+    half = near.shape[0]
+    tokens = 2 * half
     each = span_r + span_p
     slot = lax.broadcasted_iota(jnp.int32, (tokens, total), 0)
     row = lax.broadcasted_iota(jnp.int32, (tokens, total), 1)
     source, token = slot // each, slot % each
     from_r = source * (2 * span_r) + token
-    from_p = split + source * (2 * span_p) + token - span_r
+    n_resp = prompts // span_p
+    giver = (lax.axis_index("resp") + n_resp - source % n_resp) % n_resp
+    from_p = split + source // n_resp * (2 * prompts) + giver * span_p + token - span_r
     chosen = (row == jnp.where(token < span_r, from_r, from_p)).astype(jnp.float32).astype(jnp.bfloat16)
     gate_grad = jnp.dot(chosen, gate_grad, preferred_element_type=jnp.float32).astype(jnp.bfloat16)
     upward_grad = jnp.dot(chosen, upward_grad, preferred_element_type=jnp.float32).astype(jnp.bfloat16)
@@ -130,7 +144,65 @@
     for c in range(0, width, step):
         value = jnp.dot(gate_grad, gate_w[0, :, c : c + step], preferred_element_type=jnp.float32)
         value = value + jnp.dot(upward_grad, up_w[0, :, c : c + step], preferred_element_type=jnp.float32)
-        part[:, c : c + step] = value.astype(jnp.bfloat16)
+        near[:, c : c + step] = value[:half].astype(jnp.bfloat16)
+        far[:, c : c + step] = value[half:].astype(jnp.bfloat16)
+
+
+def load_kernel(*refs):
+    count = (len(refs) - 1) // 2
+    arrived = refs[-1]
+    copies = [pltpu.make_async_copy(refs[i], refs[count + i], arrived.at[i]) for i in range(count)]
+    for copy in copies:
+        copy.start()
+    for copy in copies:
+        copy.wait()
+
+
+def outer_kernel(left, values, out, turned, buffer, sent):
+    turned[...] = left[...].astype(jnp.float32).T.astype(jnp.bfloat16)
+    steps = sent.shape[0]
+    step = values.shape[1] // steps
+    copies = []
+    for c in range(steps):
+        block = jnp.dot(turned[...], values[:, c * step : (c + 1) * step], preferred_element_type=jnp.float32)
+        buffer[c] = block.astype(jnp.bfloat16)
+        copies.append(pltpu.make_async_copy(buffer.at[c], out.at[0, :, pl.ds(c * step, step)], sent.at[c]))
+        copies[-1].start()
+    for copy in copies:
+        copy.wait()
+
+
+def outer(left, values, small):
+    rows, units = left.shape
+    width = values.shape[1]
+    steps = 4 if width % 512 == 0 else 1
+    given = [held(a, pltpu.VMEM) for a in (left, values)] if small else [left, values]
+    return pl.pallas_call(
+        outer_kernel,
+        out_shape=(pltpu.HBM if small else jax.ShapeDtypeStruct)((1, units, width), jnp.bfloat16),
+        in_specs=[VMEM] * 2,
+        out_specs=HBM,
+        scratch_shapes=[
+            pltpu.VMEM((units, rows), jnp.bfloat16),
+            pltpu.VMEM((steps, units, width // steps), jnp.bfloat16),
+            pltpu.SemaphoreType.DMA((steps,)),
+        ],
+        compiler_params=params(24 if small else 60),
+        cost_estimate=pl.CostEstimate(flops=2 * rows * units * width, bytes_accessed=2 * units * width, transcendentals=0),
+        name="outer",
+    )(*given)
+
+
+def finish_kernel(rows_r, *refs):
+    parts, prompt_out, resp_out = refs[:-2], refs[-2], refs[-1]
+    total = parts[0][...].astype(jnp.float32)
+    for part in parts[1:]:
+        total = total + part[...].astype(jnp.float32)
+    total = total.astype(jnp.bfloat16)
+    responses, length = resp_out.shape[1:3]
+    for i in range(responses):
+        resp_out[0, i] = total[i * length : (i + 1) * length]
+    prompt_out[0] = total[rows_r:]
 
 
 def body(
@@ -156,75 +228,98 @@
     rows_r = x_resp.shape[1] * x_resp.shape[2]
     bf16 = jnp.bfloat16
 
-    sent_r, half_p, *shares = pl.pallas_call(
+    given = [held(a, pltpu.HBM) for a in (x_prompt, x_resp, prompt_cot, resp_cot)]
+    routing = [route_prompt, jnp.swapaxes(route_resp, -1, -2), weight_prompt, jnp.swapaxes(weight_resp, -1, -2)]
+    routing = [held(a, pltpu.HBM) for a in routing]
+    prompts = prompt_cot.shape[2]
+    sent_r, sent_p = pl.pallas_call(
         functools.partial(prepare_kernel, experts),
         out_shape=[
             jax.ShapeDtypeStruct((2 * rows_r, width + LANES), bf16),
-            jax.ShapeDtypeStruct((rows_p, width + LANES), bf16),
-        ]
-        + [jax.ShapeDtypeStruct((rows_p, width), bf16)] * n_resp,
-        in_specs=[VMEM] * 4 + [SMEM] * 4,
-        out_specs=[VMEM] * (2 + n_resp),
-        compiler_params=params(16),
+            jax.ShapeDtypeStruct((2 * prompts, width + LANES), bf16),
+        ],
+        in_specs=[HBM] * 8,
+        out_specs=[VMEM] * 2,
+        scratch_shapes=[pltpu.VMEM(a.shape, a.dtype) for a in given]
+        + [pltpu.SMEM(a.shape, a.dtype) for a in routing]
+        + [pltpu.SemaphoreType.DMA((8,))],
+        compiler_params=params(8),
         name="prepare",
-    )(
-        x_prompt,
-        x_resp,
-        prompt_cot,
-        resp_cot,
-        jnp.swapaxes(route_prompt, -1, -2),
-        jnp.swapaxes(route_resp, -1, -2),
-        jnp.swapaxes(weight_prompt, -1, -2),
-        jnp.swapaxes(weight_resp, -1, -2),
-    )
-
-    def gather(message):
-        line = jnp.concatenate([message] + [along("resp", n_resp, k)(message) for k in range(1, n_resp)], axis=0)
+    )(*given, *routing)
+
+    def spread(line):
         near = [line] + [along("expert", n_expert, 2 * j)(line) for j in range(1, chips)]
         return near + [other_core(block, n_expert) for block in near]
 
-    all_r = gather(sent_r)
-    dy_prompt = shares[0].astype(jnp.float32)
-    for k in range(1, n_resp):
-        dy_prompt = dy_prompt + along("resp", n_resp, k)(shares[k]).astype(jnp.float32)
-    dy_prompt = jnp.pad(dy_prompt.astype(bf16), ((0, 0), (0, LANES)))
-    all_p = gather(jnp.concatenate([half_p, dy_prompt], axis=0))
+    weights = [w_gate, w_up, w_down]
+    small = n_resp * n_expert <= 32
+    if small:
+        weights = pl.pallas_call(
+            load_kernel,
+            out_shape=[pltpu.VMEM(w.shape, w.dtype) for w in weights],
+            in_specs=[HBM] * 3,
+            out_specs=[VMEM] * 3,
+            scratch_shapes=[pltpu.SemaphoreType.DMA((3,))],
+            compiler_params=params(8),
+            cost_estimate=pl.CostEstimate(flops=0, bytes_accessed=6 * w_gate.size, transcendentals=0),
+            name="load",
+        )(*[held(w, pltpu.HBM) for w in weights])
+    by = 1
+    while by < n_resp:
+        if by == 2:
+            sent_p, *weights = lax.optimization_barrier((sent_p, *weights))
+        got = lax.ppermute(sent_p, "resp", [(i, i ^ by) for i in range(n_resp)])
+        sent_p = (sent_p.astype(jnp.float32) + got.astype(jnp.float32)).astype(bf16)
+        by *= 2
+    line_r = jnp.concatenate([sent_r] + [along("resp", n_resp, k)(sent_r) for k in range(1, n_resp)], axis=0)
+    all_r = spread(line_r)
+    all_p = spread(sent_p)
 
     count = len(all_r)
     rows = sum(b.shape[0] for b in (*all_r, *all_p))
     tokens = rows // 2
-    part, values, gate_grad, upward_grad, hidden = pl.pallas_call(
-        functools.partial(expert_kernel, count, (rows_r, rows_p), experts),
+    half = tokens // 2
+    kept = pltpu.VMEM if small else jax.ShapeDtypeStruct
+    taken = [*all_r, *all_p, *weights]
+    if small:
+        taken = [held(a, pltpu.VMEM) for a in taken]
+    near, far, values, gate_grad, upward_grad, hidden = pl.pallas_call(
+        functools.partial(expert_kernel, count, (rows_r, rows_p, prompts), experts),
         out_shape=[
-            jax.ShapeDtypeStruct((tokens, width), bf16),
-            jax.ShapeDtypeStruct((rows, width), bf16),
+            kept((half, width), bf16),
+            kept((half, width), bf16),
+            kept((rows, width), bf16),
         ]
-        + [jax.ShapeDtypeStruct((rows, hidden_units), bf16)] * 3,
+        + [kept((rows, hidden_units), bf16)] * 3,
         in_specs=[VMEM] * (2 * count + 3),
-        out_specs=[VMEM] * 5,
-        compiler_params=params(60),
+        out_specs=[VMEM] * 6,
+        compiler_params=params(24 if small else 60),
         cost_estimate=pl.CostEstimate(flops=10 * rows * width * hidden_units, bytes_accessed=20 * 2**20, transcendentals=0),
         name="expert",
-    )(*all_r, *all_p, w_gate, w_up, w_down)
-
-    half = tokens // 2
-    total = part[:half].astype(jnp.float32) + other_core(part[half:], n_expert).astype(jnp.float32)
+    )(*taken)
+
+    total = near.astype(jnp.float32) + other_core(far, n_expert).astype(jnp.float32)
     total = total.astype(bf16)
+    total, values, gate_grad, upward_grad, hidden = lax.optimization_barrier((total, values, gate_grad, upward_grad, hidden))
     block = half // chips
     line = total[:block].astype(jnp.float32)
     for j in range(1, chips):
         line = line + along("expert", n_expert, -2 * j)(total[j * block : (j + 1) * block]).astype(jnp.float32)
     line = line.astype(bf16)
     each = rows_r + rows_p
-    own = line[:each].astype(jnp.float32)
-    for k in range(1, n_resp):
-        own = own + along("resp", n_resp, -k)(line[k * each : (k + 1) * each]).astype(jnp.float32)
-    own = own.astype(bf16)
-
-    grad_gate = contract_first(gate_grad, values).astype(bf16)[None]
-    grad_up = contract_first(upward_grad, values).astype(bf16)[None]
-    grad_down = contract_first(hidden, values).astype(bf16)[None]
-    return (own[rows_r:][None], own[:rows_r].reshape(x_resp.shape), grad_gate, grad_up, grad_down)
+    own = [line[:each]] + [along("resp", n_resp, -k)(line[k * each : (k + 1) * each]) for k in range(1, n_resp)]
+    grad_prompt, grad_resp = pl.pallas_call(
+        functools.partial(finish_kernel, rows_r),
+        out_shape=[jax.ShapeDtypeStruct(x_prompt.shape, bf16), jax.ShapeDtypeStruct(x_resp.shape, bf16)],
+        in_specs=[VMEM] * n_resp,
+        out_specs=[VMEM] * 2,
+        compiler_params=params(8),
+        name="finish",
+    )(*own)
+    grad_gate = outer(gate_grad, values, small)
+    grad_up = outer(upward_grad, values, small)
+    grad_down = outer(hidden, values, small)
+    return (grad_prompt, grad_resp, grad_gate, grad_up, grad_down)
 
 
 def solution(mesh):

time: 74.4 us -> 53.5 us (0.72)
  local copies, waits for them, and re-layouts: 10 us -> 0.11 us
  matrix products: 9.63 us -> 0 us
  waiting for transfers between devices: 23.9 us -> 16.9 us
  Pallas kernels: 10.4 us -> 16.6 us
    ppermute x15 -> x9, waiting for transfers between devices: 22.6 us -> 5.68 us  [along(): lax.ppermute(value, axis, [(i, (i + by) % size) for i in range(size)])]
    dot_general x3 -> x0, matrix products: 9.63 us -> none  [contract_first(): lax.dot_general(left, right, (((0,), (0,)), ((), ())), preferred_element_...]
    ppermute x0 -> x2, waiting for transfers between devices: none -> 8.31 us  [body(): got = lax.ppermute(sent_p, 'resp', [(i, i ^ by) for i in range(n_resp)])]
    unnamed x41 -> x3, local copies, waits for them, and re-layouts: 7.43 us -> 0.03 us
    pallas_call x1 -> x6, Pallas kernels: 9.78 us -> 15.5 us  [the longest x3 6.41 us: outer(): pl.pallas_call(outer_kernel, out_shape=(pltpu.HBM if small else jax.Shape...]
    ppermute x15 -> x9, starting transfers between devices: 18.1 us -> 15.3 us  [along(): lax.ppermute(value, axis, [(i, (i + by) % size) for i in range(size)])]
    ppermute x0 -> x2, starting transfers between devices: none -> 2.55 us  [body(): got = lax.ppermute(sent_p, 'resp', [(i, i ^ by) for i in range(n_resp)])]
    ppermute x5, waiting for transfers between devices: 1.35 us -> 2.92 us  [other_core(): return lax.ppermute(value, 'expert', [(i, i ^ 1) for i in range(size)])]
  transfers between devices with their start and end apart: 20 -> 16, of which waited for: 11 -> 7; matrix products, arithmetic and copies ran while one was open for 13% -> 0% of each run, Pallas kernels for 0% -> 19%
where the time goes in v2:
time: 53.5 us; the launch traced here: 53.3 us
  starting transfers between devices  18.7 us (35%)
  waiting for transfers between devices  16.9 us (32%)
  Pallas kernels  16.6 us (31%)
  between operations  0.78 us (1%)
    ppermute x9, starting transfers between devices, along(): lax.ppermute(value, axis, [(i, (i + by) % size) for i in range(size)])  15.3 us
    ppermute x2, waiting for transfers between devices, body(): got = lax.ppermute(sent_p, 'resp', [(i, i ^ by) for i in range(n_resp)])  8.31 us
    pallas_call x3, Pallas kernels, outer(): pl.pallas_call(outer_kernel, out_shape=(pltpu.HBM if small else jax.Shape...  6.41 us
    ppermute x9, waiting for transfers between devices, along(): lax.ppermute(value, axis, [(i, (i + by) % size) for i in range(size)])  5.68 us
    pallas_call x1, Pallas kernels, body(): pl.pallas_call(functools.partial(expert_kernel, count, (rows_r, rows_p, p...  4.7 us
    pallas_call x1, Pallas kernels, body(): pl.pallas_call(load_kernel, out_shape=[pltpu.VMEM(w.shape, w.dtype) for w...  3.78 us
    ppermute x5, waiting for transfers between devices, other_core(): return lax.ppermute(value, 'expert', [(i, i ^ 1) for i in range(size)])  2.92 us
    ppermute x2, starting transfers between devices, body(): got = lax.ppermute(sent_p, 'resp', [(i, i ^ by) for i in range(n_resp)])  2.55 us
  transfers between devices with their start and end apart: 16, of which 7 were waited for; matrix products, arithmetic and copies ran while one was open for 0% of the time, Pallas kernels for 19%

profile of v2, /device:TPU:0, one launch (start us, length us, event | category | flops | bytes accessed | tf_op | source)
XLA Modules:
  0.0 53.3 jit_solution(10285926115062453707)
XLA Ops:
  0.6 1.0 %prepare.1 = (bf16[8,4224]{1,0:T(8,128)(2,1)S(1)}, bf16[16,4224]{1,0:T(8,128)(2,1)S(1)}) custom-call(bf16[1,2,4096]{2,1,0:T(2,128)(2,1)} %refs_0_.2, bf16[1,1,4,4096]{3,2,1,0:T(4,128)(2,1)} %refs_1_.2, bf16[1,1,8,4096]{3,2,1,0:T(8,128)(2,1)} %refs_2_.2, bf16[1,1,4,4096]{3,2,1,0:T(4,128)(2,1)} %refs_3_.1, s32[1,2,2]{2,1,0:T(2,128)} %refs_4_.1, ...), custom_call_target="tpu_custom_call" | custom-call | tf_op jit(solution)/shard_map/prepare/pallas_call | solution.py:235
  1.7 5.1 %collective-permute-start.2 = (bf16[8,4224]{1,0:T(8,128)(2,1)S(1)}, bf16[8,4224]{1,0:T(8,128)(2,1)S(1)}, u32[]{:S(2)}, u32[]{:S(2)}) collective-permute-start(bf16[8,4224]{1,0:T(8,128)(2,1)S(1)} %get-tuple-element.27), channel_id=1, source_target_pairs={{0,12},{4,0},{8,4},{12,8},{1,13},{5,1},{9,5},{13,9},{2,14},{6,2},{... | collective-permute-start | bytes 202760 | tf_op jit(solution)/shard_map/ppermute | solution.py:33
  6.8 0.0 collective-permute-start.1
  6.8 1.0 %collective-permute-start = (bf16[8,4224]{1,0:T(8,128)(2,1)S(1)}, bf16[8,4224]{1,0:T(8,128)(2,1)S(1)}, u32[]{:S(2)}, u32[]{:S(2)}) collective-permute-start(bf16[8,4224]{1,0:T(8,128)(2,1)S(1)} %get-tuple-element.27), channel_id=1, source_target_pairs={{0,4},{4,8},{8,12},{12,0},{1,5},{5,9},{9,13},{13,1},{2,6},{6,10},{... | collective-permute-start | bytes 202760 | tf_op jit(solution)/shard_map/ppermute | solution.py:33
  7.8 2.5 %collective-permute-start.6 = (bf16[16,4224]{1,0:T(8,128)(2,1)S(1)}, bf16[16,4224]{1,0:T(8,128)(2,1)S(1)}, u32[]{:S(2)}, u32[]{:S(2)}) collective-permute-start(bf16[16,4224]{1,0:T(8,128)(2,1)S(1)} %get-tuple-element.28), channel_id=1, source_target_pairs={{0,4},{4,0},{8,12},{12,8},{1,5},{5,1},{9,13},{13,9},{2,6},{6,2},{1... | collective-permute-start | bytes 405512 | tf_op jit(solution)/shard_map/ppermute | solution.py:271
  10.3 3.8 %load.1 = (bf16[1,384,4096]{2,1,0:T(8,128)(2,1)S(1)}, bf16[1,384,4096]{2,1,0:T(8,128)(2,1)S(1)}, bf16[1,384,4096]{2,1,0:T(8,128)(2,1)S(1)}) custom-call(bf16[1,384,4096]{2,1,0:T(8,128)(2,1)} %refs_0_.3, bf16[1,384,4096]{2,1,0:T(8,128)(2,1)} %refs_1_.3, bf16[1,384,4096]{2,1,0:T(8,128)(2,1)} %refs_2_.3), custom_call_target="tpu_custom_call" | custom-call | bytes 9437184 | tf_op jit(solution)/shard_map/load/pallas_call | solution.py:257
  14.1 0.0 collective-permute-done
  14.1 0.0 collective-permute-done.1
  14.1 1.8 %collective-permute-done.6 = bf16[16,4224]{1,0:T(8,128)(2,1)S(1)} collective-permute-done((bf16[16,4224]{1,0:T(8,128)(2,1)S(1)}, bf16[16,4224]{1,0:T(8,128)(2,1)S(1)}, u32[]{:S(2)}, u32[]{:S(2)}) %collective-permute-start.6) | collective-permute-done | bytes 135200 | tf_op jit(solution)/shard_map/ppermute | solution.py:271
  16.0 0.1 collective-permute-start.7
  16.0 0.0 collective-permute-done.2
  16.1 0.1 collective-permute-start.4
  16.1 1.6 %collective-permute-start.3 = (bf16[32,4224]{1,0:T(8,128)(2,1)S(1)}, bf16[32,4224]{1,0:T(8,128)(2,1)S(1)}, u32[]{:S(2)}, u32[]{:S(2)}) collective-permute-start(bf16[32,4224]{1,0:T(8,128)(2,1)S(1)} %constant_dynamic-update-slice_fusion.refs_0_), channel_id=1, source_target_pairs={{0,2},{1,3},{2,0},{3,1},{4,6},{5,7},{6,4},{7,5},{8,10},{9,11},{10,... | collective-permute-start | bytes 811016 | tf_op jit(solution)/shard_map/ppermute | solution.py:33
  17.7 6.5 %collective-permute-done.7 = bf16[16,4224]{1,0:T(8,128)(2,1)S(1)} collective-permute-done((bf16[16,4224]{1,0:T(8,128)(2,1)S(1)}, bf16[16,4224]{1,0:T(8,128)(2,1)S(1)}, u32[]{:S(2)}, u32[]{:S(2)}) %collective-permute-start.7) | collective-permute-done | bytes 135200 | tf_op jit(solution)/shard_map/ppermute | solution.py:271
  24.3 1.6 %collective-permute-start.8 = (bf16[16,4224]{1,0:T(8,128)(2,1)S(1)}, bf16[16,4224]{1,0:T(8,128)(2,1)S(1)}, u32[]{:S(2)}, u32[]{:S(2)}) collective-permute-start(bf16[16,4224]{1,0:T(8,128)(2,1)S(1)} %add_convert_fusion.2.refs_4_), channel_id=1, source_target_pairs={{0,2},{1,3},{2,0},{3,1},{4,6},{5,7},{6,4},{7,5},{8,10},{9,11},{10,... | collective-permute-start | bytes 405512 | tf_op jit(solution)/shard_map/ppermute | solution.py:33
  25.9 0.0 collective-permute-done.3.refs_1_
  25.9 0.0 collective-permute-start.5
  25.9 0.5 collective-permute-start.9
  26.4 3.0 %collective-permute-done.8.refs_5_ = bf16[16,4224]{1,0:T(8,128)(2,1)S(1)} collective-permute-done((bf16[16,4224]{1,0:T(8,128)(2,1)S(1)}, bf16[16,4224]{1,0:T(8,128)(2,1)S(1)}, u32[]{:S(2)}, u32[]{:S(2)}) %collective-permute-start.8) | collective-permute-done | bytes 135200 | tf_op jit(solution)/shard_map/ppermute | solution.py:33
  29.4 0.0 collective-permute-start.10
  29.4 0.0 collective-permute-done.4.refs_2_
  29.4 0.0 collective-permute-done.9.refs_6_
  29.4 1.3 %collective-permute-done.10.refs_7_ = bf16[16,4224]{1,0:T(8,128)(2,1)S(1)} collective-permute-done((bf16[16,4224]{1,0:T(8,128)(2,1)S(1)}, bf16[16,4224]{1,0:T(8,128)(2,1)S(1)}, u32[]{:S(2)}, u32[]{:S(2)}) %collective-permute-start.10) | collective-permute-done | bytes 135200 | tf_op jit(solution)/shard_map/ppermute | solution.py:37
  30.7 0.0 collective-permute-done.5.refs_3_
  30.7 4.7 %expert.1 = (bf16[48,4096]{1,0:T(8,128)(2,1)S(1)}, bf16[48,4096]{1,0:T(8,128)(2,1)S(1)}, bf16[192,4096]{1,0:T(8,128)(2,1)S(1)}, bf16[192,384]{1,0:T(8,128)(2,1)S...) custom-call(bf16[32,4224]{1,0:T(8,128)(2,1)S(1)} %constant_dynamic-update-slice_fusion.refs_0_, ...), custom_call_target="tpu_custom_call" | custom-call | flops 3019898880 | bytes 20971520 | tf_op jit(solution)/shard_map/expert/pallas_call | solution.py:286
  35.4 0.2 collective-permute-start.11
  35.6 1.6 %collective-permute-done.11 = bf16[48,4096]{1,0:T(8,128)(2,1)S(1)} collective-permute-done((bf16[48,4096]{1,0:T(8,128)(2,1)S(1)}, bf16[48,4096]{1,0:T(8,128)(2,1)S(1)}, u32[]{:S(2)}, u32[]{:S(2)}) %collective-permute-start.11) | collective-permute-done | bytes 393248 | tf_op jit(solution)/shard_map/ppermute | solution.py:37
  37.2 0.1 add_convert_fusion
  37.3 1.6 %collective-permute-start.12 = (bf16[24,4096]{1,0:T(8,128)(2,1)S(1)}, bf16[24,4096]{1,0:T(8,128)(2,1)S(1)}, u32[]{:S(2)}, u32[]{:S(2)}) collective-permute-start(bf16[24,4096]{1,0:T(8,128)(2,1)S(1)} %slice.19), channel_id=1, source_target_pairs={{0,2},{1,3},{2,0},{3,1},{4,6},{5,7},{6,4},{7,5},{8,10},{9,11},{10,... | collective-permute-start | bytes 589832 | tf_op jit(solution)/shard_map/ppermute | solution.py:33
  38.9 2.1 %outer.3 = bf16[1,384,4096]{2,1,0:T(8,128)(2,1)} custom-call(bf16[192,384]{1,0:T(8,128)(2,1)S(1)} %get-tuple-element.45.left, bf16[192,4096]{1,0:T(8,128)(2,1)S(1)} %get-tuple-element.46.values), custom_call_target="tpu_custom_call" | custom-call | flops 603979776 | bytes 3145728 | tf_op jit(solution)/shard_map/outer/pallas_call | solution.py:180
  41.1 2.1 %outer.4 = bf16[1,384,4096]{2,1,0:T(8,128)(2,1)} custom-call(bf16[192,384]{1,0:T(8,128)(2,1)S(1)} %get-tuple-element.47.left, bf16[192,4096]{1,0:T(8,128)(2,1)S(1)} %get-tuple-element.46.values), custom_call_target="tpu_custom_call" | custom-call | flops 603979776 | bytes 3145728 | tf_op jit(solution)/shard_map/outer/pallas_call | solution.py:180
  43.2 1.1 %collective-permute-done.12 = bf16[24,4096]{1,0:T(8,128)(2,1)S(1)} collective-permute-done((bf16[24,4096]{1,0:T(8,128)(2,1)S(1)}, bf16[24,4096]{1,0:T(8,128)(2,1)S(1)}, u32[]{:S(2)}, u32[]{:S(2)}) %collective-permute-start.12) | collective-permute-done | bytes 196640 | tf_op jit(solution)/shard_map/ppermute | solution.py:33
  44.4 0.1 fusion
  44.5 0.8 %collective-permute-start.15 = (bf16[6,4096]{1,0:T(8,128)(2,1)S(1)}, bf16[6,4096]{1,0:T(8,128)(2,1)S(1)}, u32[]{:S(2)}, u32[]{:S(2)}) collective-permute-start(bf16[6,4096]{1,0:T(8,128)(2,1)S(1)} %get-tuple-element.49), channel_id=1, source_target_pairs={{0,4},{4,8},{8,12},{12,0},{1,5},{5,9},{9,13},{13,1},{2,6},{6,10},{... | collective-permute-start | bytes 147464 | tf_op jit(solution)/shard_map/ppermute | solution.py:33
  45.3 2.1 %collective-permute-start.14 = (bf16[6,4096]{1,0:T(8,128)(2,1)S(1)}, bf16[6,4096]{1,0:T(8,128)(2,1)S(1)}, u32[]{:S(2)}, u32[]{:S(2)}) collective-permute-start(bf16[6,4096]{1,0:T(8,128)(2,1)S(1)} %get-tuple-element.50), channel_id=1, source_target_pairs={{0,8},{4,12},{8,0},{12,4},{1,9},{5,13},{9,1},{13,5},{2,10},{6,14},... | collective-permute-start | bytes 147464 | tf_op jit(solution)/shard_map/ppermute | solution.py:33
  47.4 1.6 %collective-permute-start.13 = (bf16[6,4096]{1,0:T(8,128)(2,1)S(1)}, bf16[6,4096]{1,0:T(8,128)(2,1)S(1)}, u32[]{:S(2)}, u32[]{:S(2)}) collective-permute-start(bf16[6,4096]{1,0:T(8,128)(2,1)S(1)} %get-tuple-element.51), channel_id=1, source_target_pairs={{0,12},{4,0},{8,4},{12,8},{1,13},{5,1},{9,5},{13,9},{2,14},{6,2},{... | collective-permute-start | bytes 147464 | tf_op jit(solution)/shard_map/ppermute | solution.py:33
  48.9 2.1 %outer.5 = bf16[1,384,4096]{2,1,0:T(8,128)(2,1)} custom-call(bf16[192,384]{1,0:T(8,128)(2,1)S(1)} %get-tuple-element.48.left, bf16[192,4096]{1,0:T(8,128)(2,1)S(1)} %get-tuple-element.46.values), custom_call_target="tpu_custom_call" | custom-call | flops 603979776 | bytes 3145728 | tf_op jit(solution)/shard_map/outer/pallas_call | solution.py:180
  51.1 0.0 collective-permute-done.15.refs_3_
  51.1 1.5 %collective-permute-done.14.refs_2_ = bf16[6,4096]{1,0:T(8,128)(2,1)S(1)} collective-permute-done((bf16[6,4096]{1,0:T(8,128)(2,1)S(1)}, bf16[6,4096]{1,0:T(8,128)(2,1)S(1)}, u32[]{:S(2)}, u32[]{:S(2)}) %collective-permute-start.14) | collective-permute-done | bytes 49184 | tf_op jit(solution)/shard_map/ppermute | solution.py:33
  52.6 0.0 collective-permute-done.13.refs_1_
  52.6 0.7 %finish.1 = (bf16[1,2,4096]{2,1,0:T(2,128)(2,1)}, bf16[1,1,4,4096]{3,2,1,0:T(4,128)(2,1)}) custom-call(bf16[6,4096]{1,0:T(8,128)(2,1)S(1)} %get-tuple-element.52.refs_0_, bf16[6,4096]{1,0:T(8,128)(2,1)S(1)} %collective-permute-done.13.refs_1_, bf16[6,4096]{1,0:T(8,128)(2,1)S(1)} %collective-permute-done.14.refs_2_, ...), custom_call_target="tpu_custom_call" | custom-call | tf_op jit(solution)/shard_map/finish/pallas_call | solution.py:311
  (8 shorter events, 0.2 us)
Async XLA Ops:
  1.7 14.3 %collective-permute-start.2 = (bf16[8,4224]{1,0:T(8,128)(2,1)S(1)}, bf16[8,4224]{1,0:T(8,128)(2,1)S(1)}, u32[]{:S(2)}, u32[]{:S(2)}) collective-permute-start(bf16[8,4224]{1,0:T(8,128)(2,1)S(1)} %get-tuple-element.27), channel_id=1, source_target_pairs={{0,12},{4,0},{8,4},{12,8},{1,13},{5,1},{9,5},{13,9},{2,14},{6,2},{... | collective-permute-start | bytes 202760 | tf_op jit(solution)/shard_map/ppermute | solution.py:33
  6.8 7.3 %collective-permute-start.1 = (bf16[8,4224]{1,0:T(8,128)(2,1)S(1)}, bf16[8,4224]{1,0:T(8,128)(2,1)S(1)}, u32[]{:S(2)}, u32[]{:S(2)}) collective-permute-start(bf16[8,4224]{1,0:T(8,128)(2,1)S(1)} %get-tuple-element.27), channel_id=1, source_target_pairs={{0,8},{4,12},{8,0},{12,4},{1,9},{5,13},{9,1},{13,5},{2,10},{6,14},... | collective-permute-start | bytes 202760 | tf_op jit(solution)/shard_map/ppermute | solution.py:33
  6.8 7.3 %collective-permute-start = (bf16[8,4224]{1,0:T(8,128)(2,1)S(1)}, bf16[8,4224]{1,0:T(8,128)(2,1)S(1)}, u32[]{:S(2)}, u32[]{:S(2)}) collective-permute-start(bf16[8,4224]{1,0:T(8,128)(2,1)S(1)} %get-tuple-element.27), channel_id=1, source_target_pairs={{0,4},{4,8},{8,12},{12,0},{1,5},{5,9},{9,13},{13,1},{2,6},{6,10},{... | collective-permute-start | bytes 202760 | tf_op jit(solution)/shard_map/ppermute | solution.py:33
  7.8 8.1 %collective-permute-start.6 = (bf16[16,4224]{1,0:T(8,128)(2,1)S(1)}, bf16[16,4224]{1,0:T(8,128)(2,1)S(1)}, u32[]{:S(2)}, u32[]{:S(2)}) collective-permute-start(bf16[16,4224]{1,0:T(8,128)(2,1)S(1)} %get-tuple-element.28), channel_id=1, source_target_pairs={{0,4},{4,0},{8,12},{12,8},{1,5},{5,1},{9,13},{13,9},{2,6},{6,2},{1... | collective-permute-start | bytes 405512 | tf_op jit(solution)/shard_map/ppermute | solution.py:271
  16.0 8.3 %collective-permute-start.7 = (bf16[16,4224]{1,0:T(8,128)(2,1)S(1)}, bf16[16,4224]{1,0:T(8,128)(2,1)S(1)}, u32[]{:S(2)}, u32[]{:S(2)}) collective-permute-start(bf16[16,4224]{1,0:T(8,128)(2,1)S(1)} %add_convert_fusion.3), channel_id=1, source_target_pairs={{0,8},{4,12},{8,0},{12,4},{1,9},{5,13},{9,1},{13,5},{2,10},{6,14},... | collective-permute-start | bytes 405512 | tf_op jit(solution)/shard_map/ppermute | solution.py:271
  16.1 13.3 %collective-permute-start.4 = (bf16[32,4224]{1,0:T(8,128)(2,1)S(1)}, bf16[32,4224]{1,0:T(8,128)(2,1)S(1)}, u32[]{:S(2)}, u32[]{:S(2)}) collective-permute-start(bf16[32,4224]{1,0:T(8,128)(2,1)S(1)} %constant_dynamic-update-slice_fusion.refs_0_), channel_id=1, source_target_pairs={{0,1},{1,0},{2,3},{3,2},{4,5},{5,4},{6,7},{7,6},{8,9},{9,8},{10,11... | collective-permute-start | bytes 811016 | tf_op jit(solution)/shard_map/ppermute | solution.py:37
  16.1 9.7 %collective-permute-start.3 = (bf16[32,4224]{1,0:T(8,128)(2,1)S(1)}, bf16[32,4224]{1,0:T(8,128)(2,1)S(1)}, u32[]{:S(2)}, u32[]{:S(2)}) collective-permute-start(bf16[32,4224]{1,0:T(8,128)(2,1)S(1)} %constant_dynamic-update-slice_fusion.refs_0_), channel_id=1, source_target_pairs={{0,2},{1,3},{2,0},{3,1},{4,6},{5,7},{6,4},{7,5},{8,10},{9,11},{10,... | collective-permute-start | bytes 811016 | tf_op jit(solution)/shard_map/ppermute | solution.py:33
  24.3 5.1 %collective-permute-start.8 = (bf16[16,4224]{1,0:T(8,128)(2,1)S(1)}, bf16[16,4224]{1,0:T(8,128)(2,1)S(1)}, u32[]{:S(2)}, u32[]{:S(2)}) collective-permute-start(bf16[16,4224]{1,0:T(8,128)(2,1)S(1)} %add_convert_fusion.2.refs_4_), channel_id=1, source_target_pairs={{0,2},{1,3},{2,0},{3,1},{4,6},{5,7},{6,4},{7,5},{8,10},{9,11},{10,... | collective-permute-start | bytes 405512 | tf_op jit(solution)/shard_map/ppermute | solution.py:33
  25.9 4.8 %collective-permute-start.5 = (bf16[32,4224]{1,0:T(8,128)(2,1)S(1)}, bf16[32,4224]{1,0:T(8,128)(2,1)S(1)}, u32[]{:S(2)}, u32[]{:S(2)}) collective-permute-start(bf16[32,4224]{1,0:T(8,128)(2,1)S(1)} %collective-permute-done.3.refs_1_), channel_id=1, source_target_pairs={{0,1},{1,0},{2,3},{3,2},{4,5},{5,4},{6,7},{7,6},{8,9},{9,8},{10,11... | collective-permute-start | bytes 811016 | tf_op jit(solution)/shard_map/ppermute | solution.py:37
  25.9 3.5 %collective-permute-start.9 = (bf16[16,4224]{1,0:T(8,128)(2,1)S(1)}, bf16[16,4224]{1,0:T(8,128)(2,1)S(1)}, u32[]{:S(2)}, u32[]{:S(2)}) collective-permute-start(bf16[16,4224]{1,0:T(8,128)(2,1)S(1)} %add_convert_fusion.2.refs_4_), channel_id=1, source_target_pairs={{0,1},{1,0},{2,3},{3,2},{4,5},{5,4},{6,7},{7,6},{8,9},{9,8},{10,11... | collective-permute-start | bytes 405512 | tf_op jit(solution)/shard_map/ppermute | solution.py:37
  29.4 1.4 %collective-permute-start.10 = (bf16[16,4224]{1,0:T(8,128)(2,1)S(1)}, bf16[16,4224]{1,0:T(8,128)(2,1)S(1)}, u32[]{:S(2)}, u32[]{:S(2)}) collective-permute-start(bf16[16,4224]{1,0:T(8,128)(2,1)S(1)} %collective-permute-done.8.refs_5_), channel_id=1, source_target_pairs={{0,1},{1,0},{2,3},{3,2},{4,5},{5,4},{6,7},{7,6},{8,9},{9,8},{10,11... | collective-permute-start | bytes 405512 | tf_op jit(solution)/shard_map/ppermute | solution.py:37
  35.4 1.8 %collective-permute-start.11 = (bf16[48,4096]{1,0:T(8,128)(2,1)S(1)}, bf16[48,4096]{1,0:T(8,128)(2,1)S(1)}, u32[]{:S(2)}, u32[]{:S(2)}) collective-permute-start(bf16[48,4096]{1,0:T(8,128)(2,1)S(1)} %get-tuple-element.37), channel_id=1, source_target_pairs={{0,1},{1,0},{2,3},{3,2},{4,5},{5,4},{6,7},{7,6},{8,9},{9,8},{10,11... | collective-permute-start | bytes 1179656 | tf_op jit(solution)/shard_map/ppermute | solution.py:37
  37.3 7.0 %collective-permute-start.12 = (bf16[24,4096]{1,0:T(8,128)(2,1)S(1)}, bf16[24,4096]{1,0:T(8,128)(2,1)S(1)}, u32[]{:S(2)}, u32[]{:S(2)}) collective-permute-start(bf16[24,4096]{1,0:T(8,128)(2,1)S(1)} %slice.19), channel_id=1, source_target_pairs={{0,2},{1,3},{2,0},{3,1},{4,6},{5,7},{6,4},{7,5},{8,10},{9,11},{10,... | collective-permute-start | bytes 589832 | tf_op jit(solution)/shard_map/ppermute | solution.py:33
  44.5 6.6 %collective-permute-start.15 = (bf16[6,4096]{1,0:T(8,128)(2,1)S(1)}, bf16[6,4096]{1,0:T(8,128)(2,1)S(1)}, u32[]{:S(2)}, u32[]{:S(2)}) collective-permute-start(bf16[6,4096]{1,0:T(8,128)(2,1)S(1)} %get-tuple-element.49), channel_id=1, source_target_pairs={{0,4},{4,8},{8,12},{12,0},{1,5},{5,9},{9,13},{13,1},{2,6},{6,10},{... | collective-permute-start | bytes 147464 | tf_op jit(solution)/shard_map/ppermute | solution.py:33
  45.3 7.4 %collective-permute-start.14 = (bf16[6,4096]{1,0:T(8,128)(2,1)S(1)}, bf16[6,4096]{1,0:T(8,128)(2,1)S(1)}, u32[]{:S(2)}, u32[]{:S(2)}) collective-permute-start(bf16[6,4096]{1,0:T(8,128)(2,1)S(1)} %get-tuple-element.50), channel_id=1, source_target_pairs={{0,8},{4,12},{8,0},{12,4},{1,9},{5,13},{9,1},{13,5},{2,10},{6,14},... | collective-permute-start | bytes 147464 | tf_op jit(solution)/shard_map/ppermute | solution.py:33
  47.4 5.3 %collective-permute-start.13 = (bf16[6,4096]{1,0:T(8,128)(2,1)S(1)}, bf16[6,4096]{1,0:T(8,128)(2,1)S(1)}, u32[]{:S(2)}, u32[]{:S(2)}) collective-permute-start(bf16[6,4096]{1,0:T(8,128)(2,1)S(1)} %get-tuple-element.51), channel_id=1, source_target_pairs={{0,12},{4,0},{8,4},{12,8},{1,13},{5,1},{9,5},{13,9},{2,14},{6,2},{... | collective-permute-start | bytes 147464 | tf_op jit(solution)/shard_map/ppermute | solution.py:33

commit v3 on v2

--- a/solution.py
+++ b/solution.py
@@ -31,6 +31,10 @@
 
 def along(axis, size, by):
     return lambda value: lax.ppermute(value, axis, [(i, (i + by) % size) for i in range(size)])
+
+
+def across(value, size, by):
+    return lax.ppermute(value, "resp", [(i, i ^ by) for i in range(size)])
 
 
 def other_core(value, size):
@@ -67,76 +71,96 @@
     x = [x_resp[0, i].astype(jnp.float32) for i in range(responses)]
     dy = [resp_cot[0, i].astype(jnp.float32) for i in range(responses)]
     sent_r[:, :width] = jnp.concatenate(x + dy, axis=0).astype(jnp.bfloat16)
+    extra = sent_r.shape[1] - width - LANES
+    rows = x_prompt[0].astype(jnp.float32)
+    rows = [rows[t : t + 1, c : c + extra] for t in range(rows_p) for c in range(0, width, extra)]
+    sent_r[:, width : width + extra] = jnp.concatenate(rows, axis=0).astype(jnp.bfloat16)
     rows = [
         router_row(lambda t, k: route_r[0, i, k, t], lambda t, k: weight_r[0, i, k, t], t, top, experts)
         for i in range(responses)
         for t in range(length)
     ]
-    rows.append(jnp.zeros((len(rows), LANES), jnp.float32))
-    sent_r[:, width:] = jnp.concatenate(rows, axis=0).astype(jnp.bfloat16)
+    rows += [
+        router_row(lambda t, k: route_p[0, t, k], lambda t, k: weight_p[0, t, k], t, top, experts)
+        for t in range(rows_p)
+    ]
+    rows.append(jnp.zeros((sent_r.shape[0] - len(rows), LANES), jnp.float32))
+    sent_r[:, width + extra :] = jnp.concatenate(rows, axis=0).astype(jnp.bfloat16)
     cot = prompt_cot[0, 0].astype(jnp.float32)
     for i in range(1, responses):
         cot = cot + prompt_cot[0, i].astype(jnp.float32)
-    prompts = cot.shape[0]
-    here = lax.axis_index("resp") * rows_p
-    own = jnp.concatenate([x_prompt[0].astype(jnp.float32), jnp.zeros((prompts - rows_p, width), jnp.float32)], axis=0)
-    sent_p[:, :width] = jnp.concatenate([pltpu.roll(own, here, 0), cot], axis=0).astype(jnp.bfloat16)
-    rows = [
-        router_row(lambda t, k: route_p[0, t, k], lambda t, k: weight_p[0, t, k], t, top, experts)
-        for t in range(rows_p)
-    ]
-    rows.append(jnp.zeros((prompts - rows_p, LANES), jnp.float32))
-    own = pltpu.roll(jnp.concatenate(rows, axis=0), here, 0)
-    sent_p[:, width:] = jnp.concatenate([own, jnp.zeros((prompts, LANES), jnp.float32)], axis=0).astype(jnp.bfloat16)
+    sent_p[...] = cot.astype(jnp.bfloat16)
 
 
 def expert_kernel(count, spans, experts, *refs):
-    width = refs[2 * count].shape[-1]
     blocks_r, blocks_p = refs[:count], refs[count : 2 * count]
     gate_w, up_w, down_w, near, far, rows_out, gate_out, up_out, hidden_out = refs[2 * count :]
-    span_r, span_p, prompts = spans
-    tails = []
-    base = 0
-    for block in (*blocks_r, *blocks_p):
-        rows = block.shape[0]
-        rows_out[base : base + rows, :] = block[:, :width]
-        tails.append(block[:, width:].astype(jnp.float32))
-        base += rows
-    total = base
-    split = sum(b.shape[0] for b in blocks_r)
-    tail = jnp.concatenate(tails, axis=0)
-    lane = lax.broadcasted_iota(jnp.int32, tail.shape, 1)
-    mine = (lane % experts == lax.axis_index("expert")) & (lane < 3 * experts)
-    router = jnp.sum(jnp.where(mine, tail, 0.0), axis=1, keepdims=True)
+    span_r, span_p = spans
+    width = rows_out.shape[1]
+    line, prompts = blocks_r[0].shape[0], blocks_p[0].shape[0]
+    n_resp = prompts // span_p
+    extra = blocks_r[0].shape[1] - width - LANES
+    split, count_p = count * line, count * prompts
+    total = split + 2 * count_p
+    me = lax.axis_index("resp")
+
+    for i, block in enumerate(blocks_r):
+        rows_out[i * line : (i + 1) * line, :] = block[:, :width]
+    cot = [block[...].astype(jnp.float32) for block in blocks_p]
+    rows_out[split + count_p :, :] = jnp.concatenate(cot, axis=0).astype(jnp.bfloat16)
+    pieces = jnp.concatenate([block[:, width:].astype(jnp.float32) for block in blocks_r], axis=0).astype(jnp.bfloat16)
+    row = lax.broadcasted_iota(jnp.int32, (count_p, split), 0)
+    source = lax.broadcasted_iota(jnp.int32, (count_p, split), 1)
+    of = row % prompts
+    first = row // prompts * line + ((of // span_p) ^ me) * (2 * span_r)
+
+    def picked(offset):
+        return (source == first + offset).astype(jnp.float32).astype(jnp.bfloat16)
+
+    each = width // extra
+    for q in range(each):
+        part = jnp.dot(picked(of % span_p * each + q), pieces[:, :extra], preferred_element_type=jnp.float32)
+        rows_out[split : split + count_p, q * extra : (q + 1) * extra] = part.astype(jnp.bfloat16)
+
+    def router_of(tail):
+        lane = lax.broadcasted_iota(jnp.int32, tail.shape, 1)
+        mine = (lane % experts == lax.axis_index("expert")) & (lane < 3 * experts)
+        return jnp.sum(jnp.where(mine, tail, 0.0), axis=1, keepdims=True)
+
+    tail = pieces[:, extra:]
+    router_r = router_of(tail.astype(jnp.float32))
+    at = lax.broadcasted_iota(jnp.int32, router_r.shape, 0)
+    router_r = jnp.where(at % (2 * span_r) < span_r, router_r, 0.0)
+    router_p = router_of(jnp.dot(picked(span_r + of % span_p), tail, preferred_element_type=jnp.float32))
+    none = jnp.zeros((count_p, 1), jnp.float32)
+    router = jnp.concatenate([router_r, router_p, none], axis=0)
+
     values = rows_out[...]
     gate = contract_last(values, gate_w[0])
     upward = contract_last(values, up_w[0])
     wide = contract_last(values, down_w[0])
-
-    def moved(value, up):
-        top, low = value[:split], value[split:]
-        by_r, by_p = (split - span_r, total - split - prompts) if up else (span_r, prompts)
-        return jnp.concatenate([pltpu.roll(top, by_r, 0), pltpu.roll(low, by_p, 0)], axis=0)
-
     sigma = jax.nn.sigmoid(gate)
     active = gate * sigma
     hidden = router * active * upward
-    hidden_grad = router * moved(wide, True)
+    here = split + count_p
+    moved = jnp.concatenate([pltpu.roll(wide[:split], split - span_r, 0), wide[here:], wide[split:here]], axis=0)
+    hidden_out[...] = jnp.concatenate(
+        [pltpu.roll(hidden[:split], span_r, 0), hidden[here:], hidden[split:here]], axis=0
+    ).astype(jnp.bfloat16)
+    hidden_grad = router * moved
     gate_grad = (hidden_grad * upward * sigma * (1.0 + gate * (1.0 - sigma))).astype(jnp.bfloat16)
     upward_grad = (hidden_grad * active).astype(jnp.bfloat16)
     gate_out[...] = gate_grad
     up_out[...] = upward_grad
-    hidden_out[...] = moved(hidden, False).astype(jnp.bfloat16)
     half = near.shape[0]
     tokens = 2 * half
-    each = span_r + span_p
+    span = span_r + span_p
     slot = lax.broadcasted_iota(jnp.int32, (tokens, total), 0)
     row = lax.broadcasted_iota(jnp.int32, (tokens, total), 1)
-    source, token = slot // each, slot % each
+    source, token = slot // span, slot % span
     from_r = source * (2 * span_r) + token
-    n_resp = prompts // span_p
-    giver = (lax.axis_index("resp") + n_resp - source % n_resp) % n_resp
-    from_p = split + source // n_resp * (2 * prompts) + giver * span_p + token - span_r
+    giver = (source % n_resp) ^ me
+    from_p = split + source // n_resp * prompts + giver * span_p + token - span_r
     chosen = (row == jnp.where(token < span_r, from_r, from_p)).astype(jnp.float32).astype(jnp.bfloat16)
     gate_grad = jnp.dot(chosen, gate_grad, preferred_element_type=jnp.float32).astype(jnp.bfloat16)
     upward_grad = jnp.dot(chosen, upward_grad, preferred_element_type=jnp.float32).astype(jnp.bfloat16)
@@ -232,11 +256,12 @@
     routing = [route_prompt, jnp.swapaxes(route_resp, -1, -2), weight_prompt, jnp.swapaxes(weight_resp, -1, -2)]
     routing = [held(a, pltpu.HBM) for a in routing]
     prompts = prompt_cot.shape[2]
+    extra = rows_p * width // (2 * rows_r)
     sent_r, sent_p = pl.pallas_call(
         functools.partial(prepare_kernel, experts),
         out_shape=[
-            jax.ShapeDtypeStruct((2 * rows_r, width + LANES), bf16),
-            jax.ShapeDtypeStruct((2 * prompts, width + LANES), bf16),
+            jax.ShapeDtypeStruct((2 * rows_r, width + extra + LANES), bf16),
+            jax.ShapeDtypeStruct((prompts, width), bf16),
         ],
         in_specs=[HBM] * 8,
         out_specs=[VMEM] * 2,
@@ -246,10 +271,6 @@
         compiler_params=params(8),
         name="prepare",
     )(*given, *routing)
-
-    def spread(line):
-        near = [line] + [along("expert", n_expert, 2 * j)(line) for j in range(1, chips)]
-        return near + [other_core(block, n_expert) for block in near]
 
     weights = [w_gate, w_up, w_down]
     small = n_resp * n_expert <= 32
@@ -264,19 +285,29 @@
             cost_estimate=pl.CostEstimate(flops=0, bytes_accessed=6 * w_gate.size, transcendentals=0),
             name="load",
         )(*[held(w, pltpu.HBM) for w in weights])
+    if sent_p.shape[0] == sent_r.shape[0]:
+        got = across(jnp.concatenate([sent_r, sent_p], axis=1), n_resp, 1)
+        got_r, got_p = got[:, : sent_r.shape[1]], got[:, sent_r.shape[1] :]
+    else:
+        got_r, got_p = across(sent_r, n_resp, 1), across(sent_p, n_resp, 1)
+    rest_r = [got_r] + [across(sent_r, n_resp, by) for by in range(2, n_resp)]
     by = 1
     while by < n_resp:
-        if by == 2:
+        got_p = got_p if by == 1 else across(sent_p, n_resp, by)
+        sent_p = (sent_p.astype(jnp.float32) + got_p.astype(jnp.float32)).astype(bf16)
+        if by == 1:
             sent_p, *weights = lax.optimization_barrier((sent_p, *weights))
-        got = lax.ppermute(sent_p, "resp", [(i, i ^ by) for i in range(n_resp)])
-        sent_p = (sent_p.astype(jnp.float32) + got.astype(jnp.float32)).astype(bf16)
         by *= 2
-    line_r = jnp.concatenate([sent_r] + [along("resp", n_resp, k)(sent_r) for k in range(1, n_resp)], axis=0)
-    all_r = spread(line_r)
-    all_p = spread(sent_p)
-
+    over = [along("expert", n_expert, 2 * j) for j in range(1, chips)]
+    line_r = jnp.concatenate([sent_r, *rest_r], axis=0)
+    far_r = [move(line_r) for move in over]
+    far_p = [move(sent_p) for move in over]
+    far_r, far_p = lax.optimization_barrier((far_r, far_p))
+    near_r, near_p = [line_r, *far_r], [sent_p, *far_p]
+    all_r = near_r + [other_core(block, n_expert) for block in near_r]
+    all_p = near_p + [other_core(block, n_expert) for block in near_p]
     count = len(all_r)
-    rows = sum(b.shape[0] for b in (*all_r, *all_p))
+    rows = count * (line_r.shape[0] + 2 * prompts)
     tokens = rows // 2
     half = tokens // 2
     kept = pltpu.VMEM if small else jax.ShapeDtypeStruct
@@ -284,7 +315,7 @@
     if small:
         taken = [held(a, pltpu.VMEM) for a in taken]
     near, far, values, gate_grad, upward_grad, hidden = pl.pallas_call(
-        functools.partial(expert_kernel, count, (rows_r, rows_p, prompts), experts),
+        functools.partial(expert_kernel, count, (rows_r, rows_p), experts),
         out_shape=[
             kept((half, width), bf16),
             kept((half, width), bf16),
@@ -307,7 +338,7 @@
         line = line + along("expert", n_expert, -2 * j)(total[j * block : (j + 1) * block]).astype(jnp.float32)
     line = line.astype(bf16)
     each = rows_r + rows_p
-    own = [line[:each]] + [along("resp", n_resp, -k)(line[k * each : (k + 1) * each]) for k in range(1, n_resp)]
+    own = [line[:each]] + [across(line[k * each : (k + 1) * each], n_resp, k) for k in range(1, n_resp)]
     grad_prompt, grad_resp = pl.pallas_call(
         functools.partial(finish_kernel, rows_r),
         out_shape=[jax.ShapeDtypeStruct(x_prompt.shape, bf16), jax.ShapeDtypeStruct(x_resp.shape, bf16)],

time: 53.5 us -> 50 us (0.935)
  waiting for transfers between devices: 16.9 us -> 13.6 us
    ppermute x9 -> x3, starting transfers between devices: 15.3 us -> 4.55 us  [along(): lax.ppermute(value, axis, [(i, (i + by) % size) for i in range(size)])]
    ppermute x2 -> x7, starting transfers between devices: 2.55 us -> 13 us  [across(): return lax.ppermute(value, 'resp', [(i, i ^ by) for i in range(size)])]
    ppermute x2 -> x7, waiting for transfers between devices: 8.31 us -> 4.67 us  [across(): return lax.ppermute(value, 'resp', [(i, i ^ by) for i in range(size)])]
    ppermute x9 -> x3, waiting for transfers between devices: 5.68 us -> 6.07 us  [along(): lax.ppermute(value, axis, [(i, (i + by) % size) for i in range(size)])]
  transfers between devices with their start and end apart: 16 -> 15, of which waited for: 7 -> 8; matrix products, arithmetic and copies ran while one was open for 0% -> 0% of each run, Pallas kernels for 19% -> 20%
where the time goes in v3:
time: 50 us; the launch traced here: 49.8 us
  starting transfers between devices  18.3 us (37%)
  Pallas kernels  16.8 us (34%)
  waiting for transfers between devices  13.6 us (27%)
  between operations  0.76 us (2%)
    ppermute x7, starting transfers between devices, across(): return lax.ppermute(value, 'resp', [(i, i ^ by) for i in range(size)])  13 us
    pallas_call x3, Pallas kernels, outer(): pl.pallas_call(outer_kernel, out_shape=(pltpu.HBM if small else jax.Shape...  6.41 us
    ppermute x3, waiting for transfers between devices, along(): lax.ppermute(value, axis, [(i, (i + by) % size) for i in range(size)])  6.07 us
    pallas_call x1, Pallas kernels, body(): pl.pallas_call(functools.partial(expert_kernel, count, (rows_r, rows_p),...  4.94 us
    ppermute x7, waiting for transfers between devices, across(): return lax.ppermute(value, 'resp', [(i, i ^ by) for i in range(size)])  4.67 us
    ppermute x3, starting transfers between devices, along(): lax.ppermute(value, axis, [(i, (i + by) % size) for i in range(size)])  4.55 us
    pallas_call x1, Pallas kernels, body(): pl.pallas_call(load_kernel, out_shape=[pltpu.VMEM(w.shape, w.dtype) for w...  3.78 us
    ppermute x5, waiting for transfers between devices, other_core(): return lax.ppermute(value, 'expert', [(i, i ^ 1) for i in range(size)])  2.9 us
  transfers between devices with their start and end apart: 15, of which 8 were waited for; matrix products, arithmetic and copies ran while one was open for 0% of the time, Pallas kernels for 20%

profile of v3, /device:TPU:0, one launch (start us, length us, event | category | flops | bytes accessed | tf_op | source)
XLA Modules:
  0.0 49.8 jit_solution(2911983900827900283)
XLA Ops:
  0.6 1.0 %prepare.1 = (bf16[8,5248]{1,0:T(8,128)(2,1)S(1)}, bf16[8,4096]{1,0:T(8,128)(2,1)S(1)}) custom-call(bf16[1,2,4096]{2,1,0:T(2,128)(2,1)} %refs_0_.2, bf16[1,1,4,4096]{3,2,1,0:T(4,128)(2,1)} %refs_1_.2, bf16[1,1,8,4096]{3,2,1,0:T(8,128)(2,1)} %refs_2_.2, bf16[1,1,4,4096]{3,2,1,0:T(4,128)(2,1)} %refs_3_.1, s32[1,2,2]{2,1,0:T(2,128)} %refs_4_.1, ...), custom_call_target="tpu_custom_call" | custom-call | tf_op jit(solution)/shard_map/prepare/pallas_call | solution.py:260
  1.7 3.1 %collective-permute-start = (bf16[8,9344]{1,0:T(8,128)(2,1)S(1)}, bf16[8,9344]{1,0:T(8,128)(2,1)S(1)}, u32[]{:S(2)}, u32[]{:S(2)}) collective-permute-start(bf16[8,9344]{1,0:T(8,128)(2,1)S(1)} %pad_maximum_fusion.1), channel_id=1, source_target_pairs={{0,4},{4,0},{8,12},{12,8},{1,5},{5,1},{9,13},{13,9},{2,6},{6,2},{1... | collective-permute-start | bytes 448520 | tf_op jit(solution)/shard_map/ppermute | solution.py:37
  4.8 2.5 %collective-permute-start.2 = (bf16[8,5248]{1,0:T(8,128)(2,1)S(1)}, bf16[8,5248]{1,0:T(8,128)(2,1)S(1)}, u32[]{:S(2)}, u32[]{:S(2)}) collective-permute-start(bf16[8,5248]{1,0:T(8,128)(2,1)S(1)} %get-tuple-element.29), channel_id=1, source_target_pairs={{0,12},{4,8},{8,4},{12,0},{1,13},{5,9},{9,5},{13,1},{2,14},{6,10},... | collective-permute-start | bytes 251912 | tf_op jit(solution)/shard_map/ppermute | solution.py:37
  7.3 0.1 collective-permute-start.1
  7.4 3.8 %load.1 = (bf16[1,384,4096]{2,1,0:T(8,128)(2,1)S(1)}, bf16[1,384,4096]{2,1,0:T(8,128)(2,1)S(1)}, bf16[1,384,4096]{2,1,0:T(8,128)(2,1)S(1)}) custom-call(bf16[1,384,4096]{2,1,0:T(8,128)(2,1)} %refs_0_.3, bf16[1,384,4096]{2,1,0:T(8,128)(2,1)} %refs_1_.3, bf16[1,384,4096]{2,1,0:T(8,128)(2,1)} %refs_2_.3), custom_call_target="tpu_custom_call" | custom-call | bytes 9437184 | tf_op jit(solution)/shard_map/load/pallas_call | solution.py:278
  11.2 0.0 collective-permute-done
  11.2 2.9 %collective-permute-start.4 = (bf16[8,4096]{1,0:T(8,128)(2,1)S(1)}, bf16[8,4096]{1,0:T(8,128)(2,1)S(1)}, u32[]{:S(2)}, u32[]{:S(2)}) collective-permute-start(bf16[8,4096]{1,0:T(8,128)(2,1)S(1)} %add_convert_fusion.3), channel_id=1, source_target_pairs={{0,8},{4,12},{8,0},{12,4},{1,9},{5,13},{9,1},{13,5},{2,10},{6,14},... | collective-permute-start | bytes 196616 | tf_op jit(solution)/shard_map/ppermute | solution.py:37
  14.1 0.0 collective-permute-done.2
  14.1 2.6 %collective-permute-done.1 = bf16[8,5248]{1,0:T(8,128)(2,1)S(1)} collective-permute-done((bf16[8,5248]{1,0:T(8,128)(2,1)S(1)}, bf16[8,5248]{1,0:T(8,128)(2,1)S(1)}, u32[]{:S(2)}, u32[]{:S(2)}) %collective-permute-start.1) | collective-permute-done | bytes 84000 | tf_op jit(solution)/shard_map/ppermute | solution.py:37
  16.7 1.6 %collective-permute-start.3 = (bf16[32,5248]{1,0:T(8,128)(2,1)S(1)}, bf16[32,5248]{1,0:T(8,128)(2,1)S(1)}, u32[]{:S(2)}, u32[]{:S(2)}) collective-permute-start(bf16[32,5248]{1,0:T(8,128)(2,1)S(1)} %pad_maximum_fusion.refs_0_), channel_id=1, source_target_pairs={{0,2},{1,3},{2,0},{3,1},{4,6},{5,7},{6,4},{7,5},{8,10},{9,11},{10,... | collective-permute-start | bytes 1007624 | tf_op jit(solution)/shard_map/ppermute | solution.py:33
  18.3 0.0 collective-permute-done.4
  18.3 1.4 %collective-permute-start.5 = (bf16[8,4096]{1,0:T(8,128)(2,1)S(1)}, bf16[8,4096]{1,0:T(8,128)(2,1)S(1)}, u32[]{:S(2)}, u32[]{:S(2)}) collective-permute-start(bf16[8,4096]{1,0:T(8,128)(2,1)S(1)} %add_convert_fusion.2.refs_4_), channel_id=1, source_target_pairs={{0,2},{1,3},{2,0},{3,1},{4,6},{5,7},{6,4},{7,5},{8,10},{9,11},{10,... | collective-permute-start | bytes 196616 | tf_op jit(solution)/shard_map/ppermute | solution.py:33
  19.7 0.0 collective-permute-start.6
  19.7 4.9 %collective-permute-done.5.refs_5_ = bf16[8,4096]{1,0:T(8,128)(2,1)S(1)} collective-permute-done((bf16[8,4096]{1,0:T(8,128)(2,1)S(1)}, bf16[8,4096]{1,0:T(8,128)(2,1)S(1)}, u32[]{:S(2)}, u32[]{:S(2)}) %collective-permute-start.5) | collective-permute-done | bytes 65568 | tf_op jit(solution)/shard_map/ppermute | solution.py:33
  24.6 0.0 collective-permute-done.3.refs_1_
  24.6 0.0 collective-permute-start.7
  24.6 0.5 %collective-permute-start.8 = (bf16[8,4096]{1,0:T(8,128)(2,1)S(1)}, bf16[8,4096]{1,0:T(8,128)(2,1)S(1)}, u32[]{:S(2)}, u32[]{:S(2)}) collective-permute-start(bf16[8,4096]{1,0:T(8,128)(2,1)S(1)} %add_convert_fusion.2.refs_4_), channel_id=1, source_target_pairs={{0,1},{1,0},{2,3},{3,2},{4,5},{5,4},{6,7},{7,6},{8,9},{9,8},{10,11... | collective-permute-start | bytes 196616 | tf_op jit(solution)/shard_map/ppermute | solution.py:41
  25.2 0.0 collective-permute-start.9
  25.2 1.2 %collective-permute-done.8.refs_6_ = bf16[8,4096]{1,0:T(8,128)(2,1)S(1)} collective-permute-done((bf16[8,4096]{1,0:T(8,128)(2,1)S(1)}, bf16[8,4096]{1,0:T(8,128)(2,1)S(1)}, u32[]{:S(2)}, u32[]{:S(2)}) %collective-permute-start.8) | collective-permute-done | bytes 65568 | tf_op jit(solution)/shard_map/ppermute | solution.py:41
  26.4 0.0 collective-permute-done.6.refs_2_
  26.4 0.1 collective-permute-done.9.refs_7_
  26.5 0.0 collective-permute-done.7.refs_3_
  26.5 4.9 %expert.1 = (bf16[48,4096]{1,0:T(8,128)(2,1)S(1)}, bf16[48,4096]{1,0:T(8,128)(2,1)S(1)}, bf16[192,4096]{1,0:T(8,128)(2,1)S(1)}, bf16[192,384]{1,0:T(8,128)(2,1)S...) custom-call(bf16[32,5248]{1,0:T(8,128)(2,1)S(1)} %pad_maximum_fusion.refs_0_, ...), custom_call_target="tpu_custom_call" | custom-call | flops 3019898880 | bytes 20971520 | tf_op jit(solution)/shard_map/expert/pallas_call | solution.py:317
  31.4 0.2 collective-permute-start.10
  31.6 1.6 %collective-permute-done.10 = bf16[48,4096]{1,0:T(8,128)(2,1)S(1)} collective-permute-done((bf16[48,4096]{1,0:T(8,128)(2,1)S(1)}, bf16[48,4096]{1,0:T(8,128)(2,1)S(1)}, u32[]{:S(2)}, u32[]{:S(2)}) %collective-permute-start.10) | collective-permute-done | bytes 393248 | tf_op jit(solution)/shard_map/ppermute | solution.py:41
  33.2 0.1 add_convert_fusion
  33.3 1.6 %collective-permute-start.11 = (bf16[24,4096]{1,0:T(8,128)(2,1)S(1)}, bf16[24,4096]{1,0:T(8,128)(2,1)S(1)}, u32[]{:S(2)}, u32[]{:S(2)}) collective-permute-start(bf16[24,4096]{1,0:T(8,128)(2,1)S(1)} %slice.27), channel_id=1, source_target_pairs={{0,2},{1,3},{2,0},{3,1},{4,6},{5,7},{6,4},{7,5},{8,10},{9,11},{10,... | collective-permute-start | bytes 589832 | tf_op jit(solution)/shard_map/ppermute | solution.py:33
  34.9 2.1 %outer.3 = bf16[1,384,4096]{2,1,0:T(8,128)(2,1)} custom-call(bf16[192,384]{1,0:T(8,128)(2,1)S(1)} %get-tuple-element.49.left, bf16[192,4096]{1,0:T(8,128)(2,1)S(1)} %get-tuple-element.50.values), custom_call_target="tpu_custom_call" | custom-call | flops 603979776 | bytes 3145728 | tf_op jit(solution)/shard_map/outer/pallas_call | solution.py:204
  37.1 2.1 %outer.4 = bf16[1,384,4096]{2,1,0:T(8,128)(2,1)} custom-call(bf16[192,384]{1,0:T(8,128)(2,1)S(1)} %get-tuple-element.51.left, bf16[192,4096]{1,0:T(8,128)(2,1)S(1)} %get-tuple-element.50.values), custom_call_target="tpu_custom_call" | custom-call | flops 603979776 | bytes 3145728 | tf_op jit(solution)/shard_map/outer/pallas_call | solution.py:204
  39.2 1.1 %collective-permute-done.11 = bf16[24,4096]{1,0:T(8,128)(2,1)S(1)} collective-permute-done((bf16[24,4096]{1,0:T(8,128)(2,1)S(1)}, bf16[24,4096]{1,0:T(8,128)(2,1)S(1)}, u32[]{:S(2)}, u32[]{:S(2)}) %collective-permute-start.11) | collective-permute-done | bytes 196640 | tf_op jit(solution)/shard_map/ppermute | solution.py:33
  40.4 0.1 fusion
  40.5 3.0 %collective-permute-start.14 = (bf16[6,4096]{1,0:T(8,128)(2,1)S(1)}, bf16[6,4096]{1,0:T(8,128)(2,1)S(1)}, u32[]{:S(2)}, u32[]{:S(2)}) collective-permute-start(bf16[6,4096]{1,0:T(8,128)(2,1)S(1)} %get-tuple-element.53), channel_id=1, source_target_pairs={{0,12},{4,8},{8,4},{12,0},{1,13},{5,9},{9,5},{13,1},{2,14},{6,10},... | collective-permute-start | bytes 147464 | tf_op jit(solution)/shard_map/ppermute | solution.py:37
  43.5 0.0 collective-permute-start.13
  43.5 1.4 %collective-permute-start.12 = (bf16[6,4096]{1,0:T(8,128)(2,1)S(1)}, bf16[6,4096]{1,0:T(8,128)(2,1)S(1)}, u32[]{:S(2)}, u32[]{:S(2)}) collective-permute-start(bf16[6,4096]{1,0:T(8,128)(2,1)S(1)} %get-tuple-element.55), channel_id=1, source_target_pairs={{0,4},{4,0},{8,12},{12,8},{1,5},{5,1},{9,13},{13,9},{2,6},{6,2},{1... | collective-permute-start | bytes 147464 | tf_op jit(solution)/shard_map/ppermute | solution.py:37
  44.9 2.1 %outer.5 = bf16[1,384,4096]{2,1,0:T(8,128)(2,1)} custom-call(bf16[192,384]{1,0:T(8,128)(2,1)S(1)} %get-tuple-element.52.left, bf16[192,4096]{1,0:T(8,128)(2,1)S(1)} %get-tuple-element.50.values), custom_call_target="tpu_custom_call" | custom-call | flops 603979776 | bytes 3145728 | tf_op jit(solution)/shard_map/outer/pallas_call | solution.py:204
  47.1 0.0 collective-permute-done.14.refs_3_
  47.1 1.9 %collective-permute-done.13.refs_2_ = bf16[6,4096]{1,0:T(8,128)(2,1)S(1)} collective-permute-done((bf16[6,4096]{1,0:T(8,128)(2,1)S(1)}, bf16[6,4096]{1,0:T(8,128)(2,1)S(1)}, u32[]{:S(2)}, u32[]{:S(2)}) %collective-permute-start.13) | collective-permute-done | bytes 49184 | tf_op jit(solution)/shard_map/ppermute | solution.py:37
  49.0 0.1 collective-permute-done.12.refs_1_
  49.1 0.7 %finish.1 = (bf16[1,2,4096]{2,1,0:T(2,128)(2,1)}, bf16[1,1,4,4096]{3,2,1,0:T(4,128)(2,1)}) custom-call(bf16[6,4096]{1,0:T(8,128)(2,1)S(1)} %get-tuple-element.56.refs_0_, bf16[6,4096]{1,0:T(8,128)(2,1)S(1)} %collective-permute-done.12.refs_1_, bf16[6,4096]{1,0:T(8,128)(2,1)S(1)} %collective-permute-done.13.refs_2_, ...), custom_call_target="tpu_custom_call" | custom-call | tf_op jit(solution)/shard_map/finish/pallas_call | solution.py:342
  (7 shorter events, 0.1 us)
Async XLA Ops:
  1.7 9.5 %collective-permute-start = (bf16[8,9344]{1,0:T(8,128)(2,1)S(1)}, bf16[8,9344]{1,0:T(8,128)(2,1)S(1)}, u32[]{:S(2)}, u32[]{:S(2)}) collective-permute-start(bf16[8,9344]{1,0:T(8,128)(2,1)S(1)} %pad_maximum_fusion.1), channel_id=1, source_target_pairs={{0,4},{4,0},{8,12},{12,8},{1,5},{5,1},{9,13},{13,9},{2,6},{6,2},{1... | collective-permute-start | bytes 448520 | tf_op jit(solution)/shard_map/ppermute | solution.py:37
  4.8 9.3 %collective-permute-start.2 = (bf16[8,5248]{1,0:T(8,128)(2,1)S(1)}, bf16[8,5248]{1,0:T(8,128)(2,1)S(1)}, u32[]{:S(2)}, u32[]{:S(2)}) collective-permute-start(bf16[8,5248]{1,0:T(8,128)(2,1)S(1)} %get-tuple-element.29), channel_id=1, source_target_pairs={{0,12},{4,8},{8,4},{12,0},{1,13},{5,9},{9,5},{13,1},{2,14},{6,10},... | collective-permute-start | bytes 251912 | tf_op jit(solution)/shard_map/ppermute | solution.py:37
  7.3 9.4 %collective-permute-start.1 = (bf16[8,5248]{1,0:T(8,128)(2,1)S(1)}, bf16[8,5248]{1,0:T(8,128)(2,1)S(1)}, u32[]{:S(2)}, u32[]{:S(2)}) collective-permute-start(bf16[8,5248]{1,0:T(8,128)(2,1)S(1)} %get-tuple-element.29), channel_id=1, source_target_pairs={{0,8},{4,12},{8,0},{12,4},{1,9},{5,13},{9,1},{13,5},{2,10},{6,14},... | collective-permute-start | bytes 251912 | tf_op jit(solution)/shard_map/ppermute | solution.py:37
  11.2 7.1 %collective-permute-start.4 = (bf16[8,4096]{1,0:T(8,128)(2,1)S(1)}, bf16[8,4096]{1,0:T(8,128)(2,1)S(1)}, u32[]{:S(2)}, u32[]{:S(2)}) collective-permute-start(bf16[8,4096]{1,0:T(8,128)(2,1)S(1)} %add_convert_fusion.3), channel_id=1, source_target_pairs={{0,8},{4,12},{8,0},{12,4},{1,9},{5,13},{9,1},{13,5},{2,10},{6,14},... | collective-permute-start | bytes 196616 | tf_op jit(solution)/shard_map/ppermute | solution.py:37
  16.7 7.9 %collective-permute-start.3 = (bf16[32,5248]{1,0:T(8,128)(2,1)S(1)}, bf16[32,5248]{1,0:T(8,128)(2,1)S(1)}, u32[]{:S(2)}, u32[]{:S(2)}) collective-permute-start(bf16[32,5248]{1,0:T(8,128)(2,1)S(1)} %pad_maximum_fusion.refs_0_), channel_id=1, source_target_pairs={{0,2},{1,3},{2,0},{3,1},{4,6},{5,7},{6,4},{7,5},{8,10},{9,11},{10,... | collective-permute-start | bytes 1007624 | tf_op jit(solution)/shard_map/ppermute | solution.py:33
  18.3 6.3 %collective-permute-start.5 = (bf16[8,4096]{1,0:T(8,128)(2,1)S(1)}, bf16[8,4096]{1,0:T(8,128)(2,1)S(1)}, u32[]{:S(2)}, u32[]{:S(2)}) collective-permute-start(bf16[8,4096]{1,0:T(8,128)(2,1)S(1)} %add_convert_fusion.2.refs_4_), channel_id=1, source_target_pairs={{0,2},{1,3},{2,0},{3,1},{4,6},{5,7},{6,4},{7,5},{8,10},{9,11},{10,... | collective-permute-start | bytes 196616 | tf_op jit(solution)/shard_map/ppermute | solution.py:33
  19.7 6.7 %collective-permute-start.6 = (bf16[32,5248]{1,0:T(8,128)(2,1)S(1)}, bf16[32,5248]{1,0:T(8,128)(2,1)S(1)}, u32[]{:S(2)}, u32[]{:S(2)}) collective-permute-start(bf16[32,5248]{1,0:T(8,128)(2,1)S(1)} %pad_maximum_fusion.refs_0_), channel_id=1, source_target_pairs={{0,1},{1,0},{2,3},{3,2},{4,5},{5,4},{6,7},{7,6},{8,9},{9,8},{10,11... | collective-permute-start | bytes 1007624 | tf_op jit(solution)/shard_map/ppermute | solution.py:41
  24.6 1.8 %collective-permute-start.7 = (bf16[32,5248]{1,0:T(8,128)(2,1)S(1)}, bf16[32,5248]{1,0:T(8,128)(2,1)S(1)}, u32[]{:S(2)}, u32[]{:S(2)}) collective-permute-start(bf16[32,5248]{1,0:T(8,128)(2,1)S(1)} %collective-permute-done.3.refs_1_), channel_id=1, source_target_pairs={{0,1},{1,0},{2,3},{3,2},{4,5},{5,4},{6,7},{7,6},{8,9},{9,8},{10,11... | collective-permute-start | bytes 1007624 | tf_op jit(solution)/shard_map/ppermute | solution.py:41
  24.6 1.7 %collective-permute-start.8 = (bf16[8,4096]{1,0:T(8,128)(2,1)S(1)}, bf16[8,4096]{1,0:T(8,128)(2,1)S(1)}, u32[]{:S(2)}, u32[]{:S(2)}) collective-permute-start(bf16[8,4096]{1,0:T(8,128)(2,1)S(1)} %add_convert_fusion.2.refs_4_), channel_id=1, source_target_pairs={{0,1},{1,0},{2,3},{3,2},{4,5},{5,4},{6,7},{7,6},{8,9},{9,8},{10,11... | collective-permute-start | bytes 196616 | tf_op jit(solution)/shard_map/ppermute | solution.py:41
  25.2 1.3 %collective-permute-start.9 = (bf16[8,4096]{1,0:T(8,128)(2,1)S(1)}, bf16[8,4096]{1,0:T(8,128)(2,1)S(1)}, u32[]{:S(2)}, u32[]{:S(2)}) collective-permute-start(bf16[8,4096]{1,0:T(8,128)(2,1)S(1)} %collective-permute-done.5.refs_5_), channel_id=1, source_target_pairs={{0,1},{1,0},{2,3},{3,2},{4,5},{5,4},{6,7},{7,6},{8,9},{9,8},{10,11... | collective-permute-start | bytes 196616 | tf_op jit(solution)/shard_map/ppermute | solution.py:41
  31.4 1.8 %collective-permute-start.10 = (bf16[48,4096]{1,0:T(8,128)(2,1)S(1)}, bf16[48,4096]{1,0:T(8,128)(2,1)S(1)}, u32[]{:S(2)}, u32[]{:S(2)}) collective-permute-start(bf16[48,4096]{1,0:T(8,128)(2,1)S(1)} %get-tuple-element.41), channel_id=1, source_target_pairs={{0,1},{1,0},{2,3},{3,2},{4,5},{5,4},{6,7},{7,6},{8,9},{9,8},{10,11... | collective-permute-start | bytes 1179656 | tf_op jit(solution)/shard_map/ppermute | solution.py:41
  33.3 7.0 %collective-permute-start.11 = (bf16[24,4096]{1,0:T(8,128)(2,1)S(1)}, bf16[24,4096]{1,0:T(8,128)(2,1)S(1)}, u32[]{:S(2)}, u32[]{:S(2)}) collective-permute-start(bf16[24,4096]{1,0:T(8,128)(2,1)S(1)} %slice.27), channel_id=1, source_target_pairs={{0,2},{1,3},{2,0},{3,1},{4,6},{5,7},{6,4},{7,5},{8,10},{9,11},{10,... | collective-permute-start | bytes 589832 | tf_op jit(solution)/shard_map/ppermute | solution.py:33
  40.5 6.6 %collective-permute-start.14 = (bf16[6,4096]{1,0:T(8,128)(2,1)S(1)}, bf16[6,4096]{1,0:T(8,128)(2,1)S(1)}, u32[]{:S(2)}, u32[]{:S(2)}) collective-permute-start(bf16[6,4096]{1,0:T(8,128)(2,1)S(1)} %get-tuple-element.53), channel_id=1, source_target_pairs={{0,12},{4,8},{8,4},{12,0},{1,13},{5,9},{9,5},{13,1},{2,14},{6,10},... | collective-permute-start | bytes 147464 | tf_op jit(solution)/shard_map/ppermute | solution.py:37
  43.5 5.5 %collective-permute-start.13 = (bf16[6,4096]{1,0:T(8,128)(2,1)S(1)}, bf16[6,4096]{1,0:T(8,128)(2,1)S(1)}, u32[]{:S(2)}, u32[]{:S(2)}) collective-permute-start(bf16[6,4096]{1,0:T(8,128)(2,1)S(1)} %get-tuple-element.54), channel_id=1, source_target_pairs={{0,8},{4,12},{8,0},{12,4},{1,9},{5,13},{9,1},{13,5},{2,10},{6,14},... | collective-permute-start | bytes 147464 | tf_op jit(solution)/shard_map/ppermute | solution.py:37
  43.5 5.7 %collective-permute-start.12 = (bf16[6,4096]{1,0:T(8,128)(2,1)S(1)}, bf16[6,4096]{1,0:T(8,128)(2,1)S(1)}, u32[]{:S(2)}, u32[]{:S(2)}) collective-permute-start(bf16[6,4096]{1,0:T(8,128)(2,1)S(1)} %get-tuple-element.55), channel_id=1, source_target_pairs={{0,4},{4,0},{8,12},{12,8},{1,5},{5,1},{9,13},{13,9},{2,6},{6,2},{1... | collective-permute-start | bytes 147464 | tf_op jit(solution)/shard_map/ppermute | solution.py:37

commit v4 on v3

--- a/solution.py
+++ b/solution.py
@@ -94,7 +94,7 @@
 
 def expert_kernel(count, spans, experts, *refs):
     blocks_r, blocks_p = refs[:count], refs[count : 2 * count]
-    gate_w, up_w, down_w, near, far, rows_out, gate_out, up_out, hidden_out = refs[2 * count :]
+    gate_w, up_w, down_w, near, far, rows_out, gate_out, up_out, hidden_out = refs[2 * count : 2 * count + 9]
     span_r, span_p = spans
     width = rows_out.shape[1]
     line, prompts = blocks_r[0].shape[0], blocks_p[0].shape[0]
@@ -152,24 +152,45 @@
     upward_grad = (hidden_grad * active).astype(jnp.bfloat16)
     gate_out[...] = gate_grad
     up_out[...] = upward_grad
+    packed = refs[-1] if len(refs) > 2 * count + 9 else None
     half = near.shape[0]
-    tokens = 2 * half
+    sources = count * n_resp
     span = span_r + span_p
+    tokens = sources * span
     slot = lax.broadcasted_iota(jnp.int32, (tokens, total), 0)
     row = lax.broadcasted_iota(jnp.int32, (tokens, total), 1)
-    source, token = slot // span, slot % span
+    if packed is None:
+        source, token = slot // span, slot % span
+        of_prompt = token >= span_r
+        prompt = token - span_r
+    else:
+        of_prompt = slot >= sources * span_r
+        prompt = slot - sources * span_r
+        source = jnp.where(of_prompt, prompt // span_p, slot // span_r)
+        token, prompt = slot % span_r, prompt % span_p
     from_r = source * (2 * span_r) + token
     giver = (source % n_resp) ^ me
-    from_p = split + source // n_resp * prompts + giver * span_p + token - span_r
-    chosen = (row == jnp.where(token < span_r, from_r, from_p)).astype(jnp.float32).astype(jnp.bfloat16)
+    from_p = split + source // n_resp * prompts + giver * span_p + prompt
+    chosen = (row == jnp.where(of_prompt, from_p, from_r)).astype(jnp.float32).astype(jnp.bfloat16)
     gate_grad = jnp.dot(chosen, gate_grad, preferred_element_type=jnp.float32).astype(jnp.bfloat16)
     upward_grad = jnp.dot(chosen, upward_grad, preferred_element_type=jnp.float32).astype(jnp.bfloat16)
-    step = 1024 if width % 1024 == 0 else width
-    for c in range(0, width, step):
-        value = jnp.dot(gate_grad, gate_w[0, :, c : c + step], preferred_element_type=jnp.float32)
-        value = value + jnp.dot(upward_grad, up_w[0, :, c : c + step], preferred_element_type=jnp.float32)
-        near[:, c : c + step] = value[:half].astype(jnp.bfloat16)
-        far[:, c : c + step] = value[half:].astype(jnp.bfloat16)
+    for q in range(each):
+        c = q * extra
+        value = jnp.dot(gate_grad, gate_w[0, :, c : c + extra], preferred_element_type=jnp.float32)
+        value = value + jnp.dot(upward_grad, up_w[0, :, c : c + extra], preferred_element_type=jnp.float32)
+        if packed is None:
+            near[:, c : c + extra] = value[:half].astype(jnp.bfloat16)
+            far[:, c : c + extra] = value[half:].astype(jnp.bfloat16)
+        else:
+            line, at = divmod(c, width // 2)
+            for i in range(0, extra, LANES):
+                lanes = value[:, i : i + LANES]
+                packed[(at + i) // LANES, pl.ds(line, sources * span_r, stride=2), :] = lanes[: sources * span_r]
+                packed[(width // 2 + i) // LANES, pl.ds(q, sources * span_p, stride=each), :] = lanes[sources * span_r :]
+    if packed is not None:
+        for i in range(packed.shape[0]):
+            near[:, i * LANES : (i + 1) * LANES] = packed[i, :half].astype(jnp.bfloat16)
+            far[:, i * LANES : (i + 1) * LANES] = packed[i, half:].astype(jnp.bfloat16)
 
 
 def load_kernel(*refs):
@@ -217,16 +238,30 @@
     )(*given)
 
 
-def finish_kernel(rows_r, *refs):
-    parts, prompt_out, resp_out = refs[:-2], refs[-2], refs[-1]
+def finish_kernel(rows_r, rows_p, *refs):
+    parts, prompt_out, resp_out = refs[: -3], refs[-3], refs[-2]
+    scratch = refs[-1]
     total = parts[0][...].astype(jnp.float32)
     for part in parts[1:]:
         total = total + part[...].astype(jnp.float32)
-    total = total.astype(jnp.bfloat16)
+    width = prompt_out.shape[-1]
     responses, length = resp_out.shape[1:3]
+    if total.shape[1] == width:
+        total = total.astype(jnp.bfloat16)
+        for i in range(responses):
+            resp_out[0, i] = total[i * length : (i + 1) * length]
+        prompt_out[0] = total[rows_r:]
+        return
+    lanes, half = scratch.shape[0], width // 2 // LANES
+    for i in range(lanes):
+        scratch[i] = total[:, i * LANES : (i + 1) * LANES]
+    rows = [scratch[i, pl.ds(line, rows_r, stride=2), :] for line in range(2) for i in range(half)]
+    rows = jnp.concatenate(rows, axis=1).astype(jnp.bfloat16)
     for i in range(responses):
-        resp_out[0, i] = total[i * length : (i + 1) * length]
-    prompt_out[0] = total[rows_r:]
+        resp_out[0, i] = rows[i * length : (i + 1) * length]
+    each = 2 * rows_r // rows_p
+    rows = [scratch[i, pl.ds(q, rows_p, stride=each), :] for q in range(each) for i in range(half, lanes)]
+    prompt_out[0] = jnp.concatenate(rows, axis=1).astype(jnp.bfloat16)
 
 
 def body(
@@ -309,7 +344,9 @@
     count = len(all_r)
     rows = count * (line_r.shape[0] + 2 * prompts)
     tokens = rows // 2
-    half = tokens // 2
+    packed = small and 2 * rows_r % rows_p == 0 and (2 * rows_r // rows_p) % 2 == 0
+    each, columns = (2 * rows_r, width // 2 + extra) if packed else (rows_r + rows_p, width)
+    half = n_resp * chips * each
     kept = pltpu.VMEM if small else jax.ShapeDtypeStruct
     taken = [*all_r, *all_p, *weights]
     if small:
@@ -317,8 +354,8 @@
     near, far, values, gate_grad, upward_grad, hidden = pl.pallas_call(
         functools.partial(expert_kernel, count, (rows_r, rows_p), experts),
         out_shape=[
-            kept((half, width), bf16),
-            kept((half, width), bf16),
+            kept((half, columns), bf16),
+            kept((half, columns), bf16),
             kept((rows, width), bf16),
         ]
         + [kept((rows, hidden_units), bf16)] * 3,
@@ -326,6 +363,7 @@
         out_specs=[VMEM] * 6,
         compiler_params=params(24 if small else 60),
         cost_estimate=pl.CostEstimate(flops=10 * rows * width * hidden_units, bytes_accessed=20 * 2**20, transcendentals=0),
+        scratch_shapes=[pltpu.VMEM((columns // LANES, 2 * half, LANES), jnp.float32)] if packed else [],
         name="expert",
     )(*taken)
 
@@ -337,13 +375,13 @@
     for j in range(1, chips):
         line = line + along("expert", n_expert, -2 * j)(total[j * block : (j + 1) * block]).astype(jnp.float32)
     line = line.astype(bf16)
-    each = rows_r + rows_p
     own = [line[:each]] + [across(line[k * each : (k + 1) * each], n_resp, k) for k in range(1, n_resp)]
     grad_prompt, grad_resp = pl.pallas_call(
-        functools.partial(finish_kernel, rows_r),
+        functools.partial(finish_kernel, rows_r, rows_p),
         out_shape=[jax.ShapeDtypeStruct(x_prompt.shape, bf16), jax.ShapeDtypeStruct(x_resp.shape, bf16)],
         in_specs=[VMEM] * n_resp,
         out_specs=[VMEM] * 2,
+        scratch_shapes=[pltpu.VMEM((columns // LANES, each, LANES), jnp.float32)],
         compiler_params=params(8),
         name="finish",
     )(*own)

time: 50 us -> 49.4 us (0.988)
  waiting for transfers between devices: 13.6 us -> 13 us
    ppermute x7, waiting for transfers between devices: 4.67 us -> 4.03 us  [across(): return lax.ppermute(value, 'resp', [(i, i ^ by) for i in range(size)])]
  transfers between devices with their start and end apart: 15 -> 15, of which waited for: 8 -> 7; matrix products, arithmetic and copies ran while one was open for 0% -> 0% of each run, Pallas kernels for 20% -> 21%
where the time goes in v4:
time: 49.4 us; the launch traced here: 49.1 us
  starting transfers between devices  18.3 us (37%)
  Pallas kernels  16.8 us (34%)
  waiting for transfers between devices  13 us (26%)
  between operations  0.76 us (2%)
    ppermute x7, starting transfers between devices, across(): return lax.ppermute(value, 'resp', [(i, i ^ by) for i in range(size)])  13 us
    pallas_call x3, Pallas kernels, outer(): pl.pallas_call(outer_kernel, out_shape=(pltpu.HBM if small else jax.Shape...  6.41 us
    ppermute x3, waiting for transfers between devices, along(): lax.ppermute(value, axis, [(i, (i + by) % size) for i in range(size)])  6.08 us
    pallas_call x1, Pallas kernels, body(): pl.pallas_call(functools.partial(expert_kernel, count, (rows_r, rows_p),...  4.94 us
    ppermute x3, starting transfers between devices, along(): lax.ppermute(value, axis, [(i, (i + by) % size) for i in range(size)])  4.54 us
    ppermute x7, waiting for transfers between devices, across(): return lax.ppermute(value, 'resp', [(i, i ^ by) for i in range(size)])  4.03 us
    pallas_call x1, Pallas kernels, body(): pl.pallas_call(load_kernel, out_shape=[pltpu.VMEM(w.shape, w.dtype) for w...  3.78 us
    ppermute x5, waiting for transfers between devices, other_core(): return lax.ppermute(value, 'expert', [(i, i ^ 1) for i in range(size)])  2.9 us
  transfers between devices with their start and end apart: 15, of which 7 were waited for; matrix products, arithmetic and copies ran while one was open for 0% of the time, Pallas kernels for 21%

profile of v4, /device:TPU:0, one launch (start us, length us, event | category | flops | bytes accessed | tf_op | source)
XLA Modules:
  0.0 49.1 jit_solution(6241431524361260400)
XLA Ops:
  0.6 1.0 %prepare.1 = (bf16[8,5248]{1,0:T(8,128)(2,1)S(1)}, bf16[8,4096]{1,0:T(8,128)(2,1)S(1)}) custom-call(bf16[1,2,4096]{2,1,0:T(2,128)(2,1)} %refs_0_.2, bf16[1,1,4,4096]{3,2,1,0:T(4,128)(2,1)} %refs_1_.2, bf16[1,1,8,4096]{3,2,1,0:T(8,128)(2,1)} %refs_2_.2, bf16[1,1,4,4096]{3,2,1,0:T(4,128)(2,1)} %refs_3_.1, s32[1,2,2]{2,1,0:T(2,128)} %refs_4_.1, ...), custom_call_target="tpu_custom_call" | custom-call | tf_op jit(solution)/shard_map/prepare/pallas_call | solution.py:295
  1.7 3.1 %collective-permute-start = (bf16[8,9344]{1,0:T(8,128)(2,1)S(1)}, bf16[8,9344]{1,0:T(8,128)(2,1)S(1)}, u32[]{:S(2)}, u32[]{:S(2)}) collective-permute-start(bf16[8,9344]{1,0:T(8,128)(2,1)S(1)} %pad_maximum_fusion.1), channel_id=1, source_target_pairs={{0,4},{4,0},{8,12},{12,8},{1,5},{5,1},{9,13},{13,9},{2,6},{6,2},{1... | collective-permute-start | bytes 448520 | tf_op jit(solution)/shard_map/ppermute | solution.py:37
  4.8 2.5 %collective-permute-start.2 = (bf16[8,5248]{1,0:T(8,128)(2,1)S(1)}, bf16[8,5248]{1,0:T(8,128)(2,1)S(1)}, u32[]{:S(2)}, u32[]{:S(2)}) collective-permute-start(bf16[8,5248]{1,0:T(8,128)(2,1)S(1)} %get-tuple-element.29), channel_id=1, source_target_pairs={{0,12},{4,8},{8,4},{12,0},{1,13},{5,9},{9,5},{13,1},{2,14},{6,10},... | collective-permute-start | bytes 251912 | tf_op jit(solution)/shard_map/ppermute | solution.py:37
  7.3 0.1 collective-permute-start.1
  7.4 3.8 %load.1 = (bf16[1,384,4096]{2,1,0:T(8,128)(2,1)S(1)}, bf16[1,384,4096]{2,1,0:T(8,128)(2,1)S(1)}, bf16[1,384,4096]{2,1,0:T(8,128)(2,1)S(1)}) custom-call(bf16[1,384,4096]{2,1,0:T(8,128)(2,1)} %refs_0_.3, bf16[1,384,4096]{2,1,0:T(8,128)(2,1)} %refs_1_.3, bf16[1,384,4096]{2,1,0:T(8,128)(2,1)} %refs_2_.3), custom_call_target="tpu_custom_call" | custom-call | bytes 9437184 | tf_op jit(solution)/shard_map/load/pallas_call | solution.py:313
  11.2 0.0 collective-permute-done
  11.2 2.9 %collective-permute-start.4 = (bf16[8,4096]{1,0:T(8,128)(2,1)S(1)}, bf16[8,4096]{1,0:T(8,128)(2,1)S(1)}, u32[]{:S(2)}, u32[]{:S(2)}) collective-permute-start(bf16[8,4096]{1,0:T(8,128)(2,1)S(1)} %add_convert_fusion.3), channel_id=1, source_target_pairs={{0,8},{4,12},{8,0},{12,4},{1,9},{5,13},{9,1},{13,5},{2,10},{6,14},... | collective-permute-start | bytes 196616 | tf_op jit(solution)/shard_map/ppermute | solution.py:37
  14.1 0.0 collective-permute-done.2
  14.1 2.6 %collective-permute-done.1 = bf16[8,5248]{1,0:T(8,128)(2,1)S(1)} collective-permute-done((bf16[8,5248]{1,0:T(8,128)(2,1)S(1)}, bf16[8,5248]{1,0:T(8,128)(2,1)S(1)}, u32[]{:S(2)}, u32[]{:S(2)}) %collective-permute-start.1) | collective-permute-done | bytes 84000 | tf_op jit(solution)/shard_map/ppermute | solution.py:37
  16.7 1.6 %collective-permute-start.3 = (bf16[32,5248]{1,0:T(8,128)(2,1)S(1)}, bf16[32,5248]{1,0:T(8,128)(2,1)S(1)}, u32[]{:S(2)}, u32[]{:S(2)}) collective-permute-start(bf16[32,5248]{1,0:T(8,128)(2,1)S(1)} %pad_maximum_fusion.refs_0_), channel_id=1, source_target_pairs={{0,2},{1,3},{2,0},{3,1},{4,6},{5,7},{6,4},{7,5},{8,10},{9,11},{10,... | collective-permute-start | bytes 1007624 | tf_op jit(solution)/shard_map/ppermute | solution.py:33
  18.3 0.0 collective-permute-done.4
  18.3 1.4 %collective-permute-start.5 = (bf16[8,4096]{1,0:T(8,128)(2,1)S(1)}, bf16[8,4096]{1,0:T(8,128)(2,1)S(1)}, u32[]{:S(2)}, u32[]{:S(2)}) collective-permute-start(bf16[8,4096]{1,0:T(8,128)(2,1)S(1)} %add_convert_fusion.2.refs_4_), channel_id=1, source_target_pairs={{0,2},{1,3},{2,0},{3,1},{4,6},{5,7},{6,4},{7,5},{8,10},{9,11},{10,... | collective-permute-start | bytes 196616 | tf_op jit(solution)/shard_map/ppermute | solution.py:33
  19.7 0.0 collective-permute-start.6
  19.7 4.9 %collective-permute-done.5.refs_5_ = bf16[8,4096]{1,0:T(8,128)(2,1)S(1)} collective-permute-done((bf16[8,4096]{1,0:T(8,128)(2,1)S(1)}, bf16[8,4096]{1,0:T(8,128)(2,1)S(1)}, u32[]{:S(2)}, u32[]{:S(2)}) %collective-permute-start.5) | collective-permute-done | bytes 65568 | tf_op jit(solution)/shard_map/ppermute | solution.py:33
  24.6 0.0 collective-permute-done.3.refs_1_
  24.6 0.0 collective-permute-start.7
  24.6 0.5 %collective-permute-start.8 = (bf16[8,4096]{1,0:T(8,128)(2,1)S(1)}, bf16[8,4096]{1,0:T(8,128)(2,1)S(1)}, u32[]{:S(2)}, u32[]{:S(2)}) collective-permute-start(bf16[8,4096]{1,0:T(8,128)(2,1)S(1)} %add_convert_fusion.2.refs_4_), channel_id=1, source_target_pairs={{0,1},{1,0},{2,3},{3,2},{4,5},{5,4},{6,7},{7,6},{8,9},{9,8},{10,11... | collective-permute-start | bytes 196616 | tf_op jit(solution)/shard_map/ppermute | solution.py:41
  25.2 0.0 collective-permute-start.9
  25.2 1.2 %collective-permute-done.8.refs_6_ = bf16[8,4096]{1,0:T(8,128)(2,1)S(1)} collective-permute-done((bf16[8,4096]{1,0:T(8,128)(2,1)S(1)}, bf16[8,4096]{1,0:T(8,128)(2,1)S(1)}, u32[]{:S(2)}, u32[]{:S(2)}) %collective-permute-start.8) | collective-permute-done | bytes 65568 | tf_op jit(solution)/shard_map/ppermute | solution.py:41
  26.4 0.0 collective-permute-done.6.refs_2_
  26.4 0.1 collective-permute-done.9.refs_7_
  26.5 0.0 collective-permute-done.7.refs_3_
  26.5 4.9 %expert.1 = (bf16[64,3072]{1,0:T(8,128)(2,1)S(1)}, bf16[64,3072]{1,0:T(8,128)(2,1)S(1)}, bf16[192,4096]{1,0:T(8,128)(2,1)S(1)}, bf16[192,384]{1,0:T(8,128)(2,1)S...) custom-call(bf16[32,5248]{1,0:T(8,128)(2,1)S(1)} %pad_maximum_fusion.refs_0_, ...), custom_call_target="tpu_custom_call" | custom-call | flops 3019898880 | bytes 20971520 | tf_op jit(solution)/shard_map/expert/pallas_call | solution.py:354
  31.4 0.2 collective-permute-start.10
  31.6 1.6 %collective-permute-done.10 = bf16[64,3072]{1,0:T(8,128)(2,1)S(1)} collective-permute-done((bf16[64,3072]{1,0:T(8,128)(2,1)S(1)}, bf16[64,3072]{1,0:T(8,128)(2,1)S(1)}, u32[]{:S(2)}, u32[]{:S(2)}) %collective-permute-start.10) | collective-permute-done | bytes 393248 | tf_op jit(solution)/shard_map/ppermute | solution.py:41
  33.2 0.1 add_convert_fusion
  33.3 1.6 %collective-permute-start.11 = (bf16[32,3072]{1,0:T(8,128)(2,1)S(1)}, bf16[32,3072]{1,0:T(8,128)(2,1)S(1)}, u32[]{:S(2)}, u32[]{:S(2)}) collective-permute-start(bf16[32,3072]{1,0:T(8,128)(2,1)S(1)} %slice.27), channel_id=1, source_target_pairs={{0,2},{1,3},{2,0},{3,1},{4,6},{5,7},{6,4},{7,5},{8,10},{9,11},{10,... | collective-permute-start | bytes 589832 | tf_op jit(solution)/shard_map/ppermute | solution.py:33
  34.9 2.1 %outer.3 = bf16[1,384,4096]{2,1,0:T(8,128)(2,1)} custom-call(bf16[192,384]{1,0:T(8,128)(2,1)S(1)} %get-tuple-element.49.left, bf16[192,4096]{1,0:T(8,128)(2,1)S(1)} %get-tuple-element.50.values), custom_call_target="tpu_custom_call" | custom-call | flops 603979776 | bytes 3145728 | tf_op jit(solution)/shard_map/outer/pallas_call | solution.py:225
  37.1 2.1 %outer.4 = bf16[1,384,4096]{2,1,0:T(8,128)(2,1)} custom-call(bf16[192,384]{1,0:T(8,128)(2,1)S(1)} %get-tuple-element.51.left, bf16[192,4096]{1,0:T(8,128)(2,1)S(1)} %get-tuple-element.50.values), custom_call_target="tpu_custom_call" | custom-call | flops 603979776 | bytes 3145728 | tf_op jit(solution)/shard_map/outer/pallas_call | solution.py:225
  39.2 1.1 %collective-permute-done.11 = bf16[32,3072]{1,0:T(8,128)(2,1)S(1)} collective-permute-done((bf16[32,3072]{1,0:T(8,128)(2,1)S(1)}, bf16[32,3072]{1,0:T(8,128)(2,1)S(1)}, u32[]{:S(2)}, u32[]{:S(2)}) %collective-permute-start.11) | collective-permute-done | bytes 196640 | tf_op jit(solution)/shard_map/ppermute | solution.py:33
  40.4 3.0 %collective-permute-start.14 = (bf16[8,3072]{1,0:T(8,128)(2,1)S(1)}, bf16[8,3072]{1,0:T(8,128)(2,1)S(1)}, u32[]{:S(2)}, u32[]{:S(2)}) collective-permute-start(bf16[8,3072]{1,0:T(8,128)(2,1)S(1)} %get-tuple-element.53), channel_id=1, source_target_pairs={{0,12},{4,8},{8,4},{12,0},{1,13},{5,9},{9,5},{13,1},{2,14},{6,10},... | collective-permute-start | bytes 147464 | tf_op jit(solution)/shard_map/ppermute | solution.py:37
  43.4 0.0 collective-permute-start.13
  43.4 1.5 %collective-permute-start.12 = (bf16[8,3072]{1,0:T(8,128)(2,1)S(1)}, bf16[8,3072]{1,0:T(8,128)(2,1)S(1)}, u32[]{:S(2)}, u32[]{:S(2)}) collective-permute-start(bf16[8,3072]{1,0:T(8,128)(2,1)S(1)} %get-tuple-element.55), channel_id=1, source_target_pairs={{0,4},{4,0},{8,12},{12,8},{1,5},{5,1},{9,13},{13,9},{2,6},{6,2},{1... | collective-permute-start | bytes 147464 | tf_op jit(solution)/shard_map/ppermute | solution.py:37
  44.9 2.1 %outer.5 = bf16[1,384,4096]{2,1,0:T(8,128)(2,1)} custom-call(bf16[192,384]{1,0:T(8,128)(2,1)S(1)} %get-tuple-element.52.left, bf16[192,4096]{1,0:T(8,128)(2,1)S(1)} %get-tuple-element.50.values), custom_call_target="tpu_custom_call" | custom-call | flops 603979776 | bytes 3145728 | tf_op jit(solution)/shard_map/outer/pallas_call | solution.py:225
  47.0 0.0 collective-permute-done.14.refs_3_
  47.0 1.4 %collective-permute-done.13.refs_2_ = bf16[8,3072]{1,0:T(8,128)(2,1)S(1)} collective-permute-done((bf16[8,3072]{1,0:T(8,128)(2,1)S(1)}, bf16[8,3072]{1,0:T(8,128)(2,1)S(1)}, u32[]{:S(2)}, u32[]{:S(2)}) %collective-permute-start.13) | collective-permute-done | bytes 49184 | tf_op jit(solution)/shard_map/ppermute | solution.py:37
  48.5 0.0 collective-permute-done.12.refs_1_
  48.5 0.7 %finish.1 = (bf16[1,2,4096]{2,1,0:T(2,128)(2,1)}, bf16[1,1,4,4096]{3,2,1,0:T(4,128)(2,1)}) custom-call(bf16[8,3072]{1,0:T(8,128)(2,1)S(1)} %get-tuple-element.56.refs_0_, bf16[8,3072]{1,0:T(8,128)(2,1)S(1)} %collective-permute-done.12.refs_1_, bf16[8,3072]{1,0:T(8,128)(2,1)S(1)} %collective-permute-done.13.refs_2_, ...), custom_call_target="tpu_custom_call" | custom-call | tf_op jit(solution)/shard_map/finish/pallas_call | solution.py:379
  (8 shorter events, 0.2 us)
Async XLA Ops:
  1.7 9.5 %collective-permute-start = (bf16[8,9344]{1,0:T(8,128)(2,1)S(1)}, bf16[8,9344]{1,0:T(8,128)(2,1)S(1)}, u32[]{:S(2)}, u32[]{:S(2)}) collective-permute-start(bf16[8,9344]{1,0:T(8,128)(2,1)S(1)} %pad_maximum_fusion.1), channel_id=1, source_target_pairs={{0,4},{4,0},{8,12},{12,8},{1,5},{5,1},{9,13},{13,9},{2,6},{6,2},{1... | collective-permute-start | bytes 448520 | tf_op jit(solution)/shard_map/ppermute | solution.py:37
  4.8 9.3 %collective-permute-start.2 = (bf16[8,5248]{1,0:T(8,128)(2,1)S(1)}, bf16[8,5248]{1,0:T(8,128)(2,1)S(1)}, u32[]{:S(2)}, u32[]{:S(2)}) collective-permute-start(bf16[8,5248]{1,0:T(8,128)(2,1)S(1)} %get-tuple-element.29), channel_id=1, source_target_pairs={{0,12},{4,8},{8,4},{12,0},{1,13},{5,9},{9,5},{13,1},{2,14},{6,10},... | collective-permute-start | bytes 251912 | tf_op jit(solution)/shard_map/ppermute | solution.py:37
  7.3 9.4 %collective-permute-start.1 = (bf16[8,5248]{1,0:T(8,128)(2,1)S(1)}, bf16[8,5248]{1,0:T(8,128)(2,1)S(1)}, u32[]{:S(2)}, u32[]{:S(2)}) collective-permute-start(bf16[8,5248]{1,0:T(8,128)(2,1)S(1)} %get-tuple-element.29), channel_id=1, source_target_pairs={{0,8},{4,12},{8,0},{12,4},{1,9},{5,13},{9,1},{13,5},{2,10},{6,14},... | collective-permute-start | bytes 251912 | tf_op jit(solution)/shard_map/ppermute | solution.py:37
  11.2 7.1 %collective-permute-start.4 = (bf16[8,4096]{1,0:T(8,128)(2,1)S(1)}, bf16[8,4096]{1,0:T(8,128)(2,1)S(1)}, u32[]{:S(2)}, u32[]{:S(2)}) collective-permute-start(bf16[8,4096]{1,0:T(8,128)(2,1)S(1)} %add_convert_fusion.3), channel_id=1, source_target_pairs={{0,8},{4,12},{8,0},{12,4},{1,9},{5,13},{9,1},{13,5},{2,10},{6,14},... | collective-permute-start | bytes 196616 | tf_op jit(solution)/shard_map/ppermute | solution.py:37
  16.7 7.9 %collective-permute-start.3 = (bf16[32,5248]{1,0:T(8,128)(2,1)S(1)}, bf16[32,5248]{1,0:T(8,128)(2,1)S(1)}, u32[]{:S(2)}, u32[]{:S(2)}) collective-permute-start(bf16[32,5248]{1,0:T(8,128)(2,1)S(1)} %pad_maximum_fusion.refs_0_), channel_id=1, source_target_pairs={{0,2},{1,3},{2,0},{3,1},{4,6},{5,7},{6,4},{7,5},{8,10},{9,11},{10,... | collective-permute-start | bytes 1007624 | tf_op jit(solution)/shard_map/ppermute | solution.py:33
  18.3 6.3 %collective-permute-start.5 = (bf16[8,4096]{1,0:T(8,128)(2,1)S(1)}, bf16[8,4096]{1,0:T(8,128)(2,1)S(1)}, u32[]{:S(2)}, u32[]{:S(2)}) collective-permute-start(bf16[8,4096]{1,0:T(8,128)(2,1)S(1)} %add_convert_fusion.2.refs_4_), channel_id=1, source_target_pairs={{0,2},{1,3},{2,0},{3,1},{4,6},{5,7},{6,4},{7,5},{8,10},{9,11},{10,... | collective-permute-start | bytes 196616 | tf_op jit(solution)/shard_map/ppermute | solution.py:33
  19.7 6.7 %collective-permute-start.6 = (bf16[32,5248]{1,0:T(8,128)(2,1)S(1)}, bf16[32,5248]{1,0:T(8,128)(2,1)S(1)}, u32[]{:S(2)}, u32[]{:S(2)}) collective-permute-start(bf16[32,5248]{1,0:T(8,128)(2,1)S(1)} %pad_maximum_fusion.refs_0_), channel_id=1, source_target_pairs={{0,1},{1,0},{2,3},{3,2},{4,5},{5,4},{6,7},{7,6},{8,9},{9,8},{10,11... | collective-permute-start | bytes 1007624 | tf_op jit(solution)/shard_map/ppermute | solution.py:41
  24.6 1.8 %collective-permute-start.7 = (bf16[32,5248]{1,0:T(8,128)(2,1)S(1)}, bf16[32,5248]{1,0:T(8,128)(2,1)S(1)}, u32[]{:S(2)}, u32[]{:S(2)}) collective-permute-start(bf16[32,5248]{1,0:T(8,128)(2,1)S(1)} %collective-permute-done.3.refs_1_), channel_id=1, source_target_pairs={{0,1},{1,0},{2,3},{3,2},{4,5},{5,4},{6,7},{7,6},{8,9},{9,8},{10,11... | collective-permute-start | bytes 1007624 | tf_op jit(solution)/shard_map/ppermute | solution.py:41
  24.6 1.7 %collective-permute-start.8 = (bf16[8,4096]{1,0:T(8,128)(2,1)S(1)}, bf16[8,4096]{1,0:T(8,128)(2,1)S(1)}, u32[]{:S(2)}, u32[]{:S(2)}) collective-permute-start(bf16[8,4096]{1,0:T(8,128)(2,1)S(1)} %add_convert_fusion.2.refs_4_), channel_id=1, source_target_pairs={{0,1},{1,0},{2,3},{3,2},{4,5},{5,4},{6,7},{7,6},{8,9},{9,8},{10,11... | collective-permute-start | bytes 196616 | tf_op jit(solution)/shard_map/ppermute | solution.py:41
  25.2 1.3 %collective-permute-start.9 = (bf16[8,4096]{1,0:T(8,128)(2,1)S(1)}, bf16[8,4096]{1,0:T(8,128)(2,1)S(1)}, u32[]{:S(2)}, u32[]{:S(2)}) collective-permute-start(bf16[8,4096]{1,0:T(8,128)(2,1)S(1)} %collective-permute-done.5.refs_5_), channel_id=1, source_target_pairs={{0,1},{1,0},{2,3},{3,2},{4,5},{5,4},{6,7},{7,6},{8,9},{9,8},{10,11... | collective-permute-start | bytes 196616 | tf_op jit(solution)/shard_map/ppermute | solution.py:41
  31.4 1.8 %collective-permute-start.10 = (bf16[64,3072]{1,0:T(8,128)(2,1)S(1)}, bf16[64,3072]{1,0:T(8,128)(2,1)S(1)}, u32[]{:S(2)}, u32[]{:S(2)}) collective-permute-start(bf16[64,3072]{1,0:T(8,128)(2,1)S(1)} %get-tuple-element.41), channel_id=1, source_target_pairs={{0,1},{1,0},{2,3},{3,2},{4,5},{5,4},{6,7},{7,6},{8,9},{9,8},{10,11... | collective-permute-start | bytes 1179656 | tf_op jit(solution)/shard_map/ppermute | solution.py:41
  33.3 7.0 %collective-permute-start.11 = (bf16[32,3072]{1,0:T(8,128)(2,1)S(1)}, bf16[32,3072]{1,0:T(8,128)(2,1)S(1)}, u32[]{:S(2)}, u32[]{:S(2)}) collective-permute-start(bf16[32,3072]{1,0:T(8,128)(2,1)S(1)} %slice.27), channel_id=1, source_target_pairs={{0,2},{1,3},{2,0},{3,1},{4,6},{5,7},{6,4},{7,5},{8,10},{9,11},{10,... | collective-permute-start | bytes 589832 | tf_op jit(solution)/shard_map/ppermute | solution.py:33
  40.4 6.6 %collective-permute-start.14 = (bf16[8,3072]{1,0:T(8,128)(2,1)S(1)}, bf16[8,3072]{1,0:T(8,128)(2,1)S(1)}, u32[]{:S(2)}, u32[]{:S(2)}) collective-permute-start(bf16[8,3072]{1,0:T(8,128)(2,1)S(1)} %get-tuple-element.53), channel_id=1, source_target_pairs={{0,12},{4,8},{8,4},{12,0},{1,13},{5,9},{9,5},{13,1},{2,14},{6,10},... | collective-permute-start | bytes 147464 | tf_op jit(solution)/shard_map/ppermute | solution.py:37
  43.4 5.0 %collective-permute-start.13 = (bf16[8,3072]{1,0:T(8,128)(2,1)S(1)}, bf16[8,3072]{1,0:T(8,128)(2,1)S(1)}, u32[]{:S(2)}, u32[]{:S(2)}) collective-permute-start(bf16[8,3072]{1,0:T(8,128)(2,1)S(1)} %get-tuple-element.54), channel_id=1, source_target_pairs={{0,8},{4,12},{8,0},{12,4},{1,9},{5,13},{9,1},{13,5},{2,10},{6,14},... | collective-permute-start | bytes 147464 | tf_op jit(solution)/shard_map/ppermute | solution.py:37
  43.4 5.0 %collective-permute-start.12 = (bf16[8,3072]{1,0:T(8,128)(2,1)S(1)}, bf16[8,3072]{1,0:T(8,128)(2,1)S(1)}, u32[]{:S(2)}, u32[]{:S(2)}) collective-permute-start(bf16[8,3072]{1,0:T(8,128)(2,1)S(1)} %get-tuple-element.55), channel_id=1, source_target_pairs={{0,4},{4,0},{8,12},{12,8},{1,5},{5,1},{9,13},{13,9},{2,6},{6,2},{1... | collective-permute-start | bytes 147464 | tf_op jit(solution)/shard_map/ppermute | solution.py:37

commit v5 on v4

--- a/solution.py
+++ b/solution.py
@@ -203,37 +203,44 @@
         copy.wait()
 
 
-def outer_kernel(left, values, out, turned, buffer, sent):
-    turned[...] = left[...].astype(jnp.float32).T.astype(jnp.bfloat16)
-    steps = sent.shape[0]
+def outer_kernel(*refs):
+    count = (len(refs) - 4) // 2
+    lefts, values, outs = refs[:count], refs[count], refs[count + 1 : 2 * count + 1]
+    turned, buffer, sent = refs[2 * count + 1 :]
+    steps = sent.shape[1]
     step = values.shape[1] // steps
     copies = []
-    for c in range(steps):
-        block = jnp.dot(turned[...], values[:, c * step : (c + 1) * step], preferred_element_type=jnp.float32)
-        buffer[c] = block.astype(jnp.bfloat16)
-        copies.append(pltpu.make_async_copy(buffer.at[c], out.at[0, :, pl.ds(c * step, step)], sent.at[c]))
-        copies[-1].start()
+    for i, (left, out) in enumerate(zip(lefts, outs, strict=True)):
+        turned[i] = left[...].astype(jnp.float32).T.astype(jnp.bfloat16)
+        for c in range(steps):
+            block = jnp.dot(turned[i], values[:, c * step : (c + 1) * step], preferred_element_type=jnp.float32)
+            buffer[i, c] = block.astype(jnp.bfloat16)
+            copies.append(pltpu.make_async_copy(buffer.at[i, c], out.at[0, :, pl.ds(c * step, step)], sent.at[i, c]))
+            copies[-1].start()
     for copy in copies:
         copy.wait()
 
 
-def outer(left, values, small):
-    rows, units = left.shape
+def outer(lefts, values, small):
+    rows, units = lefts[0].shape
     width = values.shape[1]
+    count = len(lefts)
     steps = 4 if width % 512 == 0 else 1
-    given = [held(a, pltpu.VMEM) for a in (left, values)] if small else [left, values]
+    given = [held(a, pltpu.VMEM) for a in (*lefts, values)] if small else [*lefts, values]
     return pl.pallas_call(
         outer_kernel,
-        out_shape=(pltpu.HBM if small else jax.ShapeDtypeStruct)((1, units, width), jnp.bfloat16),
-        in_specs=[VMEM] * 2,
-        out_specs=HBM,
+        out_shape=[(pltpu.HBM if small else jax.ShapeDtypeStruct)((1, units, width), jnp.bfloat16)] * count,
+        in_specs=[VMEM] * (count + 1),
+        out_specs=[HBM] * count,
         scratch_shapes=[
-            pltpu.VMEM((units, rows), jnp.bfloat16),
-            pltpu.VMEM((steps, units, width // steps), jnp.bfloat16),
-            pltpu.SemaphoreType.DMA((steps,)),
+            pltpu.VMEM((count, units, rows), jnp.bfloat16),
+            pltpu.VMEM((count, steps, units, width // steps), jnp.bfloat16),
+            pltpu.SemaphoreType.DMA((count, steps)),
         ],
         compiler_params=params(24 if small else 60),
-        cost_estimate=pl.CostEstimate(flops=2 * rows * units * width, bytes_accessed=2 * units * width, transcendentals=0),
+        cost_estimate=pl.CostEstimate(
+            flops=2 * count * rows * units * width, bytes_accessed=2 * count * units * width, transcendentals=0
+        ),
         name="outer",
     )(*given)
 
@@ -385,9 +392,8 @@
         compiler_params=params(8),
         name="finish",
     )(*own)
-    grad_gate = outer(gate_grad, values, small)
-    grad_up = outer(upward_grad, values, small)
-    grad_down = outer(hidden, values, small)
+    grad_gate, grad_up = outer([gate_grad, upward_grad], values, small)
+    (grad_down,) = outer([hidden], values, small)
     return (grad_prompt, grad_resp, grad_gate, grad_up, grad_down)
 
 

time: 49.4 us -> 49.4 us (level)
  Pallas kernels: 16.8 us -> 15.7 us
  waiting for transfers between devices: 13 us -> 14.1 us
    ppermute x3, waiting for transfers between devices: 6.08 us -> 7.18 us  [along(): lax.ppermute(value, axis, [(i, (i + by) % size) for i in range(size)])]
    pallas_call x3 -> x2, Pallas kernels: 6.41 us -> 5.32 us  [outer(): pl.pallas_call(outer_kernel, out_shape=[(pltpu.HBM if small else jax.Shap...]
  transfers between devices with their start and end apart: 15 -> 15, of which waited for: 7 -> 7; matrix products, arithmetic and copies ran while one was open for 0% -> 0% of each run, Pallas kernels for 21% -> 19%
where the time goes in v5:
time: 49.4 us; the launch traced here: 49.1 us
  starting transfers between devices  18.3 us (37%)
  Pallas kernels  15.7 us (32%)
  waiting for transfers between devices  14.1 us (29%)
  between operations  0.75 us (2%)
    ppermute x7, starting transfers between devices, across(): return lax.ppermute(value, 'resp', [(i, i ^ by) for i in range(size)])  13 us
    ppermute x3, waiting for transfers between devices, along(): lax.ppermute(value, axis, [(i, (i + by) % size) for i in range(size)])  7.18 us
    pallas_call x2, Pallas kernels, outer(): pl.pallas_call(outer_kernel, out_shape=[(pltpu.HBM if small else jax.Shap...  5.32 us
    pallas_call x1, Pallas kernels, body(): pl.pallas_call(functools.partial(expert_kernel, count, (rows_r, rows_p),...  4.94 us
    ppermute x3, starting transfers between devices, along(): lax.ppermute(value, axis, [(i, (i + by) % size) for i in range(size)])  4.54 us
    ppermute x7, waiting for transfers between devices, across(): return lax.ppermute(value, 'resp', [(i, i ^ by) for i in range(size)])  4.03 us
    pallas_call x1, Pallas kernels, body(): pl.pallas_call(load_kernel, out_shape=[pltpu.VMEM(w.shape, w.dtype) for w...  3.78 us
    ppermute x5, waiting for transfers between devices, other_core(): return lax.ppermute(value, 'expert', [(i, i ^ 1) for i in range(size)])  2.9 us
  transfers between devices with their start and end apart: 15, of which 7 were waited for; matrix products, arithmetic and copies ran while one was open for 0% of the time, Pallas kernels for 19%

profile of v5, /device:TPU:0, one launch (start us, length us, event | category | flops | bytes accessed | tf_op | source)
XLA Modules:
  0.0 49.1 jit_solution(17235157294541286251)
XLA Ops:
  0.6 1.0 %prepare.1 = (bf16[8,5248]{1,0:T(8,128)(2,1)S(1)}, bf16[8,4096]{1,0:T(8,128)(2,1)S(1)}) custom-call(bf16[1,2,4096]{2,1,0:T(2,128)(2,1)} %refs_0_.2, bf16[1,1,4,4096]{3,2,1,0:T(4,128)(2,1)} %refs_1_.2, bf16[1,1,8,4096]{3,2,1,0:T(8,128)(2,1)} %refs_2_.2, bf16[1,1,4,4096]{3,2,1,0:T(4,128)(2,1)} %refs_3_.1, s32[1,2,2]{2,1,0:T(2,128)} %refs_4_.1, ...), custom_call_target="tpu_custom_call" | custom-call | tf_op jit(solution)/shard_map/prepare/pallas_call | solution.py:302
  1.7 3.1 %collective-permute-start = (bf16[8,9344]{1,0:T(8,128)(2,1)S(1)}, bf16[8,9344]{1,0:T(8,128)(2,1)S(1)}, u32[]{:S(2)}, u32[]{:S(2)}) collective-permute-start(bf16[8,9344]{1,0:T(8,128)(2,1)S(1)} %pad_maximum_fusion.1), channel_id=1, source_target_pairs={{0,4},{4,0},{8,12},{12,8},{1,5},{5,1},{9,13},{13,9},{2,6},{6,2},{1... | collective-permute-start | bytes 448520 | tf_op jit(solution)/shard_map/ppermute | solution.py:37
  4.8 2.5 %collective-permute-start.2 = (bf16[8,5248]{1,0:T(8,128)(2,1)S(1)}, bf16[8,5248]{1,0:T(8,128)(2,1)S(1)}, u32[]{:S(2)}, u32[]{:S(2)}) collective-permute-start(bf16[8,5248]{1,0:T(8,128)(2,1)S(1)} %get-tuple-element.31), channel_id=1, source_target_pairs={{0,12},{4,8},{8,4},{12,0},{1,13},{5,9},{9,5},{13,1},{2,14},{6,10},... | collective-permute-start | bytes 251912 | tf_op jit(solution)/shard_map/ppermute | solution.py:37
  7.3 0.1 collective-permute-start.1
  7.4 3.8 %load.1 = (bf16[1,384,4096]{2,1,0:T(8,128)(2,1)S(1)}, bf16[1,384,4096]{2,1,0:T(8,128)(2,1)S(1)}, bf16[1,384,4096]{2,1,0:T(8,128)(2,1)S(1)}) custom-call(bf16[1,384,4096]{2,1,0:T(8,128)(2,1)} %refs_0_.3, bf16[1,384,4096]{2,1,0:T(8,128)(2,1)} %refs_1_.3, bf16[1,384,4096]{2,1,0:T(8,128)(2,1)} %refs_2_.3), custom_call_target="tpu_custom_call" | custom-call | bytes 9437184 | tf_op jit(solution)/shard_map/load/pallas_call | solution.py:320
  11.2 0.0 collective-permute-done
  11.2 2.9 %collective-permute-start.4 = (bf16[8,4096]{1,0:T(8,128)(2,1)S(1)}, bf16[8,4096]{1,0:T(8,128)(2,1)S(1)}, u32[]{:S(2)}, u32[]{:S(2)}) collective-permute-start(bf16[8,4096]{1,0:T(8,128)(2,1)S(1)} %add_convert_fusion.3), channel_id=1, source_target_pairs={{0,8},{4,12},{8,0},{12,4},{1,9},{5,13},{9,1},{13,5},{2,10},{6,14},... | collective-permute-start | bytes 196616 | tf_op jit(solution)/shard_map/ppermute | solution.py:37
  14.1 0.0 collective-permute-done.2
  14.1 2.6 %collective-permute-done.1 = bf16[8,5248]{1,0:T(8,128)(2,1)S(1)} collective-permute-done((bf16[8,5248]{1,0:T(8,128)(2,1)S(1)}, bf16[8,5248]{1,0:T(8,128)(2,1)S(1)}, u32[]{:S(2)}, u32[]{:S(2)}) %collective-permute-start.1) | collective-permute-done | bytes 84000 | tf_op jit(solution)/shard_map/ppermute | solution.py:37
  16.7 1.6 %collective-permute-start.3 = (bf16[32,5248]{1,0:T(8,128)(2,1)S(1)}, bf16[32,5248]{1,0:T(8,128)(2,1)S(1)}, u32[]{:S(2)}, u32[]{:S(2)}) collective-permute-start(bf16[32,5248]{1,0:T(8,128)(2,1)S(1)} %pad_maximum_fusion.refs_0_), channel_id=1, source_target_pairs={{0,2},{1,3},{2,0},{3,1},{4,6},{5,7},{6,4},{7,5},{8,10},{9,11},{10,... | collective-permute-start | bytes 1007624 | tf_op jit(solution)/shard_map/ppermute | solution.py:33
  18.3 0.0 collective-permute-done.4
  18.3 1.4 %collective-permute-start.5 = (bf16[8,4096]{1,0:T(8,128)(2,1)S(1)}, bf16[8,4096]{1,0:T(8,128)(2,1)S(1)}, u32[]{:S(2)}, u32[]{:S(2)}) collective-permute-start(bf16[8,4096]{1,0:T(8,128)(2,1)S(1)} %add_convert_fusion.2.refs_4_), channel_id=1, source_target_pairs={{0,2},{1,3},{2,0},{3,1},{4,6},{5,7},{6,4},{7,5},{8,10},{9,11},{10,... | collective-permute-start | bytes 196616 | tf_op jit(solution)/shard_map/ppermute | solution.py:33
  19.7 0.0 collective-permute-start.6
  19.7 4.9 %collective-permute-done.5.refs_5_ = bf16[8,4096]{1,0:T(8,128)(2,1)S(1)} collective-permute-done((bf16[8,4096]{1,0:T(8,128)(2,1)S(1)}, bf16[8,4096]{1,0:T(8,128)(2,1)S(1)}, u32[]{:S(2)}, u32[]{:S(2)}) %collective-permute-start.5) | collective-permute-done | bytes 65568 | tf_op jit(solution)/shard_map/ppermute | solution.py:33
  24.6 0.0 collective-permute-done.3.refs_1_
  24.6 0.0 collective-permute-start.7
  24.6 0.5 %collective-permute-start.8 = (bf16[8,4096]{1,0:T(8,128)(2,1)S(1)}, bf16[8,4096]{1,0:T(8,128)(2,1)S(1)}, u32[]{:S(2)}, u32[]{:S(2)}) collective-permute-start(bf16[8,4096]{1,0:T(8,128)(2,1)S(1)} %add_convert_fusion.2.refs_4_), channel_id=1, source_target_pairs={{0,1},{1,0},{2,3},{3,2},{4,5},{5,4},{6,7},{7,6},{8,9},{9,8},{10,11... | collective-permute-start | bytes 196616 | tf_op jit(solution)/shard_map/ppermute | solution.py:41
  25.2 0.0 collective-permute-start.9
  25.2 1.2 %collective-permute-done.8.refs_6_ = bf16[8,4096]{1,0:T(8,128)(2,1)S(1)} collective-permute-done((bf16[8,4096]{1,0:T(8,128)(2,1)S(1)}, bf16[8,4096]{1,0:T(8,128)(2,1)S(1)}, u32[]{:S(2)}, u32[]{:S(2)}) %collective-permute-start.8) | collective-permute-done | bytes 65568 | tf_op jit(solution)/shard_map/ppermute | solution.py:41
  26.4 0.0 collective-permute-done.6.refs_2_
  26.4 0.1 collective-permute-done.9.refs_7_
  26.5 0.0 collective-permute-done.7.refs_3_
  26.5 4.9 %expert.1 = (bf16[64,3072]{1,0:T(8,128)(2,1)S(1)}, bf16[64,3072]{1,0:T(8,128)(2,1)S(1)}, bf16[192,4096]{1,0:T(8,128)(2,1)S(1)}, bf16[192,384]{1,0:T(8,128)(2,1)S...) custom-call(bf16[32,5248]{1,0:T(8,128)(2,1)S(1)} %pad_maximum_fusion.refs_0_, ...), custom_call_target="tpu_custom_call" | custom-call | flops 3019898880 | bytes 20971520 | tf_op jit(solution)/shard_map/expert/pallas_call | solution.py:361
  31.4 0.2 collective-permute-start.10
  31.6 1.6 %collective-permute-done.10 = bf16[64,3072]{1,0:T(8,128)(2,1)S(1)} collective-permute-done((bf16[64,3072]{1,0:T(8,128)(2,1)S(1)}, bf16[64,3072]{1,0:T(8,128)(2,1)S(1)}, u32[]{:S(2)}, u32[]{:S(2)}) %collective-permute-start.10) | collective-permute-done | bytes 393248 | tf_op jit(solution)/shard_map/ppermute | solution.py:41
  33.2 0.1 add_convert_fusion
  33.3 1.6 %collective-permute-start.11 = (bf16[32,3072]{1,0:T(8,128)(2,1)S(1)}, bf16[32,3072]{1,0:T(8,128)(2,1)S(1)}, u32[]{:S(2)}, u32[]{:S(2)}) collective-permute-start(bf16[32,3072]{1,0:T(8,128)(2,1)S(1)} %slice.27), channel_id=1, source_target_pairs={{0,2},{1,3},{2,0},{3,1},{4,6},{5,7},{6,4},{7,5},{8,10},{9,11},{10,... | collective-permute-start | bytes 589832 | tf_op jit(solution)/shard_map/ppermute | solution.py:33
  34.9 3.2 %outer.2 = (bf16[1,384,4096]{2,1,0:T(8,128)(2,1)}, bf16[1,384,4096]{2,1,0:T(8,128)(2,1)}) custom-call(bf16[192,384]{1,0:T(8,128)(2,1)S(1)} %get-tuple-element.51.refs_0_, bf16[192,384]{1,0:T(8,128)(2,1)S(1)} %get-tuple-element.52.refs_1_, bf16[192,4096]{1,0:T(8,128)(2,1)S(1)} %get-tuple-element.53.refs_2_.refs_1_), custom_call_target="tpu_custom_call" | custom-call | flops 1207959552 | bytes 6291456 | tf_op jit(solution)/shard_map/outer/pallas_call | solution.py:230
  38.1 2.2 %collective-permute-done.11 = bf16[32,3072]{1,0:T(8,128)(2,1)S(1)} collective-permute-done((bf16[32,3072]{1,0:T(8,128)(2,1)S(1)}, bf16[32,3072]{1,0:T(8,128)(2,1)S(1)}, u32[]{:S(2)}, u32[]{:S(2)}) %collective-permute-start.11) | collective-permute-done | bytes 196640 | tf_op jit(solution)/shard_map/ppermute | solution.py:33
  40.4 3.0 %collective-permute-start.14 = (bf16[8,3072]{1,0:T(8,128)(2,1)S(1)}, bf16[8,3072]{1,0:T(8,128)(2,1)S(1)}, u32[]{:S(2)}, u32[]{:S(2)}) collective-permute-start(bf16[8,3072]{1,0:T(8,128)(2,1)S(1)} %get-tuple-element.57), channel_id=1, source_target_pairs={{0,12},{4,8},{8,4},{12,0},{1,13},{5,9},{9,5},{13,1},{2,14},{6,10},... | collective-permute-start | bytes 147464 | tf_op jit(solution)/shard_map/ppermute | solution.py:37
  43.4 0.0 collective-permute-start.13
  43.4 1.5 %collective-permute-start.12 = (bf16[8,3072]{1,0:T(8,128)(2,1)S(1)}, bf16[8,3072]{1,0:T(8,128)(2,1)S(1)}, u32[]{:S(2)}, u32[]{:S(2)}) collective-permute-start(bf16[8,3072]{1,0:T(8,128)(2,1)S(1)} %get-tuple-element.59), channel_id=1, source_target_pairs={{0,4},{4,0},{8,12},{12,8},{1,5},{5,1},{9,13},{13,9},{2,6},{6,2},{1... | collective-permute-start | bytes 147464 | tf_op jit(solution)/shard_map/ppermute | solution.py:37
  44.9 2.1 %outer.3 = bf16[1,384,4096]{2,1,0:T(8,128)(2,1)} custom-call(bf16[192,384]{1,0:T(8,128)(2,1)S(1)} %get-tuple-element.56.refs_0_, bf16[192,4096]{1,0:T(8,128)(2,1)S(1)} %get-tuple-element.53.refs_2_.refs_1_), custom_call_target="tpu_custom_call" | custom-call | flops 603979776 | bytes 3145728 | tf_op jit(solution)/shard_map/outer/pallas_call | solution.py:230
  47.0 0.0 collective-permute-done.14.refs_3_
  47.0 1.4 %collective-permute-done.13.refs_2_ = bf16[8,3072]{1,0:T(8,128)(2,1)S(1)} collective-permute-done((bf16[8,3072]{1,0:T(8,128)(2,1)S(1)}, bf16[8,3072]{1,0:T(8,128)(2,1)S(1)}, u32[]{:S(2)}, u32[]{:S(2)}) %collective-permute-start.13) | collective-permute-done | bytes 49184 | tf_op jit(solution)/shard_map/ppermute | solution.py:37
  48.5 0.0 collective-permute-done.12.refs_1_
  48.5 0.7 %finish.1 = (bf16[1,2,4096]{2,1,0:T(2,128)(2,1)}, bf16[1,1,4,4096]{3,2,1,0:T(4,128)(2,1)}) custom-call(bf16[8,3072]{1,0:T(8,128)(2,1)S(1)} %get-tuple-element.60.refs_0_, bf16[8,3072]{1,0:T(8,128)(2,1)S(1)} %collective-permute-done.12.refs_1_, bf16[8,3072]{1,0:T(8,128)(2,1)S(1)} %collective-permute-done.13.refs_2_, ...), custom_call_target="tpu_custom_call" | custom-call | tf_op jit(solution)/shard_map/finish/pallas_call | solution.py:386
  (8 shorter events, 0.2 us)
Async XLA Ops:
  1.7 9.5 %collective-permute-start = (bf16[8,9344]{1,0:T(8,128)(2,1)S(1)}, bf16[8,9344]{1,0:T(8,128)(2,1)S(1)}, u32[]{:S(2)}, u32[]{:S(2)}) collective-permute-start(bf16[8,9344]{1,0:T(8,128)(2,1)S(1)} %pad_maximum_fusion.1), channel_id=1, source_target_pairs={{0,4},{4,0},{8,12},{12,8},{1,5},{5,1},{9,13},{13,9},{2,6},{6,2},{1... | collective-permute-start | bytes 448520 | tf_op jit(solution)/shard_map/ppermute | solution.py:37
  4.8 9.3 %collective-permute-start.2 = (bf16[8,5248]{1,0:T(8,128)(2,1)S(1)}, bf16[8,5248]{1,0:T(8,128)(2,1)S(1)}, u32[]{:S(2)}, u32[]{:S(2)}) collective-permute-start(bf16[8,5248]{1,0:T(8,128)(2,1)S(1)} %get-tuple-element.31), channel_id=1, source_target_pairs={{0,12},{4,8},{8,4},{12,0},{1,13},{5,9},{9,5},{13,1},{2,14},{6,10},... | collective-permute-start | bytes 251912 | tf_op jit(solution)/shard_map/ppermute | solution.py:37
  7.3 9.4 %collective-permute-start.1 = (bf16[8,5248]{1,0:T(8,128)(2,1)S(1)}, bf16[8,5248]{1,0:T(8,128)(2,1)S(1)}, u32[]{:S(2)}, u32[]{:S(2)}) collective-permute-start(bf16[8,5248]{1,0:T(8,128)(2,1)S(1)} %get-tuple-element.31), channel_id=1, source_target_pairs={{0,8},{4,12},{8,0},{12,4},{1,9},{5,13},{9,1},{13,5},{2,10},{6,14},... | collective-permute-start | bytes 251912 | tf_op jit(solution)/shard_map/ppermute | solution.py:37
  11.2 7.1 %collective-permute-start.4 = (bf16[8,4096]{1,0:T(8,128)(2,1)S(1)}, bf16[8,4096]{1,0:T(8,128)(2,1)S(1)}, u32[]{:S(2)}, u32[]{:S(2)}) collective-permute-start(bf16[8,4096]{1,0:T(8,128)(2,1)S(1)} %add_convert_fusion.3), channel_id=1, source_target_pairs={{0,8},{4,12},{8,0},{12,4},{1,9},{5,13},{9,1},{13,5},{2,10},{6,14},... | collective-permute-start | bytes 196616 | tf_op jit(solution)/shard_map/ppermute | solution.py:37
  16.7 7.9 %collective-permute-start.3 = (bf16[32,5248]{1,0:T(8,128)(2,1)S(1)}, bf16[32,5248]{1,0:T(8,128)(2,1)S(1)}, u32[]{:S(2)}, u32[]{:S(2)}) collective-permute-start(bf16[32,5248]{1,0:T(8,128)(2,1)S(1)} %pad_maximum_fusion.refs_0_), channel_id=1, source_target_pairs={{0,2},{1,3},{2,0},{3,1},{4,6},{5,7},{6,4},{7,5},{8,10},{9,11},{10,... | collective-permute-start | bytes 1007624 | tf_op jit(solution)/shard_map/ppermute | solution.py:33
  18.3 6.3 %collective-permute-start.5 = (bf16[8,4096]{1,0:T(8,128)(2,1)S(1)}, bf16[8,4096]{1,0:T(8,128)(2,1)S(1)}, u32[]{:S(2)}, u32[]{:S(2)}) collective-permute-start(bf16[8,4096]{1,0:T(8,128)(2,1)S(1)} %add_convert_fusion.2.refs_4_), channel_id=1, source_target_pairs={{0,2},{1,3},{2,0},{3,1},{4,6},{5,7},{6,4},{7,5},{8,10},{9,11},{10,... | collective-permute-start | bytes 196616 | tf_op jit(solution)/shard_map/ppermute | solution.py:33
  19.7 6.7 %collective-permute-start.6 = (bf16[32,5248]{1,0:T(8,128)(2,1)S(1)}, bf16[32,5248]{1,0:T(8,128)(2,1)S(1)}, u32[]{:S(2)}, u32[]{:S(2)}) collective-permute-start(bf16[32,5248]{1,0:T(8,128)(2,1)S(1)} %pad_maximum_fusion.refs_0_), channel_id=1, source_target_pairs={{0,1},{1,0},{2,3},{3,2},{4,5},{5,4},{6,7},{7,6},{8,9},{9,8},{10,11... | collective-permute-start | bytes 1007624 | tf_op jit(solution)/shard_map/ppermute | solution.py:41
  24.6 1.8 %collective-permute-start.7 = (bf16[32,5248]{1,0:T(8,128)(2,1)S(1)}, bf16[32,5248]{1,0:T(8,128)(2,1)S(1)}, u32[]{:S(2)}, u32[]{:S(2)}) collective-permute-start(bf16[32,5248]{1,0:T(8,128)(2,1)S(1)} %collective-permute-done.3.refs_1_), channel_id=1, source_target_pairs={{0,1},{1,0},{2,3},{3,2},{4,5},{5,4},{6,7},{7,6},{8,9},{9,8},{10,11... | collective-permute-start | bytes 1007624 | tf_op jit(solution)/shard_map/ppermute | solution.py:41
  24.6 1.7 %collective-permute-start.8 = (bf16[8,4096]{1,0:T(8,128)(2,1)S(1)}, bf16[8,4096]{1,0:T(8,128)(2,1)S(1)}, u32[]{:S(2)}, u32[]{:S(2)}) collective-permute-start(bf16[8,4096]{1,0:T(8,128)(2,1)S(1)} %add_convert_fusion.2.refs_4_), channel_id=1, source_target_pairs={{0,1},{1,0},{2,3},{3,2},{4,5},{5,4},{6,7},{7,6},{8,9},{9,8},{10,11... | collective-permute-start | bytes 196616 | tf_op jit(solution)/shard_map/ppermute | solution.py:41
  25.2 1.3 %collective-permute-start.9 = (bf16[8,4096]{1,0:T(8,128)(2,1)S(1)}, bf16[8,4096]{1,0:T(8,128)(2,1)S(1)}, u32[]{:S(2)}, u32[]{:S(2)}) collective-permute-start(bf16[8,4096]{1,0:T(8,128)(2,1)S(1)} %collective-permute-done.5.refs_5_), channel_id=1, source_target_pairs={{0,1},{1,0},{2,3},{3,2},{4,5},{5,4},{6,7},{7,6},{8,9},{9,8},{10,11... | collective-permute-start | bytes 196616 | tf_op jit(solution)/shard_map/ppermute | solution.py:41
  31.4 1.8 %collective-permute-start.10 = (bf16[64,3072]{1,0:T(8,128)(2,1)S(1)}, bf16[64,3072]{1,0:T(8,128)(2,1)S(1)}, u32[]{:S(2)}, u32[]{:S(2)}) collective-permute-start(bf16[64,3072]{1,0:T(8,128)(2,1)S(1)} %get-tuple-element.43), channel_id=1, source_target_pairs={{0,1},{1,0},{2,3},{3,2},{4,5},{5,4},{6,7},{7,6},{8,9},{9,8},{10,11... | collective-permute-start | bytes 1179656 | tf_op jit(solution)/shard_map/ppermute | solution.py:41
  33.3 7.0 %collective-permute-start.11 = (bf16[32,3072]{1,0:T(8,128)(2,1)S(1)}, bf16[32,3072]{1,0:T(8,128)(2,1)S(1)}, u32[]{:S(2)}, u32[]{:S(2)}) collective-permute-start(bf16[32,3072]{1,0:T(8,128)(2,1)S(1)} %slice.27), channel_id=1, source_target_pairs={{0,2},{1,3},{2,0},{3,1},{4,6},{5,7},{6,4},{7,5},{8,10},{9,11},{10,... | collective-permute-start | bytes 589832 | tf_op jit(solution)/shard_map/ppermute | solution.py:33
  40.4 6.6 %collective-permute-start.14 = (bf16[8,3072]{1,0:T(8,128)(2,1)S(1)}, bf16[8,3072]{1,0:T(8,128)(2,1)S(1)}, u32[]{:S(2)}, u32[]{:S(2)}) collective-permute-start(bf16[8,3072]{1,0:T(8,128)(2,1)S(1)} %get-tuple-element.57), channel_id=1, source_target_pairs={{0,12},{4,8},{8,4},{12,0},{1,13},{5,9},{9,5},{13,1},{2,14},{6,10},... | collective-permute-start | bytes 147464 | tf_op jit(solution)/shard_map/ppermute | solution.py:37
  43.4 5.0 %collective-permute-start.13 = (bf16[8,3072]{1,0:T(8,128)(2,1)S(1)}, bf16[8,3072]{1,0:T(8,128)(2,1)S(1)}, u32[]{:S(2)}, u32[]{:S(2)}) collective-permute-start(bf16[8,3072]{1,0:T(8,128)(2,1)S(1)} %get-tuple-element.58), channel_id=1, source_target_pairs={{0,8},{4,12},{8,0},{12,4},{1,9},{5,13},{9,1},{13,5},{2,10},{6,14},... | collective-permute-start | bytes 147464 | tf_op jit(solution)/shard_map/ppermute | solution.py:37
  43.4 5.0 %collective-permute-start.12 = (bf16[8,3072]{1,0:T(8,128)(2,1)S(1)}, bf16[8,3072]{1,0:T(8,128)(2,1)S(1)}, u32[]{:S(2)}, u32[]{:S(2)}) collective-permute-start(bf16[8,3072]{1,0:T(8,128)(2,1)S(1)} %get-tuple-element.59), channel_id=1, source_target_pairs={{0,4},{4,0},{8,12},{12,8},{1,5},{5,1},{9,13},{13,9},{2,6},{6,2},{1... | collective-permute-start | bytes 147464 | tf_op jit(solution)/shard_map/ppermute | solution.py:37
